TPU v7x, 256 devices: a whole 4x4x8 slice. The times are simulated.
256 devices in a mesh: dom: 32 (over y, x, core), sub: 8 (over z).
Axes of the slice: x: 4, y: 4, z: 8, core: 2. Of those that a mesh axis runs over, the one named last changes fastest.
Arguments:
- hamiltonian: bfloat16 [256, 9, 256, 256], P(('dom', 'sub'))
- partitions: int32 [256, 5], P(('dom', 'sub')), may hold values from -1 to 255, as said below
- chemical_potential: float32 [], replicated, may hold values from -0.5 to 0.5
Outputs:
- density: float32 [256, 256, 1280], P(('dom', 'sub'))
- charges: float32 [16384], replicated
Inputs may be any that keep to these rules, and one draw needn't show every extreme that they name: `partitions`: slot 0 of each partition is a block owned by the partition's own device (row p lies on device p), each of them once. Slot 1 is -1 or a block of the device one step lower along dom (cyclically) with the same sub index, slot 2 likewise one step higher; slot 3 is -1 or a block of the device one step lower along sub in the same dom group, slot 4 one step higher; no slot 3 exists on the first sub index and no slot 4 on the last. Every halo block lies within 1 of the core block along the second grid dimension and within one along the first. Some partition has all five slots live.
All inputs are finite; a program needn't handle non-finite values.
Results may differ from a plain program's by a relative error of at most 0.0004.
Values may be sent and summed in bfloat16 or wider, within the bound.
No kernel may reach another device: no remote copies, remote signals or barrier semaphores. Data moves between devices by JAX's collectives and lax.ppermute only.
A program may use at most 64 MiB of HBM per device.

v0:
```python
import jax
import jax.numpy as jnp
from jax import lax
from jax.sharding import PartitionSpec as P

ORBS = 4
REACH = 1


def with_halo(x, sides, width, wrap):
    for axis, dim in sides:
        size, length = (lax.axis_size(axis), x.shape[dim])
        up = [(i, (i + 1) % size) for i in range(size if wrap else size - 1)]
        down = [(j, i) for i, j in up]
        last = lax.slice_in_dim(x, length - width, length, axis=dim)
        first = lax.slice_in_dim(x, 0, width, axis=dim)
        before = lax.ppermute(last, axis, up)
        after = lax.ppermute(first, axis, down)
        x = jnp.concatenate([before, x, after], axis=dim)
    return x


def column_blocks(blocks, n_dom, n_sub, part_count):
    span_size = 2 * REACH + 1
    offset = jnp.arange(3 * span_size, dtype=jnp.int32)
    dom_step = offset // span_size - 1
    sub_step = offset % span_size - REACH
    device = blocks // part_count
    dom_coord = device // n_sub
    sub_coord = device % n_sub * part_count + blocks % part_count
    dom_new = (dom_coord[..., None] + dom_step) % n_dom
    sub_new = sub_coord[..., None] + sub_step
    inside = (sub_new >= 0) & (sub_new < n_sub * part_count) & (blocks[..., None] >= 0)
    target = (dom_new * n_sub + sub_new // part_count) * part_count + sub_new % part_count
    return jnp.where(inside, target, -2)


def matching(columns, wanted_lists, live_rows):
    matches = (
        (columns[:, :, None] == wanted_lists[:, None, :])
        & (wanted_lists[:, None, :] >= 0)
        & live_rows[:, None, None]
    )
    return matches.astype(jnp.bfloat16)


def density_rows(whole, live_slots, potential):
    sub_order = whole.shape[1]
    block_size = sub_order // live_slots.shape[1]
    orbital_live = jnp.repeat(live_slots.astype(jnp.float32), block_size, axis=1)
    identity = jnp.eye(sub_order, dtype=jnp.float32)
    symmetric = 0.5 * (whole + jnp.swapaxes(whole, 1, 2))
    shifted = (
        (potential * identity - symmetric) * orbital_live[:, :, None] * orbital_live[:, None, :]
    )
    spectral = 2.0 * jnp.sqrt(jnp.max(jnp.sum(shifted * shifted, axis=2), axis=1) + 1e-06)
    initial = shifted / spectral[:, None, None]
    initial_b = initial.astype(jnp.bfloat16)
    square = jnp.einsum(
        "pij,pjk->pik", initial_b, initial_b, preferred_element_type=jnp.float32
    ).astype(jnp.bfloat16)
    first_step = 0.5 * (
        3.0 * initial
        - jnp.einsum("pij,pjk->pik", initial_b, square, preferred_element_type=jnp.float32)
    )
    first_b = first_step.astype(jnp.bfloat16)
    square_two = jnp.einsum(
        "pij,pjk->pik", first_b, first_b, preferred_element_type=jnp.float32
    ).astype(jnp.bfloat16)
    core_rows = 0.5 * (
        3.0 * first_step[:, :block_size]
        - jnp.einsum(
            "pij,pjk->pik", first_b[:, :block_size], square_two, preferred_element_type=jnp.float32
        )
    )
    return 0.5 * (identity[:block_size][None] + core_rows)


def shards(hamiltonian, partitions, chemical_potential):
    n_dom = lax.axis_size("dom")
    n_sub = lax.axis_size("sub")
    part_count = partitions.shape[0]
    slot_count = partitions.shape[1]
    block_size = hamiltonian.shape[2]
    dom_here = lax.axis_index("dom")
    sub_here = lax.axis_index("sub")
    my_index = dom_here * n_sub + sub_here
    first_block = my_index * part_count
    live_slots = partitions >= 0

    def take_from(source, wanted, first):
        return jnp.take(source, jnp.clip(wanted - first, 0, part_count - 1), axis=0)

    dom_got = with_halo(hamiltonian, (("dom", 0),), part_count, True)
    sub_got = with_halo(hamiltonian, (("sub", 0),), part_count, False)
    dom_lower_first = ((dom_here - 1) % n_dom * n_sub + sub_here) * part_count
    dom_upper_first = ((dom_here + 1) % n_dom * n_sub + sub_here) * part_count
    sub_lower_first = (my_index - 1) * part_count
    sub_upper_first = (my_index + 1) * part_count
    sources = [
        take_from(hamiltonian, partitions[:, 0], first_block),
        take_from(dom_got[:part_count], partitions[:, 1], dom_lower_first),
        take_from(dom_got[2 * part_count :], partitions[:, 2], dom_upper_first),
        take_from(sub_got[:part_count], partitions[:, 3], sub_lower_first),
        take_from(sub_got[2 * part_count :], partitions[:, 4], sub_upper_first),
    ]
    pieces = []
    for slot in range(slot_count):
        requested = partitions[:, slot]
        columns = column_blocks(requested, n_dom, n_sub, part_count)
        matches = matching(columns, partitions, requested >= 0)
        pieces.append(
            jnp.einsum("pkj,pkab->pajb", matches, sources[slot], preferred_element_type=jnp.float32)
        )
    whole = jnp.stack(pieces, axis=1).reshape(
        part_count, slot_count * block_size, slot_count * block_size
    )
    density = density_rows(whole, live_slots, chemical_potential)
    diagonal = jnp.diagonal(density[:, :, :block_size], axis1=1, axis2=2)
    local_charges = 4.0 - 2.0 * jnp.sum(
        diagonal.reshape(part_count * block_size // ORBS, ORBS), axis=1
    )
    charges = lax.all_gather(local_charges, ("dom", "sub"), axis=0, tiled=True)
    return (density, charges)


def solution(mesh):
    return jax.shard_map(
        shards,
        mesh=mesh,
        in_specs=(P(("dom", "sub"), None, None, None), P(("dom", "sub"), None), P()),
        out_specs=(P(("dom", "sub"), None, None), P()),
        check_vma=False,
    )
```

profile of v0, /device:TPU:1, one launch (start us, length us, event | category | flops | bytes accessed | tf_op | source)
XLA Modules:
  0.0 373.5 jit_solution(6058959115739504035)
XLA Ops:
  7.2 0.0 copy-start.2
  7.2 0.0 all-reduce.3.cloned.1.call-start
  7.2 2.7 collective-permute-start
  9.9 0.7 collective-permute-start.1
  10.6 2.9 collective-permute-start.2
  13.5 1.3 collective-permute-start.3
  14.8 1.5 fusion.114
  35.0 0.7 fusion.101
  38.5 0.1 broadcast_in_dim.119
  39.4 0.7 broadcast_compare_fusion
  40.1 3.7 bitcast_dynamic-update-slice_fusion.4
  43.8 0.0 collective-permute-done
  43.8 3.7 bitcast_dynamic-update-slice_fusion.3
  47.5 0.0 collective-permute-done.1
  47.5 0.0 copy-done.2
  47.5 3.7 bitcast_dynamic-update-slice_fusion.2
  51.1 0.0 collective-permute-done.2
  51.1 2.4 bitcast_dynamic-update-slice_fusion.1
  53.6 0.0 collective-permute-done.3
  53.6 2.5 bitcast_dynamic-update-slice_fusion
  56.0 9.7 %reshape.723 = f32[1,1280,1280]{2,1,0:T(8,128)} reshape(f32[1,5,256,5,256]{4,3,2,1,0:T(8,128)} %bitcast_dynamic-update-slice_fusion) | data formatting | bytes 13107200 | tf_op jit(solution)/shard_map/reshape | solution.py:115
  65.7 8.2 %copy.22 = f32[1,1280,1280]{1,2,0:T(8,128)} copy(f32[1,1280,1280]{2,1,0:T(8,128)} %reshape.723) | data formatting | bytes 13107200 | tf_op jit(solution)/shard_map/reshape | solution.py:115
  73.9 0.0 slice-start
  73.9 6.2 %multiply_reduce_fusion = f32[1280]{0:T(1024)S(1)} fusion(f32[1280]{0:T(1024)S(1)} %broadcast_in_dim.120, f32[1,1280,1280]{2,1,0:T(8,128)} %reshape.723, f32[1,1280,1280]{1,2,0:T(8,128)} %copy.22, f32[]{:T(128)S(6)} %copy.59), kind=kLoop, calls=%fused_computation.11 | loop fusion | flops 14744320 | bytes 13117444 | tf_op jit(solution)/shard_map/reduce_sum | solution.py:56
  80.1 0.6 reduce_max.9
  81.4 0.0 slice-start.1
  81.5 14.2 %convolution_convert_fusion.1.clone.1.clone.5 = bf16[1280,1280]{1,0:T(8,128)(2,1)S(1)} fusion(f32[]{:T(128)S(6)} %mul.129, f32[1,1280,1280]{2,1,0:T(8,128)} %reshape.723, f32[1,1280,1280]{1,2,0:T(8,128)} %copy.22, f32[1280]{0:T(1024)S(1)} %broadcast_in_dim.120, f32[]{:T(128)S(6)} %copy.59), kind=kOutput, calls=%fused_computation.5.clone.clone.clone.clone.clone.2 | convolution fusion | flops 4210688000 | bytes 16389128 | tf_op jit(solution)/shard_map/pij,pjk->pik/dot_general | solution.py:59
  95.6 0.0 slice-done
  95.6 0.0 slice-done.1
  95.7 13.8 %fusion.115 = (bf16[1,1280,1280]{2,1,0:T(8,128)(2,1)}, f32[1,1280,1280]{2,1,0:T(8,128)}) fusion(f32[]{:T(128)S(6)} %mul.129, f32[1,1280,1280]{2,1,0:T(8,128)S(1)} %bitcast.190, f32[1,1280,1280]{1,2,0:T(8,128)} %copy.22, f32[1280]{0:T(1024)S(1)} %broadcast_in_dim.120, f32[]{:T(128)S(6)} %copy.59, ...), kind=kOutput, calls=%fused_computation.151 | convolution fusion | flops 4228710400 | bytes 26219528 | tf_op jit(solution)/shard_map/pij,pjk->pik/dot_general | solution.py:64
  109.4 9.0 %fusion.14 = f32[1,256,1280]{2,1,0:T(8,128)S(1)} fusion(f32[1,1280,1280]{2,1,0:T(8,128)} %get-tuple-element.8, bf16[1,1280,1280]{2,1,0:T(8,128)(2,1)} %get-tuple-element.7), kind=kOutput, calls=%fused_computation.23 | convolution fusion | flops 5037424640 | bytes 6553600 | tf_op jit(solution)/shard_map/pij,pjk->pik/dot_general | solution.py:72
  118.4 0.0 copy-start.1
  118.4 2.3 gather_fusion
  120.8 0.1 reshape.727
  120.9 0.1 reduce_sum.19
  121.0 0.1 subtract_dynamic-update-slice_fusion
  121.1 0.0 copy-start
  121.1 0.6 copy-done
  121.8 0.0 all-reduce.3.cloned.1.call-update
  121.8 243.4 %all-reduce.3.cloned.1.call-done = f32[16384]{0:T(1024)} async-done(((f32[16384]{0:T(1024)}), f32[16384]{0:T(1024)}) %all-reduce.3.cloned.1.call-update) | async-done | bytes 65552
  365.2 1.5 copy.60
  366.6 0.0 copy-done.1
  (10 shorter events, 0.1 us)
Async XLA Ops:
  7.2 40.3 %copy-start.2 = (s32[1,5]{1,0:T(1,128)S(1)}, s32[1,5]{1,0:T(1,128)}, u32[]{:S(2)}) copy-start(s32[1,5]{1,0:T(1,128)} %param.4) | copy-start | bytes 64
  7.2 358.0 %all-reduce.3.cloned.1.call-start = ((), (), s32[]{:S(2)}) async-start(), calls=%async_computation | async-start | bytes 131072
  7.2 36.6 %collective-permute-start = (bf16[1,9,256,256]{3,2,1,0:T(8,128)(2,1)}, bf16[1,9,256,256]{3,2,1,0:T(8,128)(2,1)}, u32[]{:S(2)}, u32[]{:S(2)}) collective-permute-start(bf16[1,9,256,256]{3,2,1,0:T(8,128)(2,1)} %param.3), channel_id=1, source_target_pairs={{0,8},{8,16},{16,24},{24,32},{32,40},{40,48},{48,56},{56,64},{64,7... | collective-permute-start | bytes 3538952 | tf_op jit(solution)/shard_map/ppermute | solution.py:17
  9.9 37.6 %collective-permute-start.1 = (bf16[1,9,256,256]{3,2,1,0:T(8,128)(2,1)}, bf16[1,9,256,256]{3,2,1,0:T(8,128)(2,1)}, u32[]{:S(2)}, u32[]{:S(2)}) collective-permute-start(bf16[1,9,256,256]{3,2,1,0:T(8,128)(2,1)} %param.3), channel_id=1, source_target_pairs={{8,0},{16,8},{24,16},{32,24},{40,32},{48,40},{56,48},{64,56},{72,6... | collective-permute-start | bytes 3538952 | tf_op jit(solution)/shard_map/ppermute | solution.py:18
  10.6 40.5 %collective-permute-start.2 = (bf16[1,9,256,256]{3,2,1,0:T(8,128)(2,1)}, bf16[1,9,256,256]{3,2,1,0:T(8,128)(2,1)S(1)}, u32[]{:S(2)}, u32[]{:S(2)}) collective-permute-start(bf16[1,9,256,256]{3,2,1,0:T(8,128)(2,1)} %param.3), channel_id=1, source_target_pairs={{0,1},{1,2},{2,3},{3,4},{4,5},{5,6},{6,7},{8,9},{9,10},{10,11},{11... | collective-permute-start | bytes 3538952 | tf_op jit(solution)/shard_map/ppermute | solution.py:17
  13.5 40.1 %collective-permute-start.3 = (bf16[1,9,256,256]{3,2,1,0:T(8,128)(2,1)}, bf16[1,9,256,256]{3,2,1,0:T(8,128)(2,1)S(1)}, u32[]{:S(2)}, u32[]{:S(2)}) collective-permute-start(bf16[1,9,256,256]{3,2,1,0:T(8,128)(2,1)} %param.3), channel_id=1, source_target_pairs={{1,0},{2,1},{3,2},{4,3},{5,4},{6,5},{7,6},{9,8},{10,9},{11,10},{12... | collective-permute-start | bytes 3538952 | tf_op jit(solution)/shard_map/ppermute | solution.py:18
  73.9 21.7 %slice-start = ((s8[6553600]{0:T(1024)(128)(4,1)}), s8[2359296]{0:T(1024)(128)(4,1)S(1)}, s32[]{:S(2)}) async-start(s8[6553600]{0:T(1024)(128)(4,1)} %bitcast.189), calls=%async_computation.1 | async-start | bytes 4718592
  81.4 14.2 %slice-start.1 = ((s8[6553600]{0:T(1024)(128)(4,1)}), s8[4194304]{0:T(1024)(128)(4,1)S(1)}, s32[]{:S(2)}) async-start(s8[6553600]{0:T(1024)(128)(4,1)} %bitcast.189), calls=%async_computation.2 | async-start | bytes 8388608
  118.4 248.3 %copy-start.1 = (f32[1,256,1280]{2,1,0:T(8,128)}, f32[1,256,1280]{2,1,0:T(8,128)S(1)}, u32[]{:S(2)}) copy-start(f32[1,256,1280]{2,1,0:T(8,128)S(1)} %fusion.14) | copy-start | bytes 3932164
  121.1 0.6 copy-start
Sparse Core Ops, SparseCore 0:
  121.9 243.2 all-reduce.2
where the time goes:
time: 374 us; the launch traced here: 373 us
  waiting for transfers between devices  243 us (65%)
  matrix products  52.8 us (14%)
  between operations  37.1 us (10%)
  local copies, waits for them, and re-layouts  24.1 us (6%)
  other arithmetic  8.5 us (2%)
  starting transfers between devices  7.62 us (2%)
    unnamed x2, waiting for transfers between devices  243 us
    reshape x2, local copies, waits for them, and re-layouts, shards(): jnp.stack(pieces, axis=1)  17.9 us
    dot_general x5, matrix products, shards(): jnp.einsum('pkj,pkab->pajb', matches, sources[slot], preferred_element_ty...  15.9 us
    dot_general x1, matrix products, density_rows(): jnp.einsum('pij,pjk->pik', initial_b, initial_b, preferred_element_type=j...  14.2 us
    dot_general x1, matrix products, density_rows(): jnp.einsum('pij,pjk->pik', initial_b, square, preferred_element_type=jnp....  13.8 us
    dot_general x1, matrix products, density_rows(): jnp.einsum('pij,pjk->pik', first_b[:, :block_size], square_two, preferred...  8.96 us
  transfers between devices with their start and end apart: 5, of which 1 were waited for; matrix products, arithmetic and copies ran while one was open for 4% of the time, Pallas kernels for 0%

commit v1 on v0

v1 whole, which is shorter than its diff:
```python
import functools

import jax
import jax.numpy as jnp
from jax import lax
from jax.experimental import pallas as pl
from jax.experimental.pallas import tpu as pltpu
from jax.sharding import PartitionSpec as P

ORBS = 4
LANES = 128
SLOTS = 5
STEPS = ((0, 0), (-1, 0), (1, 0), (0, -1), (0, 1))
SENT = {1: (4, 7, 6, 8), 2: (4, 1, 0, 2), 3: (4, 5, 2, 8), 4: (4, 3, 0, 6)}


def tile_of(i, j):
    da = STEPS[j][0] - STEPS[i][0]
    db = STEPS[j][1] - STEPS[i][1]
    if abs(da) > 1 or abs(db) > 1:
        return None
    return (da + 1) * 3 + db + 1


COUPLED = {(i, j): tile_of(i, j) is not None for i in range(SLOTS) for j in range(SLOTS)}


def density_kernel(slots, potential, own, r1, r2, r3, r4, density, charges, m, m0, w, wb):
    blk = own.shape[-1]
    f32, bf16 = jnp.float32, jnp.bfloat16
    received = {1: r1, 2: r2, 3: r3, 4: r4}

    def tile(i, j):
        k = tile_of(i, j)
        if i == 0:
            return own[0, k]
        return received[i][0, SENT[i].index(k)]

    def at(i):
        return slice(i * blk, (i + 1) * blk)

    rows = lax.broadcasted_iota(jnp.int32, (blk, blk), 0)
    cols = lax.broadcasted_iota(jnp.int32, (blk, blk), 1)
    eye = rows == cols
    live = [(slots[0, i] >= 0).astype(f32) for i in range(SLOTS)]
    cp = potential[0, 0]

    row_sums = [None] * SLOTS
    col_sums = [None] * SLOTS

    def added(old, new):
        return new if old is None else old + new

    for i in range(SLOTS):
        for j in range(i, SLOTS):
            if not COUPLED[i, j]:
                m[at(i), at(j)] = jnp.zeros((blk, blk), bf16)
                m[at(j), at(i)] = jnp.zeros((blk, blk), bf16)
                continue
            both = tile(i, j).astype(f32) + tile(j, i).T.astype(f32)
            if i == j:
                block = (jnp.where(eye, cp, 0.0) - 0.5 * both) * live[i]
            else:
                block = both * (-0.5 * live[i] * live[j])
            squares = block * block
            row_sums[i] = added(row_sums[i], jnp.sum(squares, axis=1, keepdims=True))
            rounded = block.astype(bf16)
            m[at(i), at(j)] = rounded
            if i == 0:
                m0[:, at(j)] = block
            if i != j:
                col_sums[j] = added(col_sums[j], jnp.sum(squares, axis=0, keepdims=True))
                m[at(j), at(i)] = rounded.T
    largest = jnp.max(row_sums[0], axis=0, keepdims=True)
    for j in range(1, SLOTS):
        turned = jnp.sum(jnp.where(eye, col_sums[j], 0.0), axis=1, keepdims=True)
        largest = jnp.maximum(largest, jnp.max(row_sums[j] + turned, axis=0, keepdims=True))
    inv = 1.0 / (2.0 * jnp.sqrt(largest + 1e-06))

    for i in range(SLOTS):
        for j in range(i, SLOTS):
            total = None
            for k in range(SLOTS):
                if COUPLED[i, k] and COUPLED[k, j]:
                    term = jnp.dot(m[at(i), at(k)], m[at(k), at(j)], preferred_element_type=f32)
                    total = added(total, term)
            w[at(i), at(j)] = total
    for i in range(SLOTS):
        for j in range(i, SLOTS):
            rounded = (w[at(i), at(j)] * inv * inv).astype(bf16)
            wb[at(i), at(j)] = rounded
            if i != j:
                wb[at(j), at(i)] = rounded.T

    def times_w(left, j):
        return jnp.dot(left, wb[:, at(j)], preferred_element_type=f32)

    def join(parts):
        return jnp.concatenate(parts, axis=1)

    left = m[at(0), :]
    first = [
        inv * (1.5 * m0[:, at(j)] - 0.5 * times_w(left, j)) for j in range(SLOTS)
    ]
    left = join([part.astype(bf16) for part in first])
    for j in range(SLOTS):
        m0[:, at(j)] = first[j]
    second = [times_w(left, j) for j in range(SLOTS)]
    left = join([part.astype(bf16) for part in second])
    third = [1.5 * second[j] - 0.5 * times_w(left, j) for j in range(SLOTS)]
    left = join([part.astype(bf16) for part in third])
    for j in range(SLOTS):
        sign = 1.5 * m0[:, at(j)] - 0.75 * third[j] + 0.25 * times_w(left, j)
        if j == 0:
            sign = jnp.where(eye, 1.0 + sign, sign)
        density[0, :, at(j)] = 0.5 * sign
    occupied = jnp.sum(jnp.where(eye, density[0, :, at(0)], 0.0), axis=1, keepdims=True)
    copies, height, lanes = charges.shape
    atoms = blk // ORBS
    place = slots[0, 0] % copies * atoms
    atom = lax.broadcasted_iota(jnp.int32, (blk, lanes), 0) // ORBS + place % lanes
    lane = lax.broadcasted_iota(jnp.int32, (blk, lanes), 1)
    held = jnp.sum(jnp.where(atom == lane, 4.0 / ORBS - 2.0 * occupied, 0.0), axis=0, keepdims=True)
    row = lax.broadcasted_iota(jnp.int32, (height, lanes), 0)
    placed = jnp.where(row == place // lanes, held, 0.0)
    for copy in range(copies):
        charges[copy] = placed


def pack_kernel(slots, own, earlier, *refs):
    packs, sems = refs[:-1], refs[-1]
    copies = []
    for place, slot in enumerate(slots):
        for index, k in enumerate(SENT[slot]):
            copies.append(
                pltpu.make_async_copy(
                    own.at[0, k], packs[place].at[0, index], sems.at[len(copies)]
                )
            )
    for copy in copies:
        copy.start()
    for copy in copies:
        copy.wait()


def packed(own, earlier, *slots):
    blk = own.shape[-1]
    anywhere = pl.BlockSpec(memory_space=pl.ANY)
    shape = jax.ShapeDtypeStruct((1, len(SENT[1]), blk, blk), own.dtype)
    return pl.pallas_call(
        functools.partial(pack_kernel, slots),
        out_shape=(shape,) * len(slots),
        in_specs=[pl.BlockSpec(memory_space=pltpu.HBM), anywhere],
        out_specs=(anywhere,) * len(slots),
        scratch_shapes=[pltpu.SemaphoreType.DMA((len(slots) * len(SENT[1]),))],
        name="pack_halo",
    )(own, earlier)


def local_part(slots, potential, own, received, n_sub):
    blk = own.shape[-1]
    order = SLOTS * blk
    vmem = pl.BlockSpec(memory_space=pltpu.VMEM)
    smem = pl.BlockSpec(memory_space=pltpu.SMEM)
    return pl.pallas_call(
        density_kernel,
        out_shape=(
            jax.ShapeDtypeStruct((1, blk, order), jnp.float32),
            jax.ShapeDtypeStruct((n_sub, 8, LANES), jnp.float32),
        ),
        in_specs=[smem, smem] + [vmem] * 5,
        out_specs=(vmem, vmem),
        scratch_shapes=[
            pltpu.VMEM((order, order), jnp.bfloat16),
            pltpu.VMEM((blk, order), jnp.float32),
            pltpu.VMEM((order, order), jnp.float32),
            pltpu.VMEM((order, order), jnp.bfloat16),
        ],
        compiler_params=pltpu.CompilerParams(vmem_limit_bytes=48 * 1024 * 1024),
        name="density_rows",
    )(slots, potential, own, *received)


def shards(hamiltonian, partitions, chemical_potential):
    n_dom = lax.axis_size("dom")
    n_sub = lax.axis_size("sub")
    blk = hamiltonian.shape[2]

    def exchanged(up, down, axis, size):
        forward = [(i, (i + 1) % size) for i in range(size)]
        return (
            lax.ppermute(up, axis, forward),
            lax.ppermute(down, axis, [(j, i) for i, j in forward]),
        )

    sub_up, sub_down = packed(hamiltonian, partitions, 3, 4)
    dom_up, dom_down = packed(hamiltonian, sub_up, 1, 2)
    r3, r4 = exchanged(sub_up, sub_down, "sub", n_sub)
    r1, r2 = exchanged(dom_up, dom_down, "dom", n_dom)
    density, placed = local_part(
        partitions, chemical_potential.reshape(1, 1), hamiltonian, (r1, r2, r3, r4), n_sub
    )
    group_rows = n_sub * blk // ORBS // LANES
    by_sub = lax.all_to_all(placed, "sub", 0, 0, tiled=True)
    group = jnp.sum(by_sub, axis=0)[:group_rows]
    copies = jnp.broadcast_to(group[None], (n_dom, group_rows, LANES))
    charges = lax.all_to_all(copies, "dom", 0, 0, tiled=True).reshape(-1)
    return (density, charges)


def solution(mesh):
    return jax.shard_map(
        shards,
        mesh=mesh,
        in_specs=(P(("dom", "sub"), None, None, None), P(("dom", "sub"), None), P()),
        out_specs=(P(("dom", "sub"), None, None), P()),
        check_vma=False,
    )
```

time: 374 us -> 119 us (0.32)
  waiting for transfers between devices: 243 us -> 8.44 us
  Pallas kernels: 0 us -> 73.6 us
  matrix products: 52.8 us -> 0 us
  between operations: 37.1 us -> 1.34 us
  blocking collectives: 0 us -> 26.6 us
  local copies, waits for them, and re-layouts: 24.1 us -> 0.66 us
  other arithmetic: 8.5 us -> 0.01 us
    unnamed x2 -> x0, waiting for transfers between devices: 243 us -> none
    pallas_call x0 -> x3, Pallas kernels: none -> 73.6 us  [the longest x2 65.9 us: packed(): pl.pallas_call(functools.partial(pack_kernel, slots), out_shape=(shape,)...]
    dot_general x8 -> x0, matrix products: 52.8 us -> none  [the longest x5 15.9 us: shards(): jnp.einsum('pkj,pkab->pajb', matches, sources[slot], preferred_element_ty...]
    all_to_all x0 -> x2, blocking collectives: none -> 26.6 us  [the longest x1 15.6 us: shards(): charges = lax.all_to_all(copies, 'dom', 0, 0, tiled=True).reshape(-1)]
    reshape x3 -> x0, local copies, waits for them, and re-layouts: 18 us -> none  [the longest x2 17.9 us: shards(): jnp.stack(pieces, axis=1)]
    ppermute x4, waiting for transfers between devices: 0.01 us -> 8.44 us  [the longest x2 5.77 us: exchanged(): lax.ppermute(up, axis, forward)]
    reduce_sum x2 -> x1, other arithmetic: 6.34 us -> 0.01 us  [shards(): group = jnp.sum(by_sub, axis=0)[:group_rows]]
  transfers between devices with their start and end apart: 5 -> 4, of which waited for: 1 -> 2; matrix products, arithmetic and copies ran while one was open for 4% -> 0% of each run, Pallas kernels for 0% -> 28%
where the time goes in v1:
time: 119 us
  Pallas kernels  73.6 us (62%)
  blocking collectives  26.6 us (22%)
  starting transfers between devices  8.62 us (7%)
  waiting for transfers between devices  8.44 us (7%)
  between operations  1.34 us (1%)
    pallas_call x2, Pallas kernels, packed(): pl.pallas_call(functools.partial(pack_kernel, slots), out_shape=(shape,)...  65.9 us
    all_to_all x1, blocking collectives, shards(): charges = lax.all_to_all(copies, 'dom', 0, 0, tiled=True).reshape(-1)  15.6 us
    all_to_all x1, blocking collectives, shards(): by_sub = lax.all_to_all(placed, 'sub', 0, 0, tiled=True)  11 us
    pallas_call x1, Pallas kernels, local_part(): pl.pallas_call(density_kernel, out_shape=(jax.ShapeDtypeStruct((1, blk, o...  7.75 us
    ppermute x2, starting transfers between devices, exchanged(): lax.ppermute(down, axis, [(j, i) for i, j in forward])  6.48 us
    ppermute x2, waiting for transfers between devices, exchanged(): lax.ppermute(up, axis, forward)  5.77 us
    ppermute x2, waiting for transfers between devices, exchanged(): lax.ppermute(down, axis, [(j, i) for i, j in forward])  2.67 us
  transfers between devices with their start and end apart: 4, of which 2 were waited for; matrix products, arithmetic and copies ran while one was open for 0% of the time, Pallas kernels for 28%

profile of v1, /device:TPU:1, one launch (start us, length us, event | category | flops | bytes accessed | tf_op | source)
XLA Modules:
  0.0 119.3 jit_solution(1243913267577750640)
XLA Ops:
  0.6 0.0 copy-start
  0.6 0.0 copy-start.1
  0.7 32.9 %pack_halo.2 = (bf16[1,4,256,256]{3,2,1,0:T(8,128)(2,1)}, bf16[1,4,256,256]{3,2,1,0:T(8,128)(2,1)}) custom-call(bf16[1,9,256,256]{3,2,1,0:T(8,128)(2,1)} %own.5, s32[1,5]{1,0:T(1,128)} %slots.1), custom_call_target="tpu_custom_call" | custom-call | tf_op jit(solution)/shard_map/pack_halo/pallas_call | solution.py:150
  33.6 6.5 %collective-permute-start.3 = (bf16[1,4,256,256]{3,2,1,0:T(8,128)(2,1)}, bf16[1,4,256,256]{3,2,1,0:T(8,128)(2,1)S(1)}, u32[]{:S(2)}, u32[]{:S(2)}) collective-permute-start(bf16[1,4,256,256]{3,2,1,0:T(8,128)(2,1)} %get-tuple-element.11), channel_id=1, source_target_pairs={{1,0},{2,1},{3,2},{4,3},{5,4},{6,5},{7,6},{0,7},{9,8},{10,9},{11,1... | collective-permute-start | bytes 1572872 | tf_op jit(solution)/shard_map/ppermute | solution.py:193
  40.1 0.0 collective-permute-start.2
  40.1 32.9 %pack_halo.3 = (bf16[1,4,256,256]{3,2,1,0:T(8,128)(2,1)}, bf16[1,4,256,256]{3,2,1,0:T(8,128)(2,1)}) custom-call(bf16[1,9,256,256]{3,2,1,0:T(8,128)(2,1)} %own.5, bf16[1,4,256,256]{3,2,1,0:T(8,128)(2,1)} %get-tuple-element.8.earlier), custom_call_target="tpu_custom_call" | custom-call | tf_op jit(solution)/shard_map/pack_halo/pallas_call | solution.py:150
  73.0 2.1 %collective-permute-start = (bf16[1,4,256,256]{3,2,1,0:T(8,128)(2,1)}, bf16[1,4,256,256]{3,2,1,0:T(8,128)(2,1)S(1)}, u32[]{:S(2)}, u32[]{:S(2)}) collective-permute-start(bf16[1,4,256,256]{3,2,1,0:T(8,128)(2,1)} %get-tuple-element.9), channel_id=1, source_target_pairs={{0,8},{8,16},{16,24},{24,32},{32,40},{40,48},{48,56},{56,64},{64,7... | collective-permute-start | bytes 1572872 | tf_op jit(solution)/shard_map/ppermute | solution.py:192
  75.2 0.0 collective-permute-start.1
  75.8 0.0 collective-permute-done.3.r4
  75.8 0.0 collective-permute-done.2.r3
  75.8 5.8 %collective-permute-done.r1 = bf16[1,4,256,256]{3,2,1,0:T(8,128)(2,1)S(1)} collective-permute-done((bf16[1,4,256,256]{3,2,1,0:T(8,128)(2,1)}, bf16[1,4,256,256]{3,2,1,0:T(8,128)(2,1)S(1)}, u32[]{:S(2)}, u32[]{:S(2)}) %collective-permute-start) | collective-permute-done | bytes 524320 | tf_op jit(solution)/shard_map/ppermute | solution.py:192
  81.6 2.7 %collective-permute-done.1.r2 = bf16[1,4,256,256]{3,2,1,0:T(8,128)(2,1)S(1)} collective-permute-done((bf16[1,4,256,256]{3,2,1,0:T(8,128)(2,1)}, bf16[1,4,256,256]{3,2,1,0:T(8,128)(2,1)S(1)}, u32[]{:S(2)}, u32[]{:S(2)}) %collective-permute-start.1) | collective-permute-done | bytes 524320 | tf_op jit(solution)/shard_map/ppermute | solution.py:193
  84.3 0.0 copy-done
  84.3 0.0 copy-done.1
  84.3 7.8 %density_rows.1 = (f32[1,256,1280]{2,1,0:T(8,128)}, f32[8,8,128]{2,1,0:T(8,128)S(1)}) custom-call(s32[1,5]{1,0:T(1,128)S(1)} %copy-done.1, f32[1,1]{1,0:T(1,128)} %bitcast.2.potential, bf16[1,9,256,256]{3,2,1,0:T(8,128)(2,1)S(1)} %copy-done, bf16[1,4,256,256]{3,2,1,0:T(8,128)(2,1)S(1)} %collective-permute-done.r1, ...), custom_call_target="tpu_custom_call" | custom-call | tf_op jit(solution)/shard_map/density_rows/pallas_call | solution.py:165
  92.0 11.0 %all_to_all.10 = f32[8,8,128]{2,1,0:T(8,128)S(1)} all-to-all(f32[8,8,128]{2,1,0:T(8,128)S(1)} %get-tuple-element.13), channel_id=1, replica_groups=mesh['dom'=32,'sub'=8] {'sub'}, dimensions={0} | all-to-all | bytes 65536 | tf_op jit(solution)/shard_map/all_to_all | solution.py:204
  103.1 15.6 %all_to_all.11 = f32[32,4,128]{2,1,0:T(4,128)S(1)} all-to-all(f32[32,4,128]{2,1,0:T(4,128)S(1)} %broadcast_in_dim.2), channel_id=1, replica_groups=mesh['dom'=32,'sub'=8] {'dom'}, dimensions={0} | all-to-all | bytes 131072 | tf_op jit(solution)/shard_map/all_to_all | solution.py:207
  118.6 0.6 copy.7
  (3 shorter events, 0.0 us)
Async XLA Ops:
  0.6 83.6 %copy-start = (bf16[1,9,256,256]{3,2,1,0:T(8,128)(2,1)S(1)}, bf16[1,9,256,256]{3,2,1,0:T(8,128)(2,1)}, u32[]{:S(2)}) copy-start(bf16[1,9,256,256]{3,2,1,0:T(8,128)(2,1)} %own.5) | copy-start | bytes 3538948
  0.6 83.6 %copy-start.1 = (s32[1,5]{1,0:T(1,128)S(1)}, s32[1,5]{1,0:T(1,128)}, u32[]{:S(2)}) copy-start(s32[1,5]{1,0:T(1,128)} %slots.1) | copy-start | bytes 64
  33.6 42.2 %collective-permute-start.3 = (bf16[1,4,256,256]{3,2,1,0:T(8,128)(2,1)}, bf16[1,4,256,256]{3,2,1,0:T(8,128)(2,1)S(1)}, u32[]{:S(2)}, u32[]{:S(2)}) collective-permute-start(bf16[1,4,256,256]{3,2,1,0:T(8,128)(2,1)} %get-tuple-element.11), channel_id=1, source_target_pairs={{1,0},{2,1},{3,2},{4,3},{5,4},{6,5},{7,6},{0,7},{9,8},{10,9},{11,1... | collective-permute-start | bytes 1572872 | tf_op jit(solution)/shard_map/ppermute | solution.py:193
  40.1 35.7 %collective-permute-start.2 = (bf16[1,4,256,256]{3,2,1,0:T(8,128)(2,1)}, bf16[1,4,256,256]{3,2,1,0:T(8,128)(2,1)S(1)}, u32[]{:S(2)}, u32[]{:S(2)}) collective-permute-start(bf16[1,4,256,256]{3,2,1,0:T(8,128)(2,1)} %get-tuple-element.8.earlier), channel_id=1, source_target_pairs={{0,1},{1,2},{2,3},{3,4},{4,5},{5,6},{6,7},{7,0},{8,9},{9,10},{10,1... | collective-permute-start | bytes 1572872 | tf_op jit(solution)/shard_map/ppermute | solution.py:192
  73.0 8.6 %collective-permute-start = (bf16[1,4,256,256]{3,2,1,0:T(8,128)(2,1)}, bf16[1,4,256,256]{3,2,1,0:T(8,128)(2,1)S(1)}, u32[]{:S(2)}, u32[]{:S(2)}) collective-permute-start(bf16[1,4,256,256]{3,2,1,0:T(8,128)(2,1)} %get-tuple-element.9), channel_id=1, source_target_pairs={{0,8},{8,16},{16,24},{24,32},{32,40},{40,48},{48,56},{56,64},{64,7... | collective-permute-start | bytes 1572872 | tf_op jit(solution)/shard_map/ppermute | solution.py:192
  75.2 9.1 %collective-permute-start.1 = (bf16[1,4,256,256]{3,2,1,0:T(8,128)(2,1)}, bf16[1,4,256,256]{3,2,1,0:T(8,128)(2,1)S(1)}, u32[]{:S(2)}, u32[]{:S(2)}) collective-permute-start(bf16[1,4,256,256]{3,2,1,0:T(8,128)(2,1)} %get-tuple-element.10), channel_id=1, source_target_pairs={{8,0},{16,8},{24,16},{32,24},{40,32},{48,40},{56,48},{64,56},{72,6... | collective-permute-start | bytes 1572872 | tf_op jit(solution)/shard_map/ppermute | solution.py:193

commit v2 on v1

v2 whole, which is shorter than its diff:
```python
import functools

import jax
import jax.numpy as jnp
from jax import lax
from jax.experimental import pallas as pl
from jax.experimental.pallas import tpu as pltpu
from jax.sharding import PartitionSpec as P

ORBS = 4
LANES = 128
SLOTS = 5
STEPS = ((0, 0), (-1, 0), (1, 0), (0, -1), (0, 1))
SENT = {1: (4, 7, 6, 8), 2: (4, 1, 0, 2), 3: (4, 5, 2, 8), 4: (4, 3, 0, 6)}


def tile_of(i, j):
    da = STEPS[j][0] - STEPS[i][0]
    db = STEPS[j][1] - STEPS[i][1]
    if abs(da) > 1 or abs(db) > 1:
        return None
    return (da + 1) * 3 + db + 1


COUPLED = {(i, j): tile_of(i, j) is not None for i in range(SLOTS) for j in range(SLOTS)}


def density_kernel(
    slots, potential, own, r1, r2, r3, r4, density, charges, x0, x0b, q0b, x1b
):
    blk = own.shape[-1]
    f32, bf16 = jnp.float32, jnp.bfloat16
    received = {1: r1, 2: r2, 3: r3, 4: r4}
    upper = [(i, j) for i in range(SLOTS) for j in range(i, SLOTS)]

    def tile(i, j):
        k = tile_of(i, j)
        if i == 0:
            return own[0, k]
        return received[i][0, SENT[i].index(k)]

    def at(i):
        return slice(i * blk, (i + 1) * blk)

    def product(left, right, i, j):
        total = None
        for k in range(SLOTS):
            if left is x0b and not COUPLED[i, k] or right is x0b and not COUPLED[k, j]:
                continue
            term = jnp.dot(left[at(i), at(k)], right[at(k), at(j)], preferred_element_type=f32)
            total = added(total, term)
        return total

    def mirror(target, i, j, block):
        rounded = block.astype(bf16)
        target[at(i), at(j)] = rounded
        if i != j:
            target[at(j), at(i)] = rounded.T

    def added(old, new):
        return new if old is None else old + new

    rows = lax.broadcasted_iota(jnp.int32, (blk, blk), 0)
    cols = lax.broadcasted_iota(jnp.int32, (blk, blk), 1)
    eye = rows == cols
    live = [(slots[0, i] >= 0).astype(f32) for i in range(SLOTS)]
    cp = potential[0, 0]

    row_sums = [None] * SLOTS
    col_sums = [None] * SLOTS
    for i, j in upper:
        if not COUPLED[i, j]:
            continue
        both = tile(i, j).astype(f32) + tile(j, i).T.astype(f32)
        if i == j:
            block = (jnp.where(eye, cp, 0.0) - 0.5 * both) * live[i]
        else:
            block = both * (-0.5 * live[i] * live[j])
        x0[at(i), at(j)] = block
        squares = block * block
        row_sums[i] = added(row_sums[i], jnp.sum(squares, axis=1, keepdims=True))
        if i != j:
            col_sums[j] = added(col_sums[j], jnp.sum(squares, axis=0, keepdims=True))
    largest = jnp.max(row_sums[0], axis=0, keepdims=True)
    for j in range(1, SLOTS):
        turned = jnp.sum(jnp.where(eye, col_sums[j], 0.0), axis=1, keepdims=True)
        largest = jnp.maximum(largest, jnp.max(row_sums[j] + turned, axis=0, keepdims=True))
    inv = 1.0 / (2.0 * jnp.sqrt(largest + 1e-06))

    for i, j in upper:
        if COUPLED[i, j]:
            block = x0[at(i), at(j)] * inv
            x0[at(i), at(j)] = block
            mirror(x0b, i, j, block)
    for i, j in upper:
        mirror(q0b, i, j, product(x0b, x0b, i, j))
    first = []
    for i, j in upper:
        block = -0.5 * product(x0b, q0b, i, j)
        if COUPLED[i, j]:
            block = 1.5 * x0[at(i), at(j)] + block
        if i == 0:
            first.append(block)
        mirror(x1b, i, j, block)
    for j in range(SLOTS):
        x0[at(0), at(j)] = first[j]
    left = jnp.concatenate(
        [
            jnp.dot(x1b[at(0), :], x1b[:, at(j)], preferred_element_type=f32).astype(bf16)
            for j in range(SLOTS)
        ],
        axis=1,
    )
    for j in range(SLOTS):
        sign = 1.5 * x0[at(0), at(j)] - 0.5 * jnp.dot(
            left, x1b[:, at(j)], preferred_element_type=f32
        )
        if j == 0:
            sign = jnp.where(eye, 1.0 + sign, sign)
        density[0, :, at(j)] = 0.5 * sign
    occupied = jnp.sum(jnp.where(eye, density[0, :, at(0)], 0.0), axis=1, keepdims=True)
    lanes = charges.shape[1]
    atoms = blk // ORBS
    atom = lax.broadcasted_iota(jnp.int32, (blk, lanes), 0) // ORBS + slots[0, 0] % 2 * atoms
    lane = lax.broadcasted_iota(jnp.int32, (blk, lanes), 1)
    charges[...] = jnp.sum(
        jnp.where(atom == lane, 4.0 / ORBS - 2.0 * occupied, 0.0), axis=0, keepdims=True
    )


def pack_kernel(slots, own, earlier, *packs):
    for slot, pack in zip(slots, packs):
        for index, k in enumerate(SENT[slot]):
            pack[0, index] = own[0, k]


def packed(own, earlier, *slots):
    blk = own.shape[-1]
    vmem = pl.BlockSpec(memory_space=pltpu.VMEM)
    shape = jax.ShapeDtypeStruct((1, len(SENT[1]), blk, blk), own.dtype)
    return pl.pallas_call(
        functools.partial(pack_kernel, slots),
        out_shape=(shape,) * len(slots),
        in_specs=[vmem, pl.BlockSpec(memory_space=pl.ANY)],
        out_specs=(vmem,) * len(slots),
        name="pack_halo",
    )(own, earlier)


def order_kernel(slots, rows, out):
    device = slots[0, 0]
    y, x, core, high = device // 64, device // 16 % 4, device // 8 % 2, device // 2 % 4
    for dy in range(4):
        for dx in range(4):
            for dcore in range(2):
                for dhigh in range(4):
                    source = ((dhigh * 4 + dy) * 4 + dx) * 2 + dcore
                    target = ((lax.rem(y + 4 - dy, 4) * 4 + lax.rem(x + 4 - dx, 4)) * 2
                              + lax.rem(core + dcore, 2)) * 4 + lax.rem(high + 4 - dhigh, 4)
                    out[pl.ds(target, 1), :] = rows[source : source + 1, :]


def in_order(slots, rows):
    return pl.pallas_call(
        order_kernel,
        out_shape=jax.ShapeDtypeStruct(rows.shape, rows.dtype),
        in_specs=[
            pl.BlockSpec(memory_space=pltpu.SMEM),
            pl.BlockSpec(memory_space=pltpu.VMEM),
        ],
        out_specs=pl.BlockSpec(memory_space=pltpu.VMEM),
        name="order_charges",
    )(slots, rows)


def moved(x, n_dom, n_sub, dy, dx, flip_core, dz, flip_z):
    pairs = []
    for d in range(n_dom):
        for z in range(n_sub):
            y, col, core = d // 8, d // 2 % 4, d % 2
            to = (((y + dy) % 4 * 4 + (col + dx) % 4) * 2 + (core ^ flip_core)) * n_sub
            pairs.append((d * n_sub + z, to + ((z + dz) % n_sub ^ flip_z)))
    return lax.ppermute(x, ("dom", "sub"), pairs)


def gathered(row, n_dom, n_sub):
    def step(x, *where):
        return moved(x, n_dom, n_sub, *where)

    here = row + step(row, 0, 0, 0, 0, 1)
    there = step(row, 0, 0, 1, 0, 0) + step(row, 0, 0, 1, 0, 1)
    block = jnp.concatenate([here, there], axis=0)
    block = jnp.concatenate([block] + [step(block, 0, d, 0, 0, 0) for d in (1, 2, 3)], axis=0)
    block = jnp.concatenate([block] + [step(block, d, 0, 0, 0, 0) for d in (1, 2, 3)], axis=0)
    return jnp.concatenate([block] + [step(block, 0, 0, 0, 2 * d, 0) for d in (1, 2, 3)], axis=0)


def local_part(slots, potential, own, received):
    blk = own.shape[-1]
    order = SLOTS * blk
    vmem = pl.BlockSpec(memory_space=pltpu.VMEM)
    smem = pl.BlockSpec(memory_space=pltpu.SMEM)
    return pl.pallas_call(
        density_kernel,
        out_shape=(
            jax.ShapeDtypeStruct((1, blk, order), jnp.float32),
            jax.ShapeDtypeStruct((1, LANES), jnp.float32),
        ),
        in_specs=[smem, smem] + [vmem] * 5,
        out_specs=(vmem, vmem),
        scratch_shapes=[
            pltpu.VMEM((order, order), jnp.float32),
            pltpu.VMEM((order, order), jnp.bfloat16),
            pltpu.VMEM((order, order), jnp.bfloat16),
            pltpu.VMEM((order, order), jnp.bfloat16),
        ],
        compiler_params=pltpu.CompilerParams(vmem_limit_bytes=48 * 1024 * 1024),
        name="density_rows",
    )(slots, potential, own, *received)


def shards(hamiltonian, partitions, chemical_potential):
    n_dom = lax.axis_size("dom")
    n_sub = lax.axis_size("sub")
    blk = hamiltonian.shape[2]

    def exchanged(up, down, axis, size):
        forward = [(i, (i + 1) % size) for i in range(size)]
        return (
            lax.ppermute(up, axis, forward),
            lax.ppermute(down, axis, [(j, i) for i, j in forward]),
        )

    sub_up, sub_down = packed(hamiltonian, partitions, 3, 4)
    dom_up, dom_down = packed(hamiltonian, sub_up, 1, 2)
    r3, r4 = exchanged(sub_up, sub_down, "sub", n_sub)
    r1, r2 = exchanged(dom_up, dom_down, "dom", n_dom)
    density, row = local_part(
        partitions, chemical_potential.reshape(1, 1), hamiltonian, (r1, r2, r3, r4)
    )
    charges = in_order(partitions, gathered(row, n_dom, n_sub)).reshape(-1)
    return (density, charges)


def solution(mesh):
    return jax.shard_map(
        shards,
        mesh=mesh,
        in_specs=(P(("dom", "sub"), None, None, None), P(("dom", "sub"), None), P()),
        out_specs=(P(("dom", "sub"), None, None), P()),
        check_vma=False,
    )
```

time: 119 us -> 68.7 us (0.58)
  the two profiles are of different devices: /device:TPU:1 before, /device:TPU:32 now
where the time goes in v2:
time: 68.7 us; the launch traced here: 68.5 us
  starting transfers between devices  24.2 us (35%)
  waiting for transfers between devices  23.3 us (34%)
  Pallas kernels  15.5 us (23%)
  local copies, waits for them, and re-layouts  4.23 us (6%)
  between operations  1.33 us (2%)
    ppermute x12, starting transfers between devices, moved(): return lax.ppermute(x, ('dom', 'sub'), pairs)  17.1 us
    ppermute x12, waiting for transfers between devices, moved(): return lax.ppermute(x, ('dom', 'sub'), pairs)  15.5 us
    pallas_call x1, Pallas kernels, local_part(): pl.pallas_call(density_kernel, out_shape=(jax.ShapeDtypeStruct((1, blk, o...  9.15 us
    ppermute x2, starting transfers between devices, exchanged(): lax.ppermute(down, axis, [(j, i) for i, j in forward])  6.91 us
    pallas_call x2, Pallas kernels, packed(): pl.pallas_call(functools.partial(pack_kernel, slots), out_shape=(shape,)...  4.69 us
    concatenate x1, local copies, waits for them, and re-layouts, gathered(): jnp.concatenate([block] + [step(block, 0, 0, 0, 2 * d, 0) for d in (1, 2,...  4.17 us
    ppermute x2, waiting for transfers between devices, exchanged(): lax.ppermute(down, axis, [(j, i) for i, j in forward])  3.99 us
    ppermute x2, waiting for transfers between devices, exchanged(): lax.ppermute(up, axis, forward)  3.77 us
  transfers between devices with their start and end apart: 16, of which 10 were waited for; matrix products, arithmetic and copies ran while one was open for 0% of the time, Pallas kernels for 3%

profile of v2, /device:TPU:32, one launch (start us, length us, event | category | flops | bytes accessed | tf_op | source)
XLA Modules:
  0.0 68.5 jit_solution(8286586715418408345)
XLA Ops:
  0.6 0.0 copy-start.1
  0.6 0.0 copy-start
  0.7 2.4 %pack_halo.2 = (bf16[1,4,256,256]{3,2,1,0:T(8,128)(2,1)}, bf16[1,4,256,256]{3,2,1,0:T(8,128)(2,1)}) custom-call(bf16[1,9,256,256]{3,2,1,0:T(8,128)(2,1)} %own.5, s32[1,5]{1,0:T(1,128)} %slots.3), custom_call_target="tpu_custom_call" | custom-call | tf_op jit(solution)/shard_map/pack_halo/pallas_call | solution.py:141
  3.0 1.8 %collective-permute-start.3 = (bf16[1,4,256,256]{3,2,1,0:T(8,128)(2,1)}, bf16[1,4,256,256]{3,2,1,0:T(8,128)(2,1)S(1)}, u32[]{:S(2)}, u32[]{:S(2)}) collective-permute-start(bf16[1,4,256,256]{3,2,1,0:T(8,128)(2,1)} %get-tuple-element.11), channel_id=1, source_target_pairs={{1,0},{2,1},{3,2},{4,3},{5,4},{6,5},{7,6},{0,7},{9,8},{10,9},{11,1... | collective-permute-start | bytes 1572872 | tf_op jit(solution)/shard_map/ppermute | solution.py:231
  4.9 0.2 collective-permute-start.2
  5.1 2.3 %pack_halo.3 = (bf16[1,4,256,256]{3,2,1,0:T(8,128)(2,1)}, bf16[1,4,256,256]{3,2,1,0:T(8,128)(2,1)}) custom-call(bf16[1,9,256,256]{3,2,1,0:T(8,128)(2,1)} %own.5, bf16[1,4,256,256]{3,2,1,0:T(8,128)(2,1)} %get-tuple-element.8.earlier), custom_call_target="tpu_custom_call" | custom-call | tf_op jit(solution)/shard_map/pack_halo/pallas_call | solution.py:141
  7.4 0.0 collective-permute-start
  7.4 5.1 %collective-permute-start.1 = (bf16[1,4,256,256]{3,2,1,0:T(8,128)(2,1)}, bf16[1,4,256,256]{3,2,1,0:T(8,128)(2,1)S(1)}, u32[]{:S(2)}, u32[]{:S(2)}) collective-permute-start(bf16[1,4,256,256]{3,2,1,0:T(8,128)(2,1)} %get-tuple-element.10), channel_id=1, source_target_pairs={{8,0},{16,8},{24,16},{32,24},{40,32},{48,40},{56,48},{64,56},{72,6... | collective-permute-start | bytes 1572872 | tf_op jit(solution)/shard_map/ppermute | solution.py:231
  13.1 4.0 %collective-permute-done.3.r4 = bf16[1,4,256,256]{3,2,1,0:T(8,128)(2,1)S(1)} collective-permute-done((bf16[1,4,256,256]{3,2,1,0:T(8,128)(2,1)}, bf16[1,4,256,256]{3,2,1,0:T(8,128)(2,1)S(1)}, u32[]{:S(2)}, u32[]{:S(2)}) %collective-permute-start.3) | collective-permute-done | bytes 524320 | tf_op jit(solution)/shard_map/ppermute | solution.py:231
  17.1 3.8 %collective-permute-done.2.r3 = bf16[1,4,256,256]{3,2,1,0:T(8,128)(2,1)S(1)} collective-permute-done((bf16[1,4,256,256]{3,2,1,0:T(8,128)(2,1)}, bf16[1,4,256,256]{3,2,1,0:T(8,128)(2,1)S(1)}, u32[]{:S(2)}, u32[]{:S(2)}) %collective-permute-start.2) | collective-permute-done | bytes 524320 | tf_op jit(solution)/shard_map/ppermute | solution.py:230
  20.8 0.0 collective-permute-done.r1
  20.8 0.0 collective-permute-done.1.r2
  20.8 0.0 copy-done.1
  20.9 0.0 copy-done
  20.9 9.2 %density_rows.1 = (f32[1,256,1280]{2,1,0:T(8,128)}, f32[1,128]{1,0:T(1,128)S(1)}) custom-call(s32[1,5]{1,0:T(1,128)S(1)} %copy-done.1, f32[1,1]{1,0:T(1,128)} %bitcast.2.potential, bf16[1,9,256,256]{3,2,1,0:T(8,128)(2,1)S(1)} %copy-done, bf16[1,4,256,256]{3,2,1,0:T(8,128)(2,1)S(1)} %collective-permute-done.r1, ...), custom_call_target="tpu_custom_call" | custom-call | tf_op jit(solution)/shard_map/density_rows/pallas_call | solution.py:203
  30.0 2.9 %collective-permute-start.4 = (f32[1,128]{1,0:T(1,128)S(1)}, f32[1,128]{1,0:T(1,128)S(1)}, u32[]{:S(2)}, u32[]{:S(2)}) collective-permute-start(f32[1,128]{1,0:T(1,128)S(1)} %get-tuple-element.13), channel_id=1, source_target_pairs={{0,1},{1,0},{2,3},{3,2},{4,5},{5,4},{6,7},{7,6},{8,9},{9,8},{10,11... | collective-permute-start | bytes 1544 | tf_op jit(solution)/shard_map/ppermute | solution.py:183
  33.0 0.0 collective-permute-start.6
  33.0 0.1 collective-permute-start.5
  33.1 1.4 %collective-permute-done.4 = f32[1,128]{1,0:T(1,128)S(1)} collective-permute-done((f32[1,128]{1,0:T(1,128)S(1)}, f32[1,128]{1,0:T(1,128)S(1)}, u32[]{:S(2)}, u32[]{:S(2)}) %collective-permute-start.4) | collective-permute-done | bytes 544 | tf_op jit(solution)/shard_map/ppermute | solution.py:183
  34.5 1.4 %collective-permute-done.6 = f32[1,128]{1,0:T(1,128)S(1)} collective-permute-done((f32[1,128]{1,0:T(1,128)S(1)}, f32[1,128]{1,0:T(1,128)S(1)}, u32[]{:S(2)}, u32[]{:S(2)}) %collective-permute-start.6) | collective-permute-done | bytes 544 | tf_op jit(solution)/shard_map/ppermute | solution.py:183
  35.9 0.0 collective-permute-done.5
  35.9 3.0 %collective-permute-start.9 = (f32[2,128]{1,0:T(2,128)S(1)}, f32[2,128]{1,0:T(2,128)S(1)}, u32[]{:S(2)}, u32[]{:S(2)}) collective-permute-start(f32[2,128]{1,0:T(2,128)S(1)} %pad_maximum_fusion), channel_id=1, source_target_pairs={{0,48},{1,49},{2,50},{3,51},{4,52},{5,53},{6,54},{7,55},{8,56},{9,... | collective-permute-start | bytes 3080 | tf_op jit(solution)/shard_map/ppermute | solution.py:183
  39.0 0.8 %collective-permute-start.8 = (f32[2,128]{1,0:T(2,128)S(1)}, f32[2,128]{1,0:T(2,128)S(1)}, u32[]{:S(2)}, u32[]{:S(2)}) collective-permute-start(f32[2,128]{1,0:T(2,128)S(1)} %pad_maximum_fusion), channel_id=1, source_target_pairs={{0,32},{1,33},{2,34},{3,35},{4,36},{5,37},{6,38},{7,39},{8,40},{9,... | collective-permute-start | bytes 3080 | tf_op jit(solution)/shard_map/ppermute | solution.py:183
  39.8 0.9 %collective-permute-start.7 = (f32[2,128]{1,0:T(2,128)S(1)}, f32[2,128]{1,0:T(2,128)S(1)}, u32[]{:S(2)}, u32[]{:S(2)}) collective-permute-start(f32[2,128]{1,0:T(2,128)S(1)} %pad_maximum_fusion), channel_id=1, source_target_pairs={{0,16},{1,17},{2,18},{3,19},{4,20},{5,21},{6,22},{7,23},{8,24},{9,... | collective-permute-start | bytes 3080 | tf_op jit(solution)/shard_map/ppermute | solution.py:183
  40.7 0.0 collective-permute-done.9
  40.7 3.4 %collective-permute-done.8 = f32[2,128]{1,0:T(2,128)S(1)} collective-permute-done((f32[2,128]{1,0:T(2,128)S(1)}, f32[2,128]{1,0:T(2,128)S(1)}, u32[]{:S(2)}, u32[]{:S(2)}) %collective-permute-start.8) | collective-permute-done | bytes 1056 | tf_op jit(solution)/shard_map/ppermute | solution.py:183
  44.0 0.5 collective-permute-done.7
  44.6 3.1 %collective-permute-start.12 = (f32[8,128]{1,0:T(8,128)S(1)}, f32[8,128]{1,0:T(8,128)S(1)}, u32[]{:S(2)}, u32[]{:S(2)}) collective-permute-start(f32[8,128]{1,0:T(8,128)S(1)} %concatenate.16), channel_id=1, source_target_pairs={{0,192},{1,193},{2,194},{3,195},{4,196},{5,197},{6,198},{7,199},{8... | collective-permute-start | bytes 12296 | tf_op jit(solution)/shard_map/ppermute | solution.py:183
  47.7 0.6 collective-permute-start.11
  48.3 1.0 %collective-permute-start.10 = (f32[8,128]{1,0:T(8,128)S(1)}, f32[8,128]{1,0:T(8,128)S(1)}, u32[]{:S(2)}, u32[]{:S(2)}) collective-permute-start(f32[8,128]{1,0:T(8,128)S(1)} %concatenate.16), channel_id=1, source_target_pairs={{0,64},{1,65},{2,66},{3,67},{4,68},{5,69},{6,70},{7,71},{8,72},{9,... | collective-permute-start | bytes 12296 | tf_op jit(solution)/shard_map/ppermute | solution.py:183
  49.3 0.0 collective-permute-done.12
  49.3 3.5 %collective-permute-done.11 = f32[8,128]{1,0:T(8,128)S(1)} collective-permute-done((f32[8,128]{1,0:T(8,128)S(1)}, f32[8,128]{1,0:T(8,128)S(1)}, u32[]{:S(2)}, u32[]{:S(2)}) %collective-permute-start.11) | collective-permute-done | bytes 4128 | tf_op jit(solution)/shard_map/ppermute | solution.py:183
  52.8 0.3 collective-permute-done.10
  53.1 1.9 %collective-permute-start.15 = (f32[32,128]{1,0:T(8,128)S(1)}, f32[32,128]{1,0:T(8,128)S(1)}, u32[]{:S(2)}, u32[]{:S(2)}) collective-permute-start(f32[32,128]{1,0:T(8,128)S(1)} %concatenate.17), channel_id=1, source_target_pairs={{0,6},{1,7},{2,0},{3,1},{4,2},{5,3},{6,4},{7,5},{8,14},{9,15},{10,... | collective-permute-start | bytes 49160 | tf_op jit(solution)/shard_map/ppermute | solution.py:183
  55.1 1.4 %collective-permute-start.14 = (f32[32,128]{1,0:T(8,128)S(1)}, f32[32,128]{1,0:T(8,128)S(1)}, u32[]{:S(2)}, u32[]{:S(2)}) collective-permute-start(f32[32,128]{1,0:T(8,128)S(1)} %concatenate.17), channel_id=1, source_target_pairs={{0,4},{1,5},{2,6},{3,7},{4,0},{5,1},{6,2},{7,3},{8,12},{9,13},{10,... | collective-permute-start | bytes 49160 | tf_op jit(solution)/shard_map/ppermute | solution.py:183
  56.5 1.2 %collective-permute-start.13 = (f32[32,128]{1,0:T(8,128)S(1)}, f32[32,128]{1,0:T(8,128)S(1)}, u32[]{:S(2)}, u32[]{:S(2)}) collective-permute-start(f32[32,128]{1,0:T(8,128)S(1)} %concatenate.17), channel_id=1, source_target_pairs={{0,2},{1,3},{2,4},{3,5},{4,6},{5,7},{6,0},{7,1},{8,10},{9,11},{10,... | collective-permute-start | bytes 49160 | tf_op jit(solution)/shard_map/ppermute | solution.py:183
  57.7 0.1 collective-permute-done.15
  57.8 4.9 %collective-permute-done.14 = f32[32,128]{1,0:T(8,128)S(1)} collective-permute-done((f32[32,128]{1,0:T(8,128)S(1)}, f32[32,128]{1,0:T(8,128)S(1)}, u32[]{:S(2)}, u32[]{:S(2)}) %collective-permute-start.14) | collective-permute-done | bytes 16416 | tf_op jit(solution)/shard_map/ppermute | solution.py:183
  62.7 0.0 collective-permute-done.13
  62.7 4.2 %concatenate.18.rows = f32[128,128]{1,0:T(8,128)} concatenate(f32[1,128]{1,0:T(1,128)S(1)} %add.6, f32[1,128]{1,0:T(1,128)S(1)} %add.7, f32[2,128]{1,0:T(2,128)S(1)} %collective-permute-done.7, f32[2,128]{1,0:T(2,128)S(1)} %collective-permute-done.8, f32[2,128]{1,0:T(2,128)S(1)} %collective-permute-done.9, f32[8,128]{1,0:T(8,128)S(1)} %collective-permute-done.10, ...), dimensions={0} | concatenate | bytes 131072 | tf_op jit(solution)/shard_map/concatenate | solution.py:195
  66.9 1.6 %order_charges.1 = f32[128,128]{1,0:T(8,128)} custom-call(s32[1,5]{1,0:T(1,128)} %slots.3, f32[128,128]{1,0:T(8,128)} %concatenate.18.rows), custom_call_target="tpu_custom_call" | custom-call | tf_op jit(solution)/shard_map/order_charges/pallas_call | solution.py:164
  (5 shorter events, 0.1 us)
Async XLA Ops:
  0.6 20.2 %copy-start.1 = (s32[1,5]{1,0:T(1,128)S(1)}, s32[1,5]{1,0:T(1,128)}, u32[]{:S(2)}) copy-start(s32[1,5]{1,0:T(1,128)} %slots.3) | copy-start | bytes 64
  0.6 20.2 %copy-start = (bf16[1,9,256,256]{3,2,1,0:T(8,128)(2,1)S(1)}, bf16[1,9,256,256]{3,2,1,0:T(8,128)(2,1)}, u32[]{:S(2)}) copy-start(bf16[1,9,256,256]{3,2,1,0:T(8,128)(2,1)} %own.5) | copy-start | bytes 3538948
  3.0 14.0 %collective-permute-start.3 = (bf16[1,4,256,256]{3,2,1,0:T(8,128)(2,1)}, bf16[1,4,256,256]{3,2,1,0:T(8,128)(2,1)S(1)}, u32[]{:S(2)}, u32[]{:S(2)}) collective-permute-start(bf16[1,4,256,256]{3,2,1,0:T(8,128)(2,1)} %get-tuple-element.11), channel_id=1, source_target_pairs={{1,0},{2,1},{3,2},{4,3},{5,4},{6,5},{7,6},{0,7},{9,8},{10,9},{11,1... | collective-permute-start | bytes 1572872 | tf_op jit(solution)/shard_map/ppermute | solution.py:231
  4.9 16.0 %collective-permute-start.2 = (bf16[1,4,256,256]{3,2,1,0:T(8,128)(2,1)}, bf16[1,4,256,256]{3,2,1,0:T(8,128)(2,1)S(1)}, u32[]{:S(2)}, u32[]{:S(2)}) collective-permute-start(bf16[1,4,256,256]{3,2,1,0:T(8,128)(2,1)} %get-tuple-element.8.earlier), channel_id=1, source_target_pairs={{0,1},{1,2},{2,3},{3,4},{4,5},{5,6},{6,7},{7,0},{8,9},{9,10},{10,1... | collective-permute-start | bytes 1572872 | tf_op jit(solution)/shard_map/ppermute | solution.py:230
  7.4 13.5 %collective-permute-start = (bf16[1,4,256,256]{3,2,1,0:T(8,128)(2,1)}, bf16[1,4,256,256]{3,2,1,0:T(8,128)(2,1)S(1)}, u32[]{:S(2)}, u32[]{:S(2)}) collective-permute-start(bf16[1,4,256,256]{3,2,1,0:T(8,128)(2,1)} %get-tuple-element.9), channel_id=1, source_target_pairs={{0,8},{8,16},{16,24},{24,32},{32,40},{40,48},{48,56},{56,64},{64,7... | collective-permute-start | bytes 1572872 | tf_op jit(solution)/shard_map/ppermute | solution.py:230
  7.4 13.5 %collective-permute-start.1 = (bf16[1,4,256,256]{3,2,1,0:T(8,128)(2,1)}, bf16[1,4,256,256]{3,2,1,0:T(8,128)(2,1)S(1)}, u32[]{:S(2)}, u32[]{:S(2)}) collective-permute-start(bf16[1,4,256,256]{3,2,1,0:T(8,128)(2,1)} %get-tuple-element.10), channel_id=1, source_target_pairs={{8,0},{16,8},{24,16},{32,24},{40,32},{48,40},{56,48},{64,56},{72,6... | collective-permute-start | bytes 1572872 | tf_op jit(solution)/shard_map/ppermute | solution.py:231
  30.0 4.5 %collective-permute-start.4 = (f32[1,128]{1,0:T(1,128)S(1)}, f32[1,128]{1,0:T(1,128)S(1)}, u32[]{:S(2)}, u32[]{:S(2)}) collective-permute-start(f32[1,128]{1,0:T(1,128)S(1)} %get-tuple-element.13), channel_id=1, source_target_pairs={{0,1},{1,0},{2,3},{3,2},{4,5},{5,4},{6,7},{7,6},{8,9},{9,8},{10,11... | collective-permute-start | bytes 1544 | tf_op jit(solution)/shard_map/ppermute | solution.py:183
  33.0 3.0 %collective-permute-start.6 = (f32[1,128]{1,0:T(1,128)S(1)}, f32[1,128]{1,0:T(1,128)S(1)}, u32[]{:S(2)}, u32[]{:S(2)}) collective-permute-start(f32[1,128]{1,0:T(1,128)S(1)} %get-tuple-element.13), channel_id=1, source_target_pairs={{0,9},{1,8},{2,11},{3,10},{4,13},{5,12},{6,15},{7,14},{8,1},{9,0},... | collective-permute-start | bytes 1544 | tf_op jit(solution)/shard_map/ppermute | solution.py:183
  33.0 3.0 %collective-permute-start.5 = (f32[1,128]{1,0:T(1,128)S(1)}, f32[1,128]{1,0:T(1,128)S(1)}, u32[]{:S(2)}, u32[]{:S(2)}) collective-permute-start(f32[1,128]{1,0:T(1,128)S(1)} %get-tuple-element.13), channel_id=1, source_target_pairs={{0,8},{1,9},{2,10},{3,11},{4,12},{5,13},{6,14},{7,15},{8,0},{9,1},... | collective-permute-start | bytes 1544 | tf_op jit(solution)/shard_map/ppermute | solution.py:183
  35.9 4.7 %collective-permute-start.9 = (f32[2,128]{1,0:T(2,128)S(1)}, f32[2,128]{1,0:T(2,128)S(1)}, u32[]{:S(2)}, u32[]{:S(2)}) collective-permute-start(f32[2,128]{1,0:T(2,128)S(1)} %pad_maximum_fusion), channel_id=1, source_target_pairs={{0,48},{1,49},{2,50},{3,51},{4,52},{5,53},{6,54},{7,55},{8,56},{9,... | collective-permute-start | bytes 3080 | tf_op jit(solution)/shard_map/ppermute | solution.py:183
  39.0 5.1 %collective-permute-start.8 = (f32[2,128]{1,0:T(2,128)S(1)}, f32[2,128]{1,0:T(2,128)S(1)}, u32[]{:S(2)}, u32[]{:S(2)}) collective-permute-start(f32[2,128]{1,0:T(2,128)S(1)} %pad_maximum_fusion), channel_id=1, source_target_pairs={{0,32},{1,33},{2,34},{3,35},{4,36},{5,37},{6,38},{7,39},{8,40},{9,... | collective-permute-start | bytes 3080 | tf_op jit(solution)/shard_map/ppermute | solution.py:183
  39.8 4.8 %collective-permute-start.7 = (f32[2,128]{1,0:T(2,128)S(1)}, f32[2,128]{1,0:T(2,128)S(1)}, u32[]{:S(2)}, u32[]{:S(2)}) collective-permute-start(f32[2,128]{1,0:T(2,128)S(1)} %pad_maximum_fusion), channel_id=1, source_target_pairs={{0,16},{1,17},{2,18},{3,19},{4,20},{5,21},{6,22},{7,23},{8,24},{9,... | collective-permute-start | bytes 3080 | tf_op jit(solution)/shard_map/ppermute | solution.py:183
  44.6 4.7 %collective-permute-start.12 = (f32[8,128]{1,0:T(8,128)S(1)}, f32[8,128]{1,0:T(8,128)S(1)}, u32[]{:S(2)}, u32[]{:S(2)}) collective-permute-start(f32[8,128]{1,0:T(8,128)S(1)} %concatenate.16), channel_id=1, source_target_pairs={{0,192},{1,193},{2,194},{3,195},{4,196},{5,197},{6,198},{7,199},{8... | collective-permute-start | bytes 12296 | tf_op jit(solution)/shard_map/ppermute | solution.py:183
  47.7 5.1 %collective-permute-start.11 = (f32[8,128]{1,0:T(8,128)S(1)}, f32[8,128]{1,0:T(8,128)S(1)}, u32[]{:S(2)}, u32[]{:S(2)}) collective-permute-start(f32[8,128]{1,0:T(8,128)S(1)} %concatenate.16), channel_id=1, source_target_pairs={{0,128},{1,129},{2,130},{3,131},{4,132},{5,133},{6,134},{7,135},{8... | collective-permute-start | bytes 12296 | tf_op jit(solution)/shard_map/ppermute | solution.py:183
  48.3 4.8 %collective-permute-start.10 = (f32[8,128]{1,0:T(8,128)S(1)}, f32[8,128]{1,0:T(8,128)S(1)}, u32[]{:S(2)}, u32[]{:S(2)}) collective-permute-start(f32[8,128]{1,0:T(8,128)S(1)} %concatenate.16), channel_id=1, source_target_pairs={{0,64},{1,65},{2,66},{3,67},{4,68},{5,69},{6,70},{7,71},{8,72},{9,... | collective-permute-start | bytes 12296 | tf_op jit(solution)/shard_map/ppermute | solution.py:183
  53.1 4.7 %collective-permute-start.15 = (f32[32,128]{1,0:T(8,128)S(1)}, f32[32,128]{1,0:T(8,128)S(1)}, u32[]{:S(2)}, u32[]{:S(2)}) collective-permute-start(f32[32,128]{1,0:T(8,128)S(1)} %concatenate.17), channel_id=1, source_target_pairs={{0,6},{1,7},{2,0},{3,1},{4,2},{5,3},{6,4},{7,5},{8,14},{9,15},{10,... | collective-permute-start | bytes 49160 | tf_op jit(solution)/shard_map/ppermute | solution.py:183
  55.1 7.6 %collective-permute-start.14 = (f32[32,128]{1,0:T(8,128)S(1)}, f32[32,128]{1,0:T(8,128)S(1)}, u32[]{:S(2)}, u32[]{:S(2)}) collective-permute-start(f32[32,128]{1,0:T(8,128)S(1)} %concatenate.17), channel_id=1, source_target_pairs={{0,4},{1,5},{2,6},{3,7},{4,0},{5,1},{6,2},{7,3},{8,12},{9,13},{10,... | collective-permute-start | bytes 49160 | tf_op jit(solution)/shard_map/ppermute | solution.py:183
  56.5 6.2 %collective-permute-start.13 = (f32[32,128]{1,0:T(8,128)S(1)}, f32[32,128]{1,0:T(8,128)S(1)}, u32[]{:S(2)}, u32[]{:S(2)}) collective-permute-start(f32[32,128]{1,0:T(8,128)S(1)} %concatenate.17), channel_id=1, source_target_pairs={{0,2},{1,3},{2,4},{3,5},{4,6},{5,7},{6,0},{7,1},{8,10},{9,11},{10,... | collective-permute-start | bytes 49160 | tf_op jit(solution)/shard_map/ppermute | solution.py:183

commit v3 on v0

v3 whole, which is shorter than its diff:
```python
import functools

import jax
import jax.numpy as jnp
from jax import lax
from jax.experimental import pallas as pl
from jax.experimental.pallas import tpu as pltpu
from jax.sharding import PartitionSpec as P

ORBS = 4
SLOTS = 5
LANES = 128
MIB = 1024 * 1024
STEPS = ((0, 0), (-1, 0), (1, 0), (0, -1), (0, 1))
SENT = {1: (4, 7, 6, 8), 2: (4, 1, 0, 2), 3: (4, 5, 2, 8), 4: (4, 3, 0, 6)}
ORDER = (0, 3, 4, 1, 2)
EARLY = (0, 1, 2)


def tile_of(i, j):
    da = STEPS[j][0] - STEPS[i][0]
    db = STEPS[j][1] - STEPS[i][1]
    if abs(da) > 1 or abs(db) > 1:
        return None
    return (da + 1) * 3 + db + 1


PAIRS = [
    (ORDER[p], ORDER[q])
    for p in range(SLOTS)
    for q in range(p, SLOTS)
    if tile_of(ORDER[p], ORDER[q]) is not None
]
EARLY_PAIRS = [pair for pair in PAIRS if pair[0] in EARLY and pair[1] in EARLY]
LATE_PAIRS = [pair for pair in PAIRS if pair not in EARLY_PAIRS]
TURNED = [(i, j) for i, j in LATE_PAIRS if j in EARLY]


def runs(blocks):
    found = []
    for k in blocks:
        if found and found[-1][1] == k:
            found[-1][1] = k + 1
        else:
            found.append([k, k + 1])
    return found


def added(old, new):
    return new if old is None else old + new


class Halo:
    def __init__(self, slots, potential, own, received):
        self.own, self.received = own, received
        blk = own.shape[-1]
        rows = lax.broadcasted_iota(jnp.int32, (blk, blk), 0)
        self.eye = rows == lax.broadcasted_iota(jnp.int32, (blk, blk), 1)
        self.live = [(slots[0, i] >= 0).astype(jnp.float32) for i in range(SLOTS)]
        self.potential = potential[0, 0]
        self.row_sums = [None] * SLOTS
        self.col_sums = [None] * SLOTS

    def tile(self, i, j):
        k = tile_of(i, j)
        if i == 0:
            return self.own[0, k]
        parts = self.received[i]
        place = SENT[i].index(k)
        return parts[place // parts[0].shape[1]][0, place % parts[0].shape[1]]

    def block(self, i, j, turned=None):
        if turned is None:
            turned = self.tile(j, i).T
        both = self.tile(i, j).astype(jnp.float32) + turned.astype(jnp.float32)
        if i == j:
            block = (jnp.where(self.eye, self.potential, 0.0) - 0.5 * both) * self.live[i]
        else:
            block = both * (-0.5 * self.live[i] * self.live[j])
        squares = block * block
        folded = squares[:, :LANES]
        for lane in range(LANES, squares.shape[1], LANES):
            folded = folded + squares[:, lane : lane + LANES]
        self.row_sums[i] = added(self.row_sums[i], folded)
        if i != j:
            self.col_sums[j] = added(self.col_sums[j], jnp.sum(squares, axis=0, keepdims=True))
        return block

    def sums(self, i):
        total = self.row_sums[i]
        if total is not None:
            total = jnp.sum(total, axis=1, keepdims=True)
        if self.col_sums[i] is not None:
            turned = jnp.sum(jnp.where(self.eye, self.col_sums[i], 0.0), axis=1, keepdims=True)
            total = added(total, turned)
        return total


def early_kernel(slots, potential, own, r1a, r1b, r2a, r2b, blocks, turned, sums):
    halo = Halo(slots, potential, own, {1: (r1a, r1b), 2: (r2a, r2b)})
    for place, (i, j) in enumerate(TURNED):
        turned[place] = halo.tile(j, i).T
    for place, (i, j) in enumerate(EARLY_PAIRS):
        blocks[place] = halo.block(i, j)
    lane = lax.broadcasted_iota(jnp.int32, sums.shape, 1)
    total = jnp.zeros(sums.shape, jnp.float32)
    for i in EARLY:
        total = jnp.where(lane == i, halo.sums(i), total)
    sums[...] = total


def late_kernel(
    slots, potential, own, early, turned, sums, r3, r4, density, charges,
    x0, x0b, q0b, x1b, out, sems,
):
    blk = own.shape[-1]
    f32, bf16 = jnp.float32, jnp.bfloat16
    halo = Halo(slots, potential, own, {3: (r3,), 4: (r4,)})
    eye = halo.eye

    def at(p, q=None):
        return slice(p * blk, (p + 1 if q is None else q) * blk)

    def coupled(p, q):
        return tile_of(ORDER[p], ORDER[q]) is not None

    def product(left, right, p, q):
        inner = [
            k for k in range(SLOTS)
            if (left is not x0b or coupled(p, k)) and (right is not x0b or coupled(k, q))
        ]
        total = None
        for lo, hi in runs(inner):
            term = jnp.dot(left[at(p), at(lo, hi)], right[at(lo, hi), at(q)], preferred_element_type=f32)
            total = added(total, term)
        return total

    def mirror(target, p, q, block):
        rounded = block.astype(bf16)
        target[at(p), at(q)] = rounded
        if p != q:
            target[at(q), at(p)] = rounded.T

    def place(i, j):
        return ORDER.index(i), ORDER.index(j)

    for i, j in LATE_PAIRS:
        p, q = place(i, j)
        x0[at(p), at(q)] = halo.block(i, j, turned[TURNED.index((i, j))] if (i, j) in TURNED else None)
    largest = None
    for i in range(SLOTS):
        total = halo.sums(i)
        if i in EARLY:
            total = added(sums[:, i : i + 1], total) if total is not None else sums[:, i : i + 1]
        top = jnp.max(total, axis=0, keepdims=True)
        largest = top if largest is None else jnp.maximum(largest, top)
    inv = 1.0 / (2.0 * jnp.sqrt(largest + 1e-06))

    for i, j in PAIRS:
        p, q = place(i, j)
        if (i, j) in EARLY_PAIRS:
            block = early[EARLY_PAIRS.index((i, j))] * inv
        else:
            block = x0[at(p), at(q)] * inv
        x0[at(p), at(q)] = block
        mirror(x0b, p, q, block)
    upper = [(p, q) for p in range(SLOTS) for q in range(p, SLOTS)]
    for p, q in upper:
        mirror(q0b, p, q, product(x0b, x0b, p, q))
    for p, q in upper:
        block = -0.5 * product(x0b, q0b, p, q)
        if coupled(p, q):
            block = 1.5 * x0[at(p), at(q)] + block
        if p == 0:
            x0[at(0), at(q)] = block
        mirror(x1b, p, q, block)
    left = jnp.concatenate(
        [product(x1b, x1b, 0, q).astype(bf16) for q in range(SLOTS)], axis=1
    )
    copies = []
    for q in range(SLOTS):
        sign = 1.5 * x0[at(0), at(q)] - 0.5 * jnp.dot(
            left, x1b[:, at(q)], preferred_element_type=f32
        )
        if q == 0:
            sign = jnp.where(eye, 1.0 + sign, sign)
        result = 0.5 * sign
        out[q] = result
        copy = pltpu.make_async_copy(
            out.at[q], density.at[0, :, pl.ds(ORDER[q] * blk, blk)], sems.at[q]
        )
        copy.start()
        copies.append(copy)
        if q == 0:
            occupied = jnp.sum(jnp.where(eye, result, 0.0), axis=1, keepdims=True)
            lanes = charges.shape[1]
            atoms = blk // ORBS
            atom = lax.broadcasted_iota(jnp.int32, (blk, lanes), 0) // ORBS + slots[0, 0] % 2 * atoms
            lane = lax.broadcasted_iota(jnp.int32, (blk, lanes), 1)
            charges[...] = jnp.sum(
                jnp.where(atom == lane, 4.0 / ORBS - 2.0 * occupied, 0.0), axis=0, keepdims=True
            )
    for copy in copies:
        copy.wait()


VMEM = pl.BlockSpec(memory_space=pltpu.VMEM)
SMEM = pl.BlockSpec(memory_space=pltpu.SMEM)
ANY = pl.BlockSpec(memory_space=pl.ANY)


SMALL = pl.CostEstimate(flops=1, bytes_accessed=1, transcendentals=0)


def limit(mib):
    return pltpu.CompilerParams(vmem_limit_bytes=mib * MIB)


def early_part(slots, potential, own, *halves):
    blk = own.shape[-1]
    return pl.pallas_call(
        early_kernel,
        out_shape=(
            jax.ShapeDtypeStruct((len(EARLY_PAIRS), blk, blk), jnp.float32),
            jax.ShapeDtypeStruct((len(TURNED), blk, blk), own.dtype),
            jax.ShapeDtypeStruct((blk, LANES), jnp.float32),
        ),
        in_specs=[SMEM, SMEM] + [VMEM] * 5,
        out_specs=(VMEM, VMEM, VMEM),
        compiler_params=limit(12),
        cost_estimate=SMALL,
        name="early_blocks",
    )(slots, potential, own, *halves)


def late_part(slots, potential, own, early, turned, sums, r3, r4):
    blk = own.shape[-1]
    order = SLOTS * blk
    return pl.pallas_call(
        late_kernel,
        out_shape=(
            jax.ShapeDtypeStruct((1, blk, order), jnp.float32),
            jax.ShapeDtypeStruct((1, LANES), jnp.float32),
        ),
        in_specs=[SMEM, SMEM] + [VMEM] * 6,
        out_specs=(ANY, VMEM),
        scratch_shapes=[
            pltpu.VMEM((order, order), jnp.float32),
            pltpu.VMEM((order, order), jnp.bfloat16),
            pltpu.VMEM((order, order), jnp.bfloat16),
            pltpu.VMEM((order, order), jnp.bfloat16),
            pltpu.VMEM((SLOTS, blk, blk), jnp.float32),
            pltpu.SemaphoreType.DMA((SLOTS,)),
        ],
        compiler_params=limit(32),
        name="density_rows",
    )(slots, potential, own, early, turned, sums, r3, r4)


def pack_kernel(groups, own, earlier, *packs):
    for group, pack in zip(groups, packs):
        for index, k in enumerate(group):
            pack[0, index] = own[0, k]


def packed(own, earlier, *groups):
    blk = own.shape[-1]
    return pl.pallas_call(
        functools.partial(pack_kernel, groups),
        out_shape=tuple(
            jax.ShapeDtypeStruct((1, len(group), blk, blk), own.dtype) for group in groups
        ),
        in_specs=[VMEM, ANY],
        out_specs=(VMEM,) * len(groups),
        compiler_params=limit(4),
        cost_estimate=SMALL,
        name="pack_halo",
    )(own, earlier)


def pair_kernel(rows, out):
    half = out.shape[0]
    out[...] = rows[pl.ds(0, half, stride=2), :] + rows[pl.ds(1, half, stride=2), :]


def paired(rows):
    return pl.pallas_call(
        pair_kernel,
        out_shape=jax.ShapeDtypeStruct((rows.shape[0] // 2, rows.shape[1]), rows.dtype),
        in_specs=[VMEM],
        out_specs=VMEM,
        compiler_params=limit(2),
        name="pair_charges",
    )(rows)


def shards(hamiltonian, partitions, chemical_potential):
    n_dom = lax.axis_size("dom")
    n_sub = lax.axis_size("sub")
    potential = chemical_potential.reshape(1, 1)

    def up(x, axis, size):
        return lax.ppermute(x, axis, [(i, (i + 1) % size) for i in range(size)])

    def down(x, axis, size):
        return lax.ppermute(x, axis, [((i + 1) % size, i) for i in range(size)])

    sub_up, sub_down = packed(hamiltonian, hamiltonian, SENT[3], SENT[4])
    dom_parts = packed(
        hamiltonian, sub_up, SENT[1][:2], SENT[1][2:], SENT[2][:2], SENT[2][2:]
    )
    r3, r4 = up(sub_up, "sub", n_sub), down(sub_down, "sub", n_sub)
    halves = [up(x, "dom", n_dom) for x in dom_parts[:2]]
    halves += [down(x, "dom", n_dom) for x in dom_parts[2:]]
    early, turned, sums = early_part(partitions, potential, hamiltonian, *halves)
    density, row = late_part(
        partitions, potential, hamiltonian, early, turned, sums, r3, r4
    )
    copies = jnp.broadcast_to(row, (n_dom * n_sub, LANES))
    rows = lax.all_to_all(copies, ("dom", "sub"), 0, 0, tiled=True)
    charges = paired(rows).reshape(-1)
    return (density, charges)


def solution(mesh):
    return jax.shard_map(
        shards,
        mesh=mesh,
        in_specs=(P(("dom", "sub"), None, None, None), P(("dom", "sub"), None), P()),
        out_specs=(P(("dom", "sub"), None, None), P()),
        check_vma=False,
    )
```

time: 374 us -> 57.2 us (0.15)
  waiting for transfers between devices: 243 us -> 7.97 us
  matrix products: 52.8 us -> 0 us
  between operations: 37.1 us -> 1.33 us
  local copies, waits for them, and re-layouts: 24.1 us -> 1.34 us
  blocking collectives: 0 us -> 21.7 us
  Pallas kernels: 0 us -> 12.3 us
  other arithmetic: 8.5 us -> 0 us
  starting transfers between devices: 7.62 us -> 12.4 us
    unnamed x2 -> x0, waiting for transfers between devices: 243 us -> none
    dot_general x8 -> x0, matrix products: 52.8 us -> none  [the longest x5 15.9 us: shards(): jnp.einsum('pkj,pkab->pajb', matches, sources[slot], preferred_element_ty...]
    all_to_all x0 -> x1, blocking collectives: none -> 21.7 us  [shards(): rows = lax.all_to_all(copies, ('dom', 'sub'), 0, 0, tiled=True)]
    reshape x3 -> x0, local copies, waits for them, and re-layouts: 18 us -> none  [the longest x2 17.9 us: shards(): jnp.stack(pieces, axis=1)]
    pallas_call x0 -> x5, Pallas kernels: none -> 12.3 us  [the longest x1 8.25 us: late_part(): pl.pallas_call(late_kernel, out_shape=(jax.ShapeDtypeStruct((1, blk, orde...]
    ppermute x4 -> x6, waiting for transfers between devices: 0.01 us -> 7.97 us  [the longest x3 4.85 us: down(): return lax.ppermute(x, axis, [((i + 1) % size, i) for i in range(size)])]
    reduce_sum x2 -> x0, other arithmetic: 6.34 us -> none  [the longest x1 6.23 us: density_rows(): jnp.sum(shifted * shifted, axis=2)]
    ppermute x4 -> x6, starting transfers between devices: 7.58 us -> 12.4 us  [the longest x3 9.55 us: down(): return lax.ppermute(x, axis, [((i + 1) % size, i) for i in range(size)])]
  transfers between devices with their start and end apart: 5 -> 6, of which waited for: 1 -> 4; matrix products, arithmetic and copies ran while one was open for 4% -> 0% of each run, Pallas kernels for 0% -> 3%
where the time goes in v3:
time: 57.2 us; the launch traced here: 57.1 us
  blocking collectives  21.7 us (38%)
  starting transfers between devices  12.4 us (22%)
  Pallas kernels  12.3 us (22%)
  waiting for transfers between devices  7.97 us (14%)
  local copies, waits for them, and re-layouts  1.34 us (2%)
  between operations  1.33 us (2%)
    all_to_all x1, blocking collectives, shards(): rows = lax.all_to_all(copies, ('dom', 'sub'), 0, 0, tiled=True)  21.7 us
    ppermute x3, starting transfers between devices, down(): return lax.ppermute(x, axis, [((i + 1) % size, i) for i in range(size)])  9.55 us
    pallas_call x1, Pallas kernels, late_part(): pl.pallas_call(late_kernel, out_shape=(jax.ShapeDtypeStruct((1, blk, orde...  8.25 us
    ppermute x3, waiting for transfers between devices, down(): return lax.ppermute(x, axis, [((i + 1) % size, i) for i in range(size)])  4.85 us
    ppermute x3, waiting for transfers between devices, up(): return lax.ppermute(x, axis, [(i, (i + 1) % size) for i in range(size)])  3.12 us
    ppermute x3, starting transfers between devices, up(): return lax.ppermute(x, axis, [(i, (i + 1) % size) for i in range(size)])  2.89 us
    pallas_call x2, Pallas kernels, packed(): pl.pallas_call(functools.partial(pack_kernel, groups), out_shape=tuple((j...  1.79 us
    pallas_call x1, Pallas kernels, early_part(): pl.pallas_call(early_kernel, out_shape=(jax.ShapeDtypeStruct((len(EARLY_P...  1.64 us
  transfers between devices with their start and end apart: 6, of which 4 were waited for; matrix products, arithmetic and copies ran while one was open for 0% of the time, Pallas kernels for 3%

profile of v3, /device:TPU:1, one launch (start us, length us, event | category | flops | bytes accessed | tf_op | source)
XLA Modules:
  0.0 57.1 jit_solution(10235411523420206595)
XLA Ops:
  0.6 0.0 copy-start
  0.6 1.3 %copy-done = bf16[1,9,256,256]{3,2,1,0:T(8,128)(2,1)S(1)} copy-done((bf16[1,9,256,256]{3,2,1,0:T(8,128)(2,1)S(1)}, bf16[1,9,256,256]{3,2,1,0:T(8,128)(2,1)}, u32[]{:S(2)}) %copy-start) | copy-done | bytes 1179672
  1.9 0.9 %pack_halo.2 = (bf16[1,4,256,256]{3,2,1,0:T(8,128)(2,1)S(1)}, bf16[1,4,256,256]{3,2,1,0:T(8,128)(2,1)}) custom-call(bf16[1,9,256,256]{3,2,1,0:T(8,128)(2,1)S(1)} %copy-done, bf16[1,9,256,256]{3,2,1,0:T(8,128)(2,1)S(1)} %copy-done), custom_call_target="tpu_custom_call" | custom-call | flops 1 | bytes 1 | tf_op jit(solution)/shard_map/pack_halo/pallas_call | solution.py:268
  2.8 0.0 copy-start.1
  2.8 0.0 copy-start.2
  2.8 0.9 %pack_halo.3 = (bf16[1,2,256,256]{3,2,1,0:T(8,128)(2,1)S(1)}, bf16[1,2,256,256]{3,2,1,0:T(8,128)(2,1)}, bf16[1,2,256,256]{3,2,1,0:T(8,128)(2,1)}, bf16[1,2,256,256]{3,2,1,0:T(8,128)(2,1)}) custom-call(bf16[1,9,256,256]{3,2,1,0:T(8,128)(2,1)S(1)} %copy-done, bf16[1,4,256,256]{3,2,1,0:T(8,128)(2,1)S(1)} %get-tuple-element.13.earlier), custom_call_target="tpu_custom_call" | custom-call | flops 1 | bytes 1 | tf_op jit(solution)/shard_map/pack_halo/pallas_call | solution.py:268
  3.7 2.6 %collective-permute-start = (bf16[1,2,256,256]{3,2,1,0:T(8,128)(2,1)S(1)}, bf16[1,2,256,256]{3,2,1,0:T(8,128)(2,1)S(1)}, u32[]{:S(2)}, u32[]{:S(2)}) collective-permute-start(bf16[1,2,256,256]{3,2,1,0:T(8,128)(2,1)S(1)} %get-tuple-element.14), channel_id=1, source_target_pairs={{0,8},{8,16},{16,24},{24,32},{32,40},{40,48},{48,56},{56,64},{64,7... | collective-permute-start | bytes 786440 | tf_op jit(solution)/shard_map/ppermute | solution.py:303
  6.3 5.6 %collective-permute-start.5 = (bf16[1,4,256,256]{3,2,1,0:T(8,128)(2,1)}, bf16[1,4,256,256]{3,2,1,0:T(8,128)(2,1)S(1)}, u32[]{:S(2)}, u32[]{:S(2)}) collective-permute-start(bf16[1,4,256,256]{3,2,1,0:T(8,128)(2,1)} %get-tuple-element.21), channel_id=1, source_target_pairs={{1,0},{2,1},{3,2},{4,3},{5,4},{6,5},{7,6},{0,7},{9,8},{10,9},{11,1... | collective-permute-start | bytes 1572872 | tf_op jit(solution)/shard_map/ppermute | solution.py:306
  11.9 0.0 collective-permute-start.4
  11.9 0.3 collective-permute-start.1
  12.2 0.2 collective-permute-start.2
  12.4 0.0 collective-permute-done.r1a
  12.4 3.7 %collective-permute-start.3 = (bf16[1,2,256,256]{3,2,1,0:T(8,128)(2,1)}, bf16[1,2,256,256]{3,2,1,0:T(8,128)(2,1)}, u32[]{:S(2)}, u32[]{:S(2)}) collective-permute-start(bf16[1,2,256,256]{3,2,1,0:T(8,128)(2,1)} %get-tuple-element.17), channel_id=1, source_target_pairs={{8,0},{16,8},{24,16},{32,24},{40,32},{48,40},{56,48},{64,56},{72,6... | collective-permute-start | bytes 786440 | tf_op jit(solution)/shard_map/ppermute | solution.py:306
  16.8 0.0 collective-permute-done.1.r1b
  16.8 1.7 %collective-permute-done.2.r2a = bf16[1,2,256,256]{3,2,1,0:T(8,128)(2,1)S(1)} collective-permute-done((bf16[1,2,256,256]{3,2,1,0:T(8,128)(2,1)}, bf16[1,2,256,256]{3,2,1,0:T(8,128)(2,1)S(1)}, u32[]{:S(2)}, u32[]{:S(2)}) %collective-permute-start.2) | collective-permute-done | bytes 262176 | tf_op jit(solution)/shard_map/ppermute | solution.py:306
  18.5 2.8 %collective-permute-done.3.r2b = bf16[1,2,256,256]{3,2,1,0:T(8,128)(2,1)} collective-permute-done((bf16[1,2,256,256]{3,2,1,0:T(8,128)(2,1)}, bf16[1,2,256,256]{3,2,1,0:T(8,128)(2,1)}, u32[]{:S(2)}, u32[]{:S(2)}) %collective-permute-start.3) | collective-permute-done | bytes 262176 | tf_op jit(solution)/shard_map/ppermute | solution.py:306
  21.3 0.0 copy-done.1
  21.3 0.0 copy-done.2
  21.3 1.6 %early_blocks.1 = (f32[5,256,256]{2,1,0:T(8,128)S(1)}, bf16[4,256,256]{2,1,0:T(8,128)(2,1)S(1)}, f32[256,128]{1,0:T(8,128)S(1)}) custom-call(s32[1,5]{1,0:T(1,128)S(1)} %copy-done.2, f32[1,1]{1,0:T(1,128)} %bitcast.4.potential, bf16[1,9,256,256]{3,2,1,0:T(8,128)(2,1)S(1)} %copy-done.1, bf16[1,2,256,256]{3,2,1,0:T(8,128)(2,1)S(1)} %collective-permute-done.r1a, ...), custom_call_target="tpu_custom_call" | custom-call | flops 1 | bytes 1 | tf_op jit(solution)/shard_map/early_blocks/pallas_call | solution.py:221
  22.9 0.4 collective-permute-done.5.r4
  23.3 3.1 %collective-permute-done.4.r3 = bf16[1,4,256,256]{3,2,1,0:T(8,128)(2,1)S(1)} collective-permute-done((bf16[1,4,256,256]{3,2,1,0:T(8,128)(2,1)S(1)}, bf16[1,4,256,256]{3,2,1,0:T(8,128)(2,1)S(1)}, u32[]{:S(2)}, u32[]{:S(2)}) %collective-permute-start.4) | collective-permute-done | bytes 524320 | tf_op jit(solution)/shard_map/ppermute | solution.py:303
  26.4 8.2 %density_rows.1 = (f32[1,256,1280]{2,1,0:T(8,128)}, f32[1,128]{1,0:T(1,128)S(1)}) custom-call(s32[1,5]{1,0:T(1,128)S(1)} %copy-done.2, f32[1,1]{1,0:T(1,128)} %bitcast.5.potential, bf16[1,9,256,256]{3,2,1,0:T(8,128)(2,1)S(1)} %copy-done.1, f32[5,256,256]{2,1,0:T(8,128)S(1)} %get-tuple-element.18.early, bf16[4,256,256]{2,1,0:T(8,128)(2,1)S(1)} %get-tuple-element.19.turned, ...), custom_call_target="tpu_custom_call" | custom-call | tf_op jit(solution)/shard_map/density_rows/pallas_call | solution.py:239
  34.7 0.1 broadcast_in_dim.2
  34.8 21.7 %all_to_all.8 = f32[256,1,128]{2,1,0:T(1,128)S(1)} all-to-all(f32[256,1,128]{2,1,0:T(1,128)S(1)} %broadcast_in_dim.2), channel_id=1, replica_groups=mesh['dom'=32,'sub'=8] {'dom','sub'}, dimensions={0} | all-to-all | bytes 262144 | tf_op jit(solution)/shard_map/all_to_all | solution.py:320
  56.4 0.6 %pair_charges.1 = f32[128,128]{1,0:T(8,128)} custom-call(f32[256,128]{1,0:T(8,128)S(1)} %bitcast.6), custom_call_target="tpu_custom_call" | custom-call | tf_op jit(solution)/shard_map/pair_charges/pallas_call | solution.py:287
Async XLA Ops:
  0.6 1.3 %copy-start = (bf16[1,9,256,256]{3,2,1,0:T(8,128)(2,1)S(1)}, bf16[1,9,256,256]{3,2,1,0:T(8,128)(2,1)}, u32[]{:S(2)}) copy-start(bf16[1,9,256,256]{3,2,1,0:T(8,128)(2,1)} %own.7) | copy-start | bytes 3538948
  2.8 18.5 %copy-start.1 = (bf16[1,9,256,256]{3,2,1,0:T(8,128)(2,1)S(1)}, bf16[1,9,256,256]{3,2,1,0:T(8,128)(2,1)}, u32[]{:S(2)}) copy-start(bf16[1,9,256,256]{3,2,1,0:T(8,128)(2,1)} %own.7) | copy-start | bytes 3538948
  2.8 18.5 %copy-start.2 = (s32[1,5]{1,0:T(1,128)S(1)}, s32[1,5]{1,0:T(1,128)}, u32[]{:S(2)}) copy-start(s32[1,5]{1,0:T(1,128)} %slots.3) | copy-start | bytes 64
  3.7 8.7 %collective-permute-start = (bf16[1,2,256,256]{3,2,1,0:T(8,128)(2,1)S(1)}, bf16[1,2,256,256]{3,2,1,0:T(8,128)(2,1)S(1)}, u32[]{:S(2)}, u32[]{:S(2)}) collective-permute-start(bf16[1,2,256,256]{3,2,1,0:T(8,128)(2,1)S(1)} %get-tuple-element.14), channel_id=1, source_target_pairs={{0,8},{8,16},{16,24},{24,32},{32,40},{40,48},{48,56},{56,64},{64,7... | collective-permute-start | bytes 786440 | tf_op jit(solution)/shard_map/ppermute | solution.py:303
  6.3 17.0 %collective-permute-start.5 = (bf16[1,4,256,256]{3,2,1,0:T(8,128)(2,1)}, bf16[1,4,256,256]{3,2,1,0:T(8,128)(2,1)S(1)}, u32[]{:S(2)}, u32[]{:S(2)}) collective-permute-start(bf16[1,4,256,256]{3,2,1,0:T(8,128)(2,1)} %get-tuple-element.21), channel_id=1, source_target_pairs={{1,0},{2,1},{3,2},{4,3},{5,4},{6,5},{7,6},{0,7},{9,8},{10,9},{11,1... | collective-permute-start | bytes 1572872 | tf_op jit(solution)/shard_map/ppermute | solution.py:306
  11.9 14.5 %collective-permute-start.4 = (bf16[1,4,256,256]{3,2,1,0:T(8,128)(2,1)S(1)}, bf16[1,4,256,256]{3,2,1,0:T(8,128)(2,1)S(1)}, u32[]{:S(2)}, u32[]{:S(2)}) collective-permute-start(bf16[1,4,256,256]{3,2,1,0:T(8,128)(2,1)S(1)} %get-tuple-element.13.earlier), channel_id=1, source_target_pairs={{0,1},{1,2},{2,3},{3,4},{4,5},{5,6},{6,7},{7,0},{8,9},{9,10},{10,1... | collective-permute-start | bytes 1572872 | tf_op jit(solution)/shard_map/ppermute | solution.py:303
  11.9 4.9 %collective-permute-start.1 = (bf16[1,2,256,256]{3,2,1,0:T(8,128)(2,1)}, bf16[1,2,256,256]{3,2,1,0:T(8,128)(2,1)S(1)}, u32[]{:S(2)}, u32[]{:S(2)}) collective-permute-start(bf16[1,2,256,256]{3,2,1,0:T(8,128)(2,1)} %get-tuple-element.15), channel_id=1, source_target_pairs={{0,8},{8,16},{16,24},{24,32},{32,40},{40,48},{48,56},{56,64},{64,7... | collective-permute-start | bytes 786440 | tf_op jit(solution)/shard_map/ppermute | solution.py:303
  12.2 6.3 %collective-permute-start.2 = (bf16[1,2,256,256]{3,2,1,0:T(8,128)(2,1)}, bf16[1,2,256,256]{3,2,1,0:T(8,128)(2,1)S(1)}, u32[]{:S(2)}, u32[]{:S(2)}) collective-permute-start(bf16[1,2,256,256]{3,2,1,0:T(8,128)(2,1)} %get-tuple-element.16), channel_id=1, source_target_pairs={{8,0},{16,8},{24,16},{32,24},{40,32},{48,40},{56,48},{64,56},{72,6... | collective-permute-start | bytes 786440 | tf_op jit(solution)/shard_map/ppermute | solution.py:306
  12.4 8.9 %collective-permute-start.3 = (bf16[1,2,256,256]{3,2,1,0:T(8,128)(2,1)}, bf16[1,2,256,256]{3,2,1,0:T(8,128)(2,1)}, u32[]{:S(2)}, u32[]{:S(2)}) collective-permute-start(bf16[1,2,256,256]{3,2,1,0:T(8,128)(2,1)} %get-tuple-element.17), channel_id=1, source_target_pairs={{8,0},{16,8},{24,16},{32,24},{40,32},{48,40},{56,48},{64,56},{72,6... | collective-permute-start | bytes 786440 | tf_op jit(solution)/shard_map/ppermute | solution.py:306

commit v4 on v3

--- a/solution.py
+++ b/solution.py
@@ -110,8 +110,8 @@
 
 
 def late_kernel(
-    slots, potential, own, early, turned, sums, r3, r4, density, charges,
-    x0, x0b, q0b, x1b, out, sems,
+    slots, potential, own, early, turned, sums, r4, r3,
+    charges, core, first, y, x1b, x0, x0b, q0b,
 ):
     blk = own.shape[-1]
     f32, bf16 = jnp.float32, jnp.bfloat16
@@ -144,9 +144,9 @@
     def place(i, j):
         return ORDER.index(i), ORDER.index(j)
 
-    for i, j in LATE_PAIRS:
-        p, q = place(i, j)
-        x0[at(p), at(q)] = halo.block(i, j, turned[TURNED.index((i, j))] if (i, j) in TURNED else None)
+    for n, (i, j) in enumerate(PAIRS):
+        if (i, j) in LATE_PAIRS:
+            x0[n] = halo.block(i, j, turned[TURNED.index((i, j))] if (i, j) in TURNED else None)
     largest = None
     for i in range(SLOTS):
         total = halo.sums(i)
@@ -156,50 +156,51 @@
         largest = top if largest is None else jnp.maximum(largest, top)
     inv = 1.0 / (2.0 * jnp.sqrt(largest + 1e-06))
 
-    for i, j in PAIRS:
-        p, q = place(i, j)
-        if (i, j) in EARLY_PAIRS:
-            block = early[EARLY_PAIRS.index((i, j))] * inv
-        else:
-            block = x0[at(p), at(q)] * inv
-        x0[at(p), at(q)] = block
-        mirror(x0b, p, q, block)
+    for n, (i, j) in enumerate(PAIRS):
+        block = early[EARLY_PAIRS.index((i, j))] if (i, j) in EARLY_PAIRS else x0[n]
+        x0[n] = block * inv
+        mirror(x0b, *place(i, j), x0[n])
     upper = [(p, q) for p in range(SLOTS) for q in range(p, SLOTS)]
     for p, q in upper:
         mirror(q0b, p, q, product(x0b, x0b, p, q))
     for p, q in upper:
         block = -0.5 * product(x0b, q0b, p, q)
         if coupled(p, q):
-            block = 1.5 * x0[at(p), at(q)] + block
+            block = 1.5 * x0[PAIRS.index((ORDER[p], ORDER[q]))] + block
         if p == 0:
-            x0[at(0), at(q)] = block
+            first[:, at(q)] = block
         mirror(x1b, p, q, block)
-    left = jnp.concatenate(
-        [product(x1b, x1b, 0, q).astype(bf16) for q in range(SLOTS)], axis=1
+    for q in range(SLOTS):
+        y[:, at(q)] = product(x1b, x1b, 0, q).astype(bf16)
+    sign = 1.5 * first[:, at(0)] - 0.5 * jnp.dot(y[...], x1b[:, at(0)], preferred_element_type=f32)
+    result = 0.5 * jnp.where(eye, 1.0 + sign, sign)
+    core[...] = result
+    occupied = jnp.sum(jnp.where(eye, result, 0.0), axis=1, keepdims=True)
+    lanes = charges.shape[1]
+    atoms = blk // ORBS
+    atom = lax.broadcasted_iota(jnp.int32, (blk, lanes), 0) // ORBS + slots[0, 0] % 2 * atoms
+    lane = lax.broadcasted_iota(jnp.int32, (blk, lanes), 1)
+    charges[...] = jnp.sum(
+        jnp.where(atom == lane, 4.0 / ORBS - 2.0 * occupied, 0.0), axis=0, keepdims=True
     )
-    copies = []
-    for q in range(SLOTS):
-        sign = 1.5 * x0[at(0), at(q)] - 0.5 * jnp.dot(
-            left, x1b[:, at(q)], preferred_element_type=f32
-        )
-        if q == 0:
-            sign = jnp.where(eye, 1.0 + sign, sign)
-        result = 0.5 * sign
-        out[q] = result
+
+
+def rest_kernel(core, first, y, x1b, density, out, sems):
+    blk = core.shape[0]
+
+    def write(q, block):
+        out[q] = block
         copy = pltpu.make_async_copy(
             out.at[q], density.at[0, :, pl.ds(ORDER[q] * blk, blk)], sems.at[q]
         )
         copy.start()
-        copies.append(copy)
-        if q == 0:
-            occupied = jnp.sum(jnp.where(eye, result, 0.0), axis=1, keepdims=True)
-            lanes = charges.shape[1]
-            atoms = blk // ORBS
-            atom = lax.broadcasted_iota(jnp.int32, (blk, lanes), 0) // ORBS + slots[0, 0] % 2 * atoms
-            lane = lax.broadcasted_iota(jnp.int32, (blk, lanes), 1)
-            charges[...] = jnp.sum(
-                jnp.where(atom == lane, 4.0 / ORBS - 2.0 * occupied, 0.0), axis=0, keepdims=True
-            )
+        return copy
+
+    copies = [write(0, core[...])]
+    for q in range(1, SLOTS):
+        at = slice(q * blk, (q + 1) * blk)
+        product = jnp.dot(y[...], x1b[:, at], preferred_element_type=jnp.float32)
+        copies.append(write(q, 0.75 * first[:, at] - 0.25 * product))
     for copy in copies:
         copy.wait()
 
@@ -212,8 +213,7 @@
 SMALL = pl.CostEstimate(flops=1, bytes_accessed=1, transcendentals=0)
 
 
-def limit(mib):
-    return pltpu.CompilerParams(vmem_limit_bytes=mib * MIB)
+LIMIT = pltpu.CompilerParams(vmem_limit_bytes=20 * MIB)
 
 
 def early_part(slots, potential, own, *halves):
@@ -227,34 +227,53 @@
         ),
         in_specs=[SMEM, SMEM] + [VMEM] * 5,
         out_specs=(VMEM, VMEM, VMEM),
-        compiler_params=limit(12),
+        compiler_params=LIMIT,
         cost_estimate=SMALL,
         name="early_blocks",
     )(slots, potential, own, *halves)
 
 
-def late_part(slots, potential, own, early, turned, sums, r3, r4):
+def late_part(slots, potential, own, early, turned, sums, r4, r3):
     blk = own.shape[-1]
     order = SLOTS * blk
     return pl.pallas_call(
         late_kernel,
         out_shape=(
-            jax.ShapeDtypeStruct((1, blk, order), jnp.float32),
             jax.ShapeDtypeStruct((1, LANES), jnp.float32),
+            jax.ShapeDtypeStruct((blk, blk), jnp.float32),
+            jax.ShapeDtypeStruct((blk, order), jnp.float32),
+            jax.ShapeDtypeStruct((blk, order), jnp.bfloat16),
+            jax.ShapeDtypeStruct((order, order), jnp.bfloat16),
         ),
         in_specs=[SMEM, SMEM] + [VMEM] * 6,
-        out_specs=(ANY, VMEM),
+        out_specs=(VMEM,) * 5,
         scratch_shapes=[
-            pltpu.VMEM((order, order), jnp.float32),
+            pltpu.VMEM((len(PAIRS), blk, blk), jnp.float32),
             pltpu.VMEM((order, order), jnp.bfloat16),
             pltpu.VMEM((order, order), jnp.bfloat16),
-            pltpu.VMEM((order, order), jnp.bfloat16),
+        ],
+        compiler_params=LIMIT,
+        name="core_charges",
+    )(slots, potential, own, early, turned, sums, r4, r3)
+
+
+def rest_part(core, first, y, x1b):
+    blk, order = first.shape
+    return pl.pallas_call(
+        rest_kernel,
+        out_shape=jax.ShapeDtypeStruct((1, blk, order), jnp.float32),
+        in_specs=[VMEM] * 4,
+        out_specs=ANY,
+        scratch_shapes=[
             pltpu.VMEM((SLOTS, blk, blk), jnp.float32),
             pltpu.SemaphoreType.DMA((SLOTS,)),
         ],
-        compiler_params=limit(32),
+        compiler_params=LIMIT,
+        cost_estimate=pl.CostEstimate(
+            flops=2 * blk * order * order, bytes_accessed=4 * blk * order, transcendentals=0
+        ),
         name="density_rows",
-    )(slots, potential, own, early, turned, sums, r3, r4)
+    )(core, first, y, x1b)
 
 
 def pack_kernel(groups, own, earlier, *packs):
@@ -272,31 +291,37 @@
         ),
         in_specs=[VMEM, ANY],
         out_specs=(VMEM,) * len(groups),
-        compiler_params=limit(4),
+        compiler_params=LIMIT,
         cost_estimate=SMALL,
         name="pack_halo",
     )(own, earlier)
 
 
-def pair_kernel(rows, out):
-    half = out.shape[0]
-    out[...] = rows[pl.ds(0, half, stride=2), :] + rows[pl.ds(1, half, stride=2), :]
-
-
-def paired(rows):
-    return pl.pallas_call(
-        pair_kernel,
-        out_shape=jax.ShapeDtypeStruct((rows.shape[0] // 2, rows.shape[1]), rows.dtype),
-        in_specs=[VMEM],
+def order_kernel(slots, *refs):
+    blocks, out = refs[:-1], refs[-1]
+    me = slots[0, 0] // 2
+    height = blocks[0].shape[0]
+    for dy, block in enumerate(blocks):
+        for row in range(height):
+            dx, dz, dcore = row // 8, row // 2 % 4, row % 2
+            target = me ^ (((dy * 4 + dx) * 2 + dcore) * 4 + dz)
+            out[pl.ds(target, 1), :] = block[row : row + 1, :]
+
+
+def in_order(slots, blocks):
+    height, lanes = blocks[0].shape
+    return pl.pallas_call(
+        order_kernel,
+        out_shape=jax.ShapeDtypeStruct((len(blocks) * height, lanes), blocks[0].dtype),
+        in_specs=[SMEM] + [VMEM] * len(blocks),
         out_specs=VMEM,
-        compiler_params=limit(2),
-        name="pair_charges",
-    )(rows)
+        compiler_params=LIMIT,
+        name="order_charges",
+    )(slots, *blocks)
 
 
 def shards(hamiltonian, partitions, chemical_potential):
-    n_dom = lax.axis_size("dom")
-    n_sub = lax.axis_size("sub")
+    n_dom, n_sub = lax.axis_size("dom"), lax.axis_size("sub")
     potential = chemical_potential.reshape(1, 1)
 
     def up(x, axis, size):
@@ -305,20 +330,30 @@
     def down(x, axis, size):
         return lax.ppermute(x, axis, [((i + 1) % size, i) for i in range(size)])
 
-    sub_up, sub_down = packed(hamiltonian, hamiltonian, SENT[3], SENT[4])
+    def swapped(x, mask):
+        return lax.ppermute(x, ("dom", "sub"), [(p, p ^ mask) for p in range(n_dom * n_sub)])
+
+    def others(x, first, second):
+        return [swapped(x, mask) for mask in (first, second, first + second)]
+
+    sub_down, sub_up = packed(hamiltonian, hamiltonian, SENT[4], SENT[3])
     dom_parts = packed(
-        hamiltonian, sub_up, SENT[1][:2], SENT[1][2:], SENT[2][:2], SENT[2][2:]
+        hamiltonian, sub_down, SENT[1][:2], SENT[1][2:], SENT[2][:2], SENT[2][2:]
     )
-    r3, r4 = up(sub_up, "sub", n_sub), down(sub_down, "sub", n_sub)
+    r4 = down(sub_down, "sub", n_sub)
+    r3 = up(sub_up, "sub", n_sub)
     halves = [up(x, "dom", n_dom) for x in dom_parts[:2]]
     halves += [down(x, "dom", n_dom) for x in dom_parts[2:]]
     early, turned, sums = early_part(partitions, potential, hamiltonian, *halves)
-    density, row = late_part(
-        partitions, potential, hamiltonian, early, turned, sums, r3, r4
+    row, *held = late_part(
+        partitions, potential, hamiltonian, early, turned, sums, r4, r3
     )
-    copies = jnp.broadcast_to(row, (n_dom * n_sub, LANES))
-    rows = lax.all_to_all(copies, ("dom", "sub"), 0, 0, tiled=True)
-    charges = paired(rows).reshape(-1)
+    density = rest_part(*held)
+    near, core, both = others(row, 1, 8)
+    block = jnp.concatenate([row + near, core + both], axis=0)
+    block = jnp.concatenate([block] + others(block, 2, 4), axis=0)
+    block = jnp.concatenate([block] + others(block, 16, 32), axis=0)
+    charges = in_order(partitions, [block] + others(block, 64, 128)).reshape(-1)
     return (density, charges)
 
 

time: 57.2 us -> 68 us (1.19)
  the two profiles are of different devices: /device:TPU:1 before, /device:TPU:16 now
where the time goes in v4:
time: 68 us; the launch traced here: 67.7 us
  starting transfers between devices  28.3 us (42%)
  waiting for transfers between devices  16 us (24%)
  Pallas kernels  13.4 us (20%)
  local copies, waits for them, and re-layouts  8.6 us (13%)
  between operations  1.4 us (2%)
    ppermute x12, starting transfers between devices, swapped(): lax.ppermute(x, ('dom', 'sub'), [(p, p ^ mask) for p in range(n_dom * n_s...  18.4 us
    ppermute x12, waiting for transfers between devices, swapped(): lax.ppermute(x, ('dom', 'sub'), [(p, p ^ mask) for p in range(n_dom * n_s...  9.85 us
    unnamed x18, local copies, waits for them, and re-layouts  8.56 us
    pallas_call x1, Pallas kernels, late_part(): pl.pallas_call(late_kernel, out_shape=(jax.ShapeDtypeStruct((1, LANES), j...  6.92 us
    ppermute x3, starting transfers between devices, down(): return lax.ppermute(x, axis, [((i + 1) % size, i) for i in range(size)])  6.73 us
    ppermute x3, waiting for transfers between devices, up(): return lax.ppermute(x, axis, [(i, (i + 1) % size) for i in range(size)])  3.41 us
    ppermute x3, starting transfers between devices, up(): return lax.ppermute(x, axis, [(i, (i + 1) % size) for i in range(size)])  3.21 us
    ppermute x3, waiting for transfers between devices, down(): return lax.ppermute(x, axis, [((i + 1) % size, i) for i in range(size)])  2.76 us
  transfers between devices with their start and end apart: 18, of which 7 were waited for; matrix products, arithmetic and copies ran while one was open for 0% of the time, Pallas kernels for 5%

profile of v4, /device:TPU:16, one launch (start us, length us, event | category | flops | bytes accessed | tf_op | source)
XLA Modules:
  0.0 67.7 jit_solution(11542522853414236021)
XLA Ops:
  0.6 0.0 copy-start
  0.6 1.3 %copy-done = bf16[1,9,256,256]{3,2,1,0:T(8,128)(2,1)S(1)} copy-done((bf16[1,9,256,256]{3,2,1,0:T(8,128)(2,1)S(1)}, bf16[1,9,256,256]{3,2,1,0:T(8,128)(2,1)}, u32[]{:S(2)}) %copy-start) | copy-done | bytes 1179672
  1.9 0.9 %pack_halo.2 = (bf16[1,4,256,256]{3,2,1,0:T(8,128)(2,1)S(1)}, bf16[1,4,256,256]{3,2,1,0:T(8,128)(2,1)}) custom-call(bf16[1,9,256,256]{3,2,1,0:T(8,128)(2,1)S(1)} %copy-done, bf16[1,9,256,256]{3,2,1,0:T(8,128)(2,1)S(1)} %copy-done), custom_call_target="tpu_custom_call" | custom-call | flops 1 | bytes 1 | tf_op jit(solution)/shard_map/pack_halo/pallas_call | solution.py:287
  2.8 0.0 copy-start.1
  2.8 0.0 copy-start.8
  2.8 1.0 %pack_halo.3 = (bf16[1,2,256,256]{3,2,1,0:T(8,128)(2,1)S(1)}, bf16[1,2,256,256]{3,2,1,0:T(8,128)(2,1)}, bf16[1,2,256,256]{3,2,1,0:T(8,128)(2,1)}, bf16[1,2,256,256]{3,2,1,0:T(8,128)(2,1)}) custom-call(bf16[1,9,256,256]{3,2,1,0:T(8,128)(2,1)S(1)} %copy-done, bf16[1,4,256,256]{3,2,1,0:T(8,128)(2,1)S(1)} %get-tuple-element.16.earlier), custom_call_target="tpu_custom_call" | custom-call | flops 1 | bytes 1 | tf_op jit(solution)/shard_map/pack_halo/pallas_call | solution.py:287
  3.7 0.0 collective-permute-start
  3.7 1.9 %collective-permute-start.5 = (bf16[1,4,256,256]{3,2,1,0:T(8,128)(2,1)}, bf16[1,4,256,256]{3,2,1,0:T(8,128)(2,1)S(1)}, u32[]{:S(2)}, u32[]{:S(2)}) collective-permute-start(bf16[1,4,256,256]{3,2,1,0:T(8,128)(2,1)} %get-tuple-element.24), channel_id=1, source_target_pairs={{0,1},{1,2},{2,3},{3,4},{4,5},{5,6},{6,7},{7,0},{8,9},{9,10},{10,1... | collective-permute-start | bytes 1572872 | tf_op jit(solution)/shard_map/ppermute | solution.py:328
  5.7 4.0 %collective-permute-start.4 = (bf16[1,4,256,256]{3,2,1,0:T(8,128)(2,1)S(1)}, bf16[1,4,256,256]{3,2,1,0:T(8,128)(2,1)S(1)}, u32[]{:S(2)}, u32[]{:S(2)}) collective-permute-start(bf16[1,4,256,256]{3,2,1,0:T(8,128)(2,1)S(1)} %get-tuple-element.16.earlier), channel_id=1, source_target_pairs={{1,0},{2,1},{3,2},{4,3},{5,4},{6,5},{7,6},{0,7},{9,8},{10,9},{11,1... | collective-permute-start | bytes 1572872 | tf_op jit(solution)/shard_map/ppermute | solution.py:331
  9.6 1.3 %collective-permute-start.1 = (bf16[1,2,256,256]{3,2,1,0:T(8,128)(2,1)}, bf16[1,2,256,256]{3,2,1,0:T(8,128)(2,1)S(1)}, u32[]{:S(2)}, u32[]{:S(2)}) collective-permute-start(bf16[1,2,256,256]{3,2,1,0:T(8,128)(2,1)} %get-tuple-element.18), channel_id=1, source_target_pairs={{0,8},{8,16},{16,24},{24,32},{32,40},{40,48},{48,56},{56,64},{64,7... | collective-permute-start | bytes 786440 | tf_op jit(solution)/shard_map/ppermute | solution.py:328
  10.9 2.6 %collective-permute-start.2 = (bf16[1,2,256,256]{3,2,1,0:T(8,128)(2,1)}, bf16[1,2,256,256]{3,2,1,0:T(8,128)(2,1)S(1)}, u32[]{:S(2)}, u32[]{:S(2)}) collective-permute-start(bf16[1,2,256,256]{3,2,1,0:T(8,128)(2,1)} %get-tuple-element.19), channel_id=1, source_target_pairs={{8,0},{16,8},{24,16},{32,24},{40,32},{48,40},{56,48},{64,56},{72,6... | collective-permute-start | bytes 786440 | tf_op jit(solution)/shard_map/ppermute | solution.py:331
  13.5 0.0 collective-permute-done.r1a
  13.5 0.2 collective-permute-start.3
  14.3 3.4 %collective-permute-done.1.r1b = bf16[1,2,256,256]{3,2,1,0:T(8,128)(2,1)S(1)} collective-permute-done((bf16[1,2,256,256]{3,2,1,0:T(8,128)(2,1)}, bf16[1,2,256,256]{3,2,1,0:T(8,128)(2,1)S(1)}, u32[]{:S(2)}, u32[]{:S(2)}) %collective-permute-start.1) | collective-permute-done | bytes 262176 | tf_op jit(solution)/shard_map/ppermute | solution.py:328
  17.7 0.0 collective-permute-done.2.r2a
  17.7 2.8 %collective-permute-done.3.r2b = bf16[1,2,256,256]{3,2,1,0:T(8,128)(2,1)} collective-permute-done((bf16[1,2,256,256]{3,2,1,0:T(8,128)(2,1)}, bf16[1,2,256,256]{3,2,1,0:T(8,128)(2,1)}, u32[]{:S(2)}, u32[]{:S(2)}) %collective-permute-start.3) | collective-permute-done | bytes 262176 | tf_op jit(solution)/shard_map/ppermute | solution.py:331
  20.5 0.0 copy-done.1
  20.5 0.0 copy-done.8
  20.5 1.6 %early_blocks.1 = (f32[5,256,256]{2,1,0:T(8,128)S(1)}, bf16[4,256,256]{2,1,0:T(8,128)(2,1)S(1)}, f32[256,128]{1,0:T(8,128)S(1)}) custom-call(s32[1,5]{1,0:T(1,128)S(1)} %copy-done.8, f32[1,1]{1,0:T(1,128)} %bitcast.2.potential, bf16[1,9,256,256]{3,2,1,0:T(8,128)(2,1)S(1)} %copy-done.1, bf16[1,2,256,256]{3,2,1,0:T(8,128)(2,1)S(1)} %collective-permute-done.r1a, ...), custom_call_target="tpu_custom_call" | custom-call | flops 1 | bytes 1 | tf_op jit(solution)/shard_map/early_blocks/pallas_call | solution.py:221
  22.1 0.0 collective-permute-done.5.r3
  22.2 0.0 copy-start.4
  22.2 0.8 %copy-done.4 = bf16[1,4,256,256]{3,2,1,0:T(8,128)(2,1)} copy-done((bf16[1,4,256,256]{3,2,1,0:T(8,128)(2,1)}, bf16[1,4,256,256]{3,2,1,0:T(8,128)(2,1)S(1)}, u32[]{:S(2)}) %copy-start.4) | copy-done | bytes 524312
  23.0 0.0 collective-permute-done.4.r4
  23.0 0.0 copy-start.6
  23.0 0.8 %copy-done.6 = bf16[1,4,256,256]{3,2,1,0:T(8,128)(2,1)} copy-done((bf16[1,4,256,256]{3,2,1,0:T(8,128)(2,1)}, bf16[1,4,256,256]{3,2,1,0:T(8,128)(2,1)S(1)}, u32[]{:S(2)}) %copy-start.6) | copy-done | bytes 524312
  23.8 0.0 copy-start.5
  23.8 1.0 %copy-done.5 = bf16[1,4,256,256]{3,2,1,0:T(8,128)(2,1)S(1)} copy-done((bf16[1,4,256,256]{3,2,1,0:T(8,128)(2,1)S(1)}, bf16[1,4,256,256]{3,2,1,0:T(8,128)(2,1)}, u32[]{:S(2)}) %copy-start.5) | copy-done | bytes 524312
  24.8 0.0 copy-start.7
  24.8 1.0 %copy-done.7 = bf16[1,4,256,256]{3,2,1,0:T(8,128)(2,1)S(1)} copy-done((bf16[1,4,256,256]{3,2,1,0:T(8,128)(2,1)S(1)}, bf16[1,4,256,256]{3,2,1,0:T(8,128)(2,1)}, u32[]{:S(2)}) %copy-start.7) | copy-done | bytes 524312
  25.9 6.9 %core_charges.1 = (f32[1,128]{1,0:T(1,128)S(1)}, f32[256,256]{1,0:T(8,128)S(1)}, f32[256,1280]{1,0:T(8,128)S(1)}, bf16[256,1280]{1,0:T(8,128)(2,1)S(1)}, bf16[1280,1280]{1,0:T(8,128)(2,1)S(1)}) custom-call(s32[1,5]{1,0:T(1,128)S(1)} %copy-done.8, f32[1,1]{1,0:T(1,128)} %bitcast.3.potential, bf16[1,9,256,256]{3,2,1,0:T(8,128)(2,1)S(1)} %copy-done.1, ...), custom_call_target="tpu_custom_call" | custom-call | tf_op jit(solution)/shard_map/core_charges/pallas_call | solution.py:239
  32.8 0.0 copy-start.2
  32.8 1.7 %copy-done.2 = bf16[1280,1280]{1,0:T(8,128)(2,1)} copy-done((bf16[1280,1280]{1,0:T(8,128)(2,1)}, bf16[1280,1280]{1,0:T(8,128)(2,1)S(1)}, u32[]{:S(2)}) %copy-start.2) | copy-done | bytes 3276824
  34.5 0.0 collective-permute-start.6
  34.5 1.6 %collective-permute-start.8 = (f32[1,128]{1,0:T(1,128)S(1)}, f32[1,128]{1,0:T(1,128)S(1)}, u32[]{:S(2)}, u32[]{:S(2)}) collective-permute-start(f32[1,128]{1,0:T(1,128)S(1)} %get-tuple-element.29), channel_id=1, source_target_pairs={{0,9},{1,8},{2,11},{3,10},{4,13},{5,12},{6,15},{7,14},{8,1},{9,0},... | collective-permute-start | bytes 1544 | tf_op jit(solution)/shard_map/ppermute | solution.py:334
  36.1 0.5 collective-permute-start.7
  36.6 1.4 %collective-permute-done.6 = f32[1,128]{1,0:T(1,128)S(1)} collective-permute-done((f32[1,128]{1,0:T(1,128)S(1)}, f32[1,128]{1,0:T(1,128)S(1)}, u32[]{:S(2)}, u32[]{:S(2)}) %collective-permute-start.6) | collective-permute-done | bytes 544 | tf_op jit(solution)/shard_map/ppermute | solution.py:334
  38.0 0.0 collective-permute-done.8
  38.0 0.0 collective-permute-done.7
  38.0 3.1 %collective-permute-start.11 = (f32[2,128]{1,0:T(2,128)S(1)}, f32[2,128]{1,0:T(2,128)S(1)}, u32[]{:S(2)}, u32[]{:S(2)}) collective-permute-start(f32[2,128]{1,0:T(2,128)S(1)} %pad_maximum_fusion), channel_id=1, source_target_pairs={{0,6},{1,7},{2,4},{3,5},{4,2},{5,3},{6,0},{7,1},{8,14},{9,15},{10,... | collective-permute-start | bytes 3080 | tf_op jit(solution)/shard_map/ppermute | solution.py:334
  41.1 4.8 %collective-permute-start.10 = (f32[2,128]{1,0:T(2,128)S(1)}, f32[2,128]{1,0:T(2,128)S(1)}, u32[]{:S(2)}, u32[]{:S(2)}) collective-permute-start(f32[2,128]{1,0:T(2,128)S(1)} %pad_maximum_fusion), channel_id=1, source_target_pairs={{0,4},{1,5},{2,6},{3,7},{4,0},{5,1},{6,2},{7,3},{8,12},{9,13},{10,... | collective-permute-start | bytes 3080 | tf_op jit(solution)/shard_map/ppermute | solution.py:334
  45.9 0.0 collective-permute-start.9
  45.9 0.0 collective-permute-done.11
  45.9 2.6 %collective-permute-done.10 = f32[2,128]{1,0:T(2,128)S(1)} collective-permute-done((f32[2,128]{1,0:T(2,128)S(1)}, f32[2,128]{1,0:T(2,128)S(1)}, u32[]{:S(2)}, u32[]{:S(2)}) %collective-permute-start.10) | collective-permute-done | bytes 1056 | tf_op jit(solution)/shard_map/ppermute | solution.py:334
  48.6 1.8 %collective-permute-done.9 = f32[2,128]{1,0:T(2,128)S(1)} collective-permute-done((f32[2,128]{1,0:T(2,128)S(1)}, f32[2,128]{1,0:T(2,128)S(1)}, u32[]{:S(2)}, u32[]{:S(2)}) %collective-permute-start.9) | collective-permute-done | bytes 1056 | tf_op jit(solution)/shard_map/ppermute | solution.py:334
  50.4 3.0 %collective-permute-start.14 = (f32[8,128]{1,0:T(8,128)S(1)}, f32[8,128]{1,0:T(8,128)S(1)}, u32[]{:S(2)}, u32[]{:S(2)}) collective-permute-start(f32[8,128]{1,0:T(8,128)S(1)} %concatenate.12), channel_id=1, source_target_pairs={{0,48},{1,49},{2,50},{3,51},{4,52},{5,53},{6,54},{7,55},{8,56},{9,... | collective-permute-start | bytes 12296 | tf_op jit(solution)/shard_map/ppermute | solution.py:334
  53.4 0.6 collective-permute-start.13
  54.0 0.5 collective-permute-start.12
  54.6 0.7 %collective-permute-done.14 = f32[8,128]{1,0:T(8,128)S(1)} collective-permute-done((f32[8,128]{1,0:T(8,128)S(1)}, f32[8,128]{1,0:T(8,128)S(1)}, u32[]{:S(2)}, u32[]{:S(2)}) %collective-permute-start.14) | collective-permute-done | bytes 4128 | tf_op jit(solution)/shard_map/ppermute | solution.py:334
  55.3 3.3 %collective-permute-done.13 = f32[8,128]{1,0:T(8,128)S(1)} collective-permute-done((f32[8,128]{1,0:T(8,128)S(1)}, f32[8,128]{1,0:T(8,128)S(1)}, u32[]{:S(2)}, u32[]{:S(2)}) %collective-permute-start.13) | collective-permute-done | bytes 4128 | tf_op jit(solution)/shard_map/ppermute | solution.py:334
  58.6 0.0 collective-permute-done.12
  58.6 0.3 collective-permute-start.17
  58.9 2.2 %collective-permute-start.16 = (f32[32,128]{1,0:T(8,128)S(1)}, f32[32,128]{1,0:T(8,128)S(1)}, u32[]{:S(2)}, u32[]{:S(2)}) collective-permute-start(f32[32,128]{1,0:T(8,128)S(1)} %concatenate.13.refs_0_), channel_id=1, source_target_pairs={{0,128},{1,129},{2,130},{3,131},{4,132},{5,133},{6,134},{7,135},{8... | collective-permute-start | bytes 49160 | tf_op jit(solution)/shard_map/ppermute | solution.py:334
  61.1 1.7 %collective-permute-start.15 = (f32[32,128]{1,0:T(8,128)S(1)}, f32[32,128]{1,0:T(8,128)S(1)}, u32[]{:S(2)}, u32[]{:S(2)}) collective-permute-start(f32[32,128]{1,0:T(8,128)S(1)} %concatenate.13.refs_0_), channel_id=1, source_target_pairs={{0,64},{1,65},{2,66},{3,67},{4,68},{5,69},{6,70},{7,71},{8,72},{9,... | collective-permute-start | bytes 49160 | tf_op jit(solution)/shard_map/ppermute | solution.py:334
  62.8 0.0 copy-start.3
  62.8 1.9 %copy-done.3 = bf16[1280,1280]{1,0:T(8,128)(2,1)S(1)} copy-done((bf16[1280,1280]{1,0:T(8,128)(2,1)S(1)}, bf16[1280,1280]{1,0:T(8,128)(2,1)}, u32[]{:S(2)}) %copy-start.3) | copy-done | bytes 3276824
  64.7 1.7 %density_rows.1 = f32[1,256,1280]{2,1,0:T(8,128)} custom-call(f32[256,256]{1,0:T(8,128)S(1)} %get-tuple-element.25.core, f32[256,1280]{1,0:T(8,128)S(1)} %get-tuple-element.26.first, bf16[256,1280]{1,0:T(8,128)(2,1)S(1)} %get-tuple-element.27.y, bf16[1280,1280]{1,0:T(8,128)(2,1)S(1)} %copy-done.3), custom_call_target="tpu_custom_call" | custom-call | flops 838860800 | bytes 1310720 | tf_op jit(solution)/shard_map/density_rows/pallas_call | solution.py:262
  66.4 0.0 collective-permute-done.17.refs_3_
  66.4 0.0 collective-permute-done.16.refs_2_
  66.4 0.0 collective-permute-done.15.refs_1_
  66.5 1.2 %order_charges.1 = f32[128,128]{1,0:T(8,128)} custom-call(s32[1,5]{1,0:T(1,128)S(1)} %copy-done.8, f32[32,128]{1,0:T(8,128)S(1)} %concatenate.13.refs_0_, f32[32,128]{1,0:T(8,128)S(1)} %collective-permute-done.15.refs_1_, f32[32,128]{1,0:T(8,128)S(1)} %collective-permute-done.16.refs_2_, f32[32,128]{1,0:T(8,128)S(1)} %collective-permute-done.17.refs_3_), custom_call_target="tpu_custom_call" | custom-call | tf_op jit(solution)/shard_map/order_charges/pallas_call | solution.py:313
  (5 shorter events, 0.1 us)
Async XLA Ops:
  0.6 1.3 %copy-start = (bf16[1,9,256,256]{3,2,1,0:T(8,128)(2,1)S(1)}, bf16[1,9,256,256]{3,2,1,0:T(8,128)(2,1)}, u32[]{:S(2)}) copy-start(bf16[1,9,256,256]{3,2,1,0:T(8,128)(2,1)} %own.7) | copy-start | bytes 3538948
  2.8 17.7 %copy-start.1 = (bf16[1,9,256,256]{3,2,1,0:T(8,128)(2,1)S(1)}, bf16[1,9,256,256]{3,2,1,0:T(8,128)(2,1)}, u32[]{:S(2)}) copy-start(bf16[1,9,256,256]{3,2,1,0:T(8,128)(2,1)} %own.7) | copy-start | bytes 3538948
  2.8 17.7 %copy-start.8 = (s32[1,5]{1,0:T(1,128)S(1)}, s32[1,5]{1,0:T(1,128)}, u32[]{:S(2)}) copy-start(s32[1,5]{1,0:T(1,128)} %slots.5) | copy-start | bytes 64
  3.7 9.8 %collective-permute-start = (bf16[1,2,256,256]{3,2,1,0:T(8,128)(2,1)S(1)}, bf16[1,2,256,256]{3,2,1,0:T(8,128)(2,1)S(1)}, u32[]{:S(2)}, u32[]{:S(2)}) collective-permute-start(bf16[1,2,256,256]{3,2,1,0:T(8,128)(2,1)S(1)} %get-tuple-element.17), channel_id=1, source_target_pairs={{0,8},{8,16},{16,24},{24,32},{32,40},{40,48},{48,56},{56,64},{64,7... | collective-permute-start | bytes 786440 | tf_op jit(solution)/shard_map/ppermute | solution.py:328
  3.7 18.4 %collective-permute-start.5 = (bf16[1,4,256,256]{3,2,1,0:T(8,128)(2,1)}, bf16[1,4,256,256]{3,2,1,0:T(8,128)(2,1)S(1)}, u32[]{:S(2)}, u32[]{:S(2)}) collective-permute-start(bf16[1,4,256,256]{3,2,1,0:T(8,128)(2,1)} %get-tuple-element.24), channel_id=1, source_target_pairs={{0,1},{1,2},{2,3},{3,4},{4,5},{5,6},{6,7},{7,0},{8,9},{9,10},{10,1... | collective-permute-start | bytes 1572872 | tf_op jit(solution)/shard_map/ppermute | solution.py:328
  5.7 17.3 %collective-permute-start.4 = (bf16[1,4,256,256]{3,2,1,0:T(8,128)(2,1)S(1)}, bf16[1,4,256,256]{3,2,1,0:T(8,128)(2,1)S(1)}, u32[]{:S(2)}, u32[]{:S(2)}) collective-permute-start(bf16[1,4,256,256]{3,2,1,0:T(8,128)(2,1)S(1)} %get-tuple-element.16.earlier), channel_id=1, source_target_pairs={{1,0},{2,1},{3,2},{4,3},{5,4},{6,5},{7,6},{0,7},{9,8},{10,9},{11,1... | collective-permute-start | bytes 1572872 | tf_op jit(solution)/shard_map/ppermute | solution.py:331
  9.6 8.1 %collective-permute-start.1 = (bf16[1,2,256,256]{3,2,1,0:T(8,128)(2,1)}, bf16[1,2,256,256]{3,2,1,0:T(8,128)(2,1)S(1)}, u32[]{:S(2)}, u32[]{:S(2)}) collective-permute-start(bf16[1,2,256,256]{3,2,1,0:T(8,128)(2,1)} %get-tuple-element.18), channel_id=1, source_target_pairs={{0,8},{8,16},{16,24},{24,32},{32,40},{40,48},{48,56},{56,64},{64,7... | collective-permute-start | bytes 786440 | tf_op jit(solution)/shard_map/ppermute | solution.py:328
  10.9 6.8 %collective-permute-start.2 = (bf16[1,2,256,256]{3,2,1,0:T(8,128)(2,1)}, bf16[1,2,256,256]{3,2,1,0:T(8,128)(2,1)S(1)}, u32[]{:S(2)}, u32[]{:S(2)}) collective-permute-start(bf16[1,2,256,256]{3,2,1,0:T(8,128)(2,1)} %get-tuple-element.19), channel_id=1, source_target_pairs={{8,0},{16,8},{24,16},{32,24},{40,32},{48,40},{56,48},{64,56},{72,6... | collective-permute-start | bytes 786440 | tf_op jit(solution)/shard_map/ppermute | solution.py:331
  13.5 7.0 %collective-permute-start.3 = (bf16[1,2,256,256]{3,2,1,0:T(8,128)(2,1)}, bf16[1,2,256,256]{3,2,1,0:T(8,128)(2,1)}, u32[]{:S(2)}, u32[]{:S(2)}) collective-permute-start(bf16[1,2,256,256]{3,2,1,0:T(8,128)(2,1)} %get-tuple-element.20), channel_id=1, source_target_pairs={{8,0},{16,8},{24,16},{32,24},{40,32},{48,40},{56,48},{64,56},{72,6... | collective-permute-start | bytes 786440 | tf_op jit(solution)/shard_map/ppermute | solution.py:331
  22.2 0.8 %copy-start.4 = (bf16[1,4,256,256]{3,2,1,0:T(8,128)(2,1)}, bf16[1,4,256,256]{3,2,1,0:T(8,128)(2,1)S(1)}, u32[]{:S(2)}) copy-start(bf16[1,4,256,256]{3,2,1,0:T(8,128)(2,1)S(1)} %collective-permute-done.5.r3) | copy-start | bytes 1572868
  23.0 0.8 %copy-start.6 = (bf16[1,4,256,256]{3,2,1,0:T(8,128)(2,1)}, bf16[1,4,256,256]{3,2,1,0:T(8,128)(2,1)S(1)}, u32[]{:S(2)}) copy-start(bf16[1,4,256,256]{3,2,1,0:T(8,128)(2,1)S(1)} %collective-permute-done.4.r4) | copy-start | bytes 1572868
  23.8 1.0 %copy-start.5 = (bf16[1,4,256,256]{3,2,1,0:T(8,128)(2,1)S(1)}, bf16[1,4,256,256]{3,2,1,0:T(8,128)(2,1)}, u32[]{:S(2)}) copy-start(bf16[1,4,256,256]{3,2,1,0:T(8,128)(2,1)} %copy-done.4) | copy-start | bytes 1572868
  24.8 1.0 %copy-start.7 = (bf16[1,4,256,256]{3,2,1,0:T(8,128)(2,1)S(1)}, bf16[1,4,256,256]{3,2,1,0:T(8,128)(2,1)}, u32[]{:S(2)}) copy-start(bf16[1,4,256,256]{3,2,1,0:T(8,128)(2,1)} %copy-done.6) | copy-start | bytes 1572868
  32.8 1.7 %copy-start.2 = (bf16[1280,1280]{1,0:T(8,128)(2,1)}, bf16[1280,1280]{1,0:T(8,128)(2,1)S(1)}, u32[]{:S(2)}) copy-start(bf16[1280,1280]{1,0:T(8,128)(2,1)S(1)} %get-tuple-element.28.x1b) | copy-start | bytes 9830404
  34.5 3.5 %collective-permute-start.6 = (f32[1,128]{1,0:T(1,128)S(1)}, f32[1,128]{1,0:T(1,128)S(1)}, u32[]{:S(2)}, u32[]{:S(2)}) collective-permute-start(f32[1,128]{1,0:T(1,128)S(1)} %get-tuple-element.29), channel_id=1, source_target_pairs={{0,1},{1,0},{2,3},{3,2},{4,5},{5,4},{6,7},{7,6},{8,9},{9,8},{10,11... | collective-permute-start | bytes 1544 | tf_op jit(solution)/shard_map/ppermute | solution.py:334
  34.5 3.5 %collective-permute-start.8 = (f32[1,128]{1,0:T(1,128)S(1)}, f32[1,128]{1,0:T(1,128)S(1)}, u32[]{:S(2)}, u32[]{:S(2)}) collective-permute-start(f32[1,128]{1,0:T(1,128)S(1)} %get-tuple-element.29), channel_id=1, source_target_pairs={{0,9},{1,8},{2,11},{3,10},{4,13},{5,12},{6,15},{7,14},{8,1},{9,0},... | collective-permute-start | bytes 1544 | tf_op jit(solution)/shard_map/ppermute | solution.py:334
  36.1 2.0 %collective-permute-start.7 = (f32[1,128]{1,0:T(1,128)S(1)}, f32[1,128]{1,0:T(1,128)S(1)}, u32[]{:S(2)}, u32[]{:S(2)}) collective-permute-start(f32[1,128]{1,0:T(1,128)S(1)} %get-tuple-element.29), channel_id=1, source_target_pairs={{0,8},{1,9},{2,10},{3,11},{4,12},{5,13},{6,14},{7,15},{8,0},{9,1},... | collective-permute-start | bytes 1544 | tf_op jit(solution)/shard_map/ppermute | solution.py:334
  38.0 7.9 %collective-permute-start.11 = (f32[2,128]{1,0:T(2,128)S(1)}, f32[2,128]{1,0:T(2,128)S(1)}, u32[]{:S(2)}, u32[]{:S(2)}) collective-permute-start(f32[2,128]{1,0:T(2,128)S(1)} %pad_maximum_fusion), channel_id=1, source_target_pairs={{0,6},{1,7},{2,4},{3,5},{4,2},{5,3},{6,0},{7,1},{8,14},{9,15},{10,... | collective-permute-start | bytes 3080 | tf_op jit(solution)/shard_map/ppermute | solution.py:334
  41.1 7.5 %collective-permute-start.10 = (f32[2,128]{1,0:T(2,128)S(1)}, f32[2,128]{1,0:T(2,128)S(1)}, u32[]{:S(2)}, u32[]{:S(2)}) collective-permute-start(f32[2,128]{1,0:T(2,128)S(1)} %pad_maximum_fusion), channel_id=1, source_target_pairs={{0,4},{1,5},{2,6},{3,7},{4,0},{5,1},{6,2},{7,3},{8,12},{9,13},{10,... | collective-permute-start | bytes 3080 | tf_op jit(solution)/shard_map/ppermute | solution.py:334
  45.9 4.5 %collective-permute-start.9 = (f32[2,128]{1,0:T(2,128)S(1)}, f32[2,128]{1,0:T(2,128)S(1)}, u32[]{:S(2)}, u32[]{:S(2)}) collective-permute-start(f32[2,128]{1,0:T(2,128)S(1)} %pad_maximum_fusion), channel_id=1, source_target_pairs={{0,2},{1,3},{2,0},{3,1},{4,6},{5,7},{6,4},{7,5},{8,10},{9,11},{10,... | collective-permute-start | bytes 3080 | tf_op jit(solution)/shard_map/ppermute | solution.py:334
  50.4 4.9 %collective-permute-start.14 = (f32[8,128]{1,0:T(8,128)S(1)}, f32[8,128]{1,0:T(8,128)S(1)}, u32[]{:S(2)}, u32[]{:S(2)}) collective-permute-start(f32[8,128]{1,0:T(8,128)S(1)} %concatenate.12), channel_id=1, source_target_pairs={{0,48},{1,49},{2,50},{3,51},{4,52},{5,53},{6,54},{7,55},{8,56},{9,... | collective-permute-start | bytes 12296 | tf_op jit(solution)/shard_map/ppermute | solution.py:334
  53.4 5.1 %collective-permute-start.13 = (f32[8,128]{1,0:T(8,128)S(1)}, f32[8,128]{1,0:T(8,128)S(1)}, u32[]{:S(2)}, u32[]{:S(2)}) collective-permute-start(f32[8,128]{1,0:T(8,128)S(1)} %concatenate.12), channel_id=1, source_target_pairs={{0,32},{1,33},{2,34},{3,35},{4,36},{5,37},{6,38},{7,39},{8,40},{9,... | collective-permute-start | bytes 12296 | tf_op jit(solution)/shard_map/ppermute | solution.py:334
  54.0 4.5 %collective-permute-start.12 = (f32[8,128]{1,0:T(8,128)S(1)}, f32[8,128]{1,0:T(8,128)S(1)}, u32[]{:S(2)}, u32[]{:S(2)}) collective-permute-start(f32[8,128]{1,0:T(8,128)S(1)} %concatenate.12), channel_id=1, source_target_pairs={{0,16},{1,17},{2,18},{3,19},{4,20},{5,21},{6,22},{7,23},{8,24},{9,... | collective-permute-start | bytes 12296 | tf_op jit(solution)/shard_map/ppermute | solution.py:334
  58.6 7.8 %collective-permute-start.17 = (f32[32,128]{1,0:T(8,128)S(1)}, f32[32,128]{1,0:T(8,128)S(1)}, u32[]{:S(2)}, u32[]{:S(2)}) collective-permute-start(f32[32,128]{1,0:T(8,128)S(1)} %concatenate.13.refs_0_), channel_id=1, source_target_pairs={{0,192},{1,193},{2,194},{3,195},{4,196},{5,197},{6,198},{7,199},{8... | collective-permute-start | bytes 49160 | tf_op jit(solution)/shard_map/ppermute | solution.py:334
  58.9 7.5 %collective-permute-start.16 = (f32[32,128]{1,0:T(8,128)S(1)}, f32[32,128]{1,0:T(8,128)S(1)}, u32[]{:S(2)}, u32[]{:S(2)}) collective-permute-start(f32[32,128]{1,0:T(8,128)S(1)} %concatenate.13.refs_0_), channel_id=1, source_target_pairs={{0,128},{1,129},{2,130},{3,131},{4,132},{5,133},{6,134},{7,135},{8... | collective-permute-start | bytes 49160 | tf_op jit(solution)/shard_map/ppermute | solution.py:334
  61.1 5.3 %collective-permute-start.15 = (f32[32,128]{1,0:T(8,128)S(1)}, f32[32,128]{1,0:T(8,128)S(1)}, u32[]{:S(2)}, u32[]{:S(2)}) collective-permute-start(f32[32,128]{1,0:T(8,128)S(1)} %concatenate.13.refs_0_), channel_id=1, source_target_pairs={{0,64},{1,65},{2,66},{3,67},{4,68},{5,69},{6,70},{7,71},{8,72},{9,... | collective-permute-start | bytes 49160 | tf_op jit(solution)/shard_map/ppermute | solution.py:334
  62.8 1.9 %copy-start.3 = (bf16[1280,1280]{1,0:T(8,128)(2,1)S(1)}, bf16[1280,1280]{1,0:T(8,128)(2,1)}, u32[]{:S(2)}) copy-start(bf16[1280,1280]{1,0:T(8,128)(2,1)} %copy-done.2) | copy-start | bytes 9830404

commit v5 on v3

--- a/solution.py
+++ b/solution.py
@@ -5,6 +5,7 @@
 from jax import lax
 from jax.experimental import pallas as pl
 from jax.experimental.pallas import tpu as pltpu
+from jax.sharding import Mesh
 from jax.sharding import PartitionSpec as P
 
 ORBS = 4
@@ -110,8 +111,8 @@
 
 
 def late_kernel(
-    slots, potential, own, early, turned, sums, r3, r4, density, charges,
-    x0, x0b, q0b, x1b, out, sems,
+    n_sub, slots, potential, own, early, turned, sums, r4, r3, density, charges,
+    first, x1b, x0, x0b, q0b, out, sems,
 ):
     blk = own.shape[-1]
     f32, bf16 = jnp.float32, jnp.bfloat16
@@ -125,13 +126,10 @@
         return tile_of(ORDER[p], ORDER[q]) is not None
 
     def product(left, right, p, q):
-        inner = [
-            k for k in range(SLOTS)
-            if (left is not x0b or coupled(p, k)) and (right is not x0b or coupled(k, q))
-        ]
+        inner = [k for k in range(SLOTS) if right is not x0b or coupled(k, q)]
         total = None
         for lo, hi in runs(inner):
-            term = jnp.dot(left[at(p), at(lo, hi)], right[at(lo, hi), at(q)], preferred_element_type=f32)
+            term = jnp.dot(left[at(0, p + 1), at(lo, hi)], right[at(lo, hi), at(q)], preferred_element_type=f32)
             total = added(total, term)
         return total
 
@@ -144,9 +142,9 @@
     def place(i, j):
         return ORDER.index(i), ORDER.index(j)
 
-    for i, j in LATE_PAIRS:
-        p, q = place(i, j)
-        x0[at(p), at(q)] = halo.block(i, j, turned[TURNED.index((i, j))] if (i, j) in TURNED else None)
+    for n, (i, j) in enumerate(PAIRS):
+        if (i, j) in LATE_PAIRS:
+            x0[n] = halo.block(i, j, turned[TURNED.index((i, j))] if (i, j) in TURNED else None)
     largest = None
     for i in range(SLOTS):
         total = halo.sums(i)
@@ -156,30 +154,33 @@
         largest = top if largest is None else jnp.maximum(largest, top)
     inv = 1.0 / (2.0 * jnp.sqrt(largest + 1e-06))
 
-    for i, j in PAIRS:
-        p, q = place(i, j)
-        if (i, j) in EARLY_PAIRS:
-            block = early[EARLY_PAIRS.index((i, j))] * inv
-        else:
-            block = x0[at(p), at(q)] * inv
-        x0[at(p), at(q)] = block
-        mirror(x0b, p, q, block)
-    upper = [(p, q) for p in range(SLOTS) for q in range(p, SLOTS)]
-    for p, q in upper:
-        mirror(q0b, p, q, product(x0b, x0b, p, q))
-    for p, q in upper:
-        block = -0.5 * product(x0b, q0b, p, q)
-        if coupled(p, q):
-            block = 1.5 * x0[at(p), at(q)] + block
-        if p == 0:
-            x0[at(0), at(q)] = block
-        mirror(x1b, p, q, block)
+    for n, (i, j) in enumerate(PAIRS):
+        block = early[EARLY_PAIRS.index((i, j))] if (i, j) in EARLY_PAIRS else x0[n]
+        x0[n] = block * inv
+        mirror(x0b, *place(i, j), x0[n])
+    for p in range(SLOTS):
+        for q in range(SLOTS):
+            if not coupled(p, q):
+                x0b[at(p), at(q)] = jnp.zeros((blk, blk), bf16)
+    for q in range(SLOTS):
+        panel = product(x0b, x0b, q, q)
+        for p in range(q + 1):
+            mirror(q0b, p, q, panel[at(p)])
+    for q in range(SLOTS):
+        panel = product(x0b, q0b, q, q)
+        for p in range(q + 1):
+            block = -0.5 * panel[at(p)]
+            if coupled(p, q):
+                block = 1.5 * x0[PAIRS.index((ORDER[p], ORDER[q]))] + block
+            if p == 0:
+                first[:, at(q)] = block
+            mirror(x1b, p, q, block)
     left = jnp.concatenate(
         [product(x1b, x1b, 0, q).astype(bf16) for q in range(SLOTS)], axis=1
     )
     copies = []
     for q in range(SLOTS):
-        sign = 1.5 * x0[at(0), at(q)] - 0.5 * jnp.dot(
+        sign = 1.5 * first[:, at(q)] - 0.5 * jnp.dot(
             left, x1b[:, at(q)], preferred_element_type=f32
         )
         if q == 0:
@@ -195,7 +196,8 @@
             occupied = jnp.sum(jnp.where(eye, result, 0.0), axis=1, keepdims=True)
             lanes = charges.shape[1]
             atoms = blk // ORBS
-            atom = lax.broadcasted_iota(jnp.int32, (blk, lanes), 0) // ORBS + slots[0, 0] % 2 * atoms
+            half = slots[0, 0] // n_sub % 2
+            atom = lax.broadcasted_iota(jnp.int32, (blk, lanes), 0) // ORBS + half * atoms
             lane = lax.broadcasted_iota(jnp.int32, (blk, lanes), 1)
             charges[...] = jnp.sum(
                 jnp.where(atom == lane, 4.0 / ORBS - 2.0 * occupied, 0.0), axis=0, keepdims=True
@@ -212,8 +214,7 @@
 SMALL = pl.CostEstimate(flops=1, bytes_accessed=1, transcendentals=0)
 
 
-def limit(mib):
-    return pltpu.CompilerParams(vmem_limit_bytes=mib * MIB)
+LIMIT = pltpu.CompilerParams(vmem_limit_bytes=20 * MIB)
 
 
 def early_part(slots, potential, own, *halves):
@@ -227,17 +228,17 @@
         ),
         in_specs=[SMEM, SMEM] + [VMEM] * 5,
         out_specs=(VMEM, VMEM, VMEM),
-        compiler_params=limit(12),
+        compiler_params=LIMIT,
         cost_estimate=SMALL,
         name="early_blocks",
     )(slots, potential, own, *halves)
 
 
-def late_part(slots, potential, own, early, turned, sums, r3, r4):
+def late_part(slots, potential, own, early, turned, sums, r4, r3, n_sub):
     blk = own.shape[-1]
     order = SLOTS * blk
     return pl.pallas_call(
-        late_kernel,
+        functools.partial(late_kernel, n_sub),
         out_shape=(
             jax.ShapeDtypeStruct((1, blk, order), jnp.float32),
             jax.ShapeDtypeStruct((1, LANES), jnp.float32),
@@ -245,16 +246,17 @@
         in_specs=[SMEM, SMEM] + [VMEM] * 6,
         out_specs=(ANY, VMEM),
         scratch_shapes=[
-            pltpu.VMEM((order, order), jnp.float32),
+            pltpu.VMEM((blk, order), jnp.float32),
             pltpu.VMEM((order, order), jnp.bfloat16),
+            pltpu.VMEM((len(PAIRS), blk, blk), jnp.float32),
             pltpu.VMEM((order, order), jnp.bfloat16),
             pltpu.VMEM((order, order), jnp.bfloat16),
             pltpu.VMEM((SLOTS, blk, blk), jnp.float32),
             pltpu.SemaphoreType.DMA((SLOTS,)),
         ],
-        compiler_params=limit(32),
+        compiler_params=LIMIT,
         name="density_rows",
-    )(slots, potential, own, early, turned, sums, r3, r4)
+    )(slots, potential, own, early, turned, sums, r4, r3)
 
 
 def pack_kernel(groups, own, earlier, *packs):
@@ -272,31 +274,39 @@
         ),
         in_specs=[VMEM, ANY],
         out_specs=(VMEM,) * len(groups),
-        compiler_params=limit(4),
+        compiler_params=LIMIT,
         cost_estimate=SMALL,
         name="pack_halo",
     )(own, earlier)
 
 
-def pair_kernel(rows, out):
-    half = out.shape[0]
-    out[...] = rows[pl.ds(0, half, stride=2), :] + rows[pl.ds(1, half, stride=2), :]
-
-
-def paired(rows):
+def order_kernel(rows, out):
+    half = rows.shape[0] // 2
+    even = rows[pl.ds(0, half, stride=2), :]
+    odd = rows[pl.ds(1, half, stride=2), :]
+    low = lax.broadcasted_iota(jnp.int32, even.shape, 1) < LANES // 2
+    first = jnp.where(low, even, pltpu.roll(odd, LANES // 2, 1))
+    second = jnp.where(low, pltpu.roll(even, LANES // 2, 1), odd)
+    for chip in range(half // 4):
+        out[8 * chip : 8 * chip + 4, :] = first[4 * chip : 4 * chip + 4]
+        out[8 * chip + 4 : 8 * chip + 8, :] = second[4 * chip : 4 * chip + 4]
+
+
+def in_order(rows):
     return pl.pallas_call(
-        pair_kernel,
-        out_shape=jax.ShapeDtypeStruct((rows.shape[0] // 2, rows.shape[1]), rows.dtype),
+        order_kernel,
+        out_shape=jax.ShapeDtypeStruct(rows.shape, rows.dtype),
         in_specs=[VMEM],
         out_specs=VMEM,
-        compiler_params=limit(2),
-        name="pair_charges",
+        compiler_params=LIMIT,
+        name="order_charges",
     )(rows)
 
 
 def shards(hamiltonian, partitions, chemical_potential):
-    n_dom = lax.axis_size("dom")
-    n_sub = lax.axis_size("sub")
+    n_chip, n_core = lax.axis_size("chip"), lax.axis_size("core")
+    n_dom, n_sub = n_chip * n_core, lax.axis_size("sub")
+    dom = ("chip", "core")
     potential = chemical_potential.reshape(1, 1)
 
     def up(x, axis, size):
@@ -305,28 +315,35 @@
     def down(x, axis, size):
         return lax.ppermute(x, axis, [((i + 1) % size, i) for i in range(size)])
 
-    sub_up, sub_down = packed(hamiltonian, hamiltonian, SENT[3], SENT[4])
+    def joined(tiles):
+        return jnp.concatenate([hamiltonian[:, k : k + 1] for k in tiles], axis=1)
+
+    sub_up, sub_down = joined(SENT[3]), joined(SENT[4])
     dom_parts = packed(
         hamiltonian, sub_up, SENT[1][:2], SENT[1][2:], SENT[2][:2], SENT[2][2:]
     )
-    r3, r4 = up(sub_up, "sub", n_sub), down(sub_down, "sub", n_sub)
-    halves = [up(x, "dom", n_dom) for x in dom_parts[:2]]
-    halves += [down(x, "dom", n_dom) for x in dom_parts[2:]]
+    r4 = down(sub_down, "sub", n_sub)
+    r3 = up(sub_up, "sub", n_sub)
+    halves = [up(x, dom, n_dom) for x in dom_parts[:2]]
+    halves += [down(x, dom, n_dom) for x in dom_parts[2:]]
     early, turned, sums = early_part(partitions, potential, hamiltonian, *halves)
     density, row = late_part(
-        partitions, potential, hamiltonian, early, turned, sums, r3, r4
+        partitions, potential, hamiltonian, early, turned, sums, r4, r3, n_sub
     )
-    copies = jnp.broadcast_to(row, (n_dom * n_sub, LANES))
-    rows = lax.all_to_all(copies, ("dom", "sub"), 0, 0, tiled=True)
-    charges = paired(rows).reshape(-1)
-    return (density, charges)
+    row = row + lax.ppermute(row, "core", [(i, n_core - 1 - i) for i in range(n_core)])
+    copies = jnp.broadcast_to(row, (n_chip * n_sub, LANES))
+    rows = lax.all_to_all(copies, ("chip", "sub"), 0, 0, tiled=True)
+    return (density, in_order(rows).reshape(-1))
 
 
 def solution(mesh):
+    n_dom, n_sub = mesh.shape["dom"], mesh.shape["sub"]
+    devices = ("chip", "core", "sub")
+    cores = Mesh(mesh.devices.reshape(n_dom // 2, 2, n_sub), devices)
     return jax.shard_map(
         shards,
-        mesh=mesh,
-        in_specs=(P(("dom", "sub"), None, None, None), P(("dom", "sub"), None), P()),
-        out_specs=(P(("dom", "sub"), None, None), P()),
+        mesh=cores,
+        in_specs=(P(devices, None, None, None), P(devices, None), P()),
+        out_specs=(P(devices, None, None), P()),
         check_vma=False,
     )

time: 57.2 us -> 59.7 us (1.044)
  waiting for transfers between devices: 7.97 us -> 5.67 us
  starting transfers between devices: 12.4 us -> 14.2 us
  blocking collectives: 21.7 us -> 22.9 us
  other arithmetic: 0 us -> 0.93 us
  Pallas kernels: 12.3 us -> 13 us
    ppermute x3, waiting for transfers between devices: 3.12 us -> 0.01 us  [up(): return lax.ppermute(x, axis, [(i, (i + 1) % size) for i in range(size)])]
    ppermute x3, starting transfers between devices: 2.89 us -> 4.88 us  [up(): return lax.ppermute(x, axis, [(i, (i + 1) % size) for i in range(size)])]
    ppermute x3, starting transfers between devices: 9.55 us -> 7.77 us  [down(): return lax.ppermute(x, axis, [((i + 1) % size, i) for i in range(size)])]
    ppermute x0 -> x1, starting transfers between devices: none -> 1.6 us  [shards(): lax.ppermute(row, 'core', [(i, n_core - 1 - i) for i in range(n_core)])]
    pallas_call x2, Pallas kernels: 8.89 us -> 10.4 us  [the longest x1 9.69 us: late_part(): pl.pallas_call(functools.partial(late_kernel, n_sub), out_shape=(jax.Shap...]
    slice x0 -> x3, local copies, waits for them, and re-layouts: none -> 1.36 us  [joined(): return jnp.concatenate([hamiltonian[:, k:k + 1] for k in tiles], axis=1)]
    unnamed x6 -> x4, local copies, waits for them, and re-layouts: 1.27 us -> 0.01 us
    all_to_all x1, blocking collectives: 21.7 us -> 22.9 us  [shards(): rows = lax.all_to_all(copies, ('chip', 'sub'), 0, 0, tiled=True)]
  transfers between devices with their start and end apart: 6 -> 7, of which waited for: 4 -> 4; matrix products, arithmetic and copies ran while one was open for 0% -> 1% of each run, Pallas kernels for 3% -> 4%
where the time goes in v5:
time: 59.7 us; the launch traced here: 59.5 us
  blocking collectives  22.9 us (38%)
  starting transfers between devices  14.2 us (24%)
  Pallas kernels  13 us (22%)
  waiting for transfers between devices  5.67 us (9%)
  local copies, waits for them, and re-layouts  1.41 us (2%)
  between operations  1.37 us (2%)
  other arithmetic  0.93 us (2%)
    all_to_all x1, blocking collectives, shards(): rows = lax.all_to_all(copies, ('chip', 'sub'), 0, 0, tiled=True)  22.9 us
    pallas_call x1, Pallas kernels, late_part(): pl.pallas_call(functools.partial(late_kernel, n_sub), out_shape=(jax.Shap...  9.69 us
    ppermute x3, starting transfers between devices, down(): return lax.ppermute(x, axis, [((i + 1) % size, i) for i in range(size)])  7.77 us
    ppermute x3, starting transfers between devices, up(): return lax.ppermute(x, axis, [(i, (i + 1) % size) for i in range(size)])  4.88 us
    ppermute x3, waiting for transfers between devices, down(): return lax.ppermute(x, axis, [((i + 1) % size, i) for i in range(size)])  4.85 us
    pallas_call x1, Pallas kernels, early_part(): pl.pallas_call(early_kernel, out_shape=(jax.ShapeDtypeStruct((len(EARLY_P...  1.64 us
    ppermute x1, starting transfers between devices, shards(): lax.ppermute(row, 'core', [(i, n_core - 1 - i) for i in range(n_core)])  1.6 us
    slice x3, local copies, waits for them, and re-layouts, joined(): return jnp.concatenate([hamiltonian[:, k:k + 1] for k in tiles], axis=1)  1.36 us
  transfers between devices with their start and end apart: 7, of which 4 were waited for; matrix products, arithmetic and copies ran while one was open for 1% of the time, Pallas kernels for 4%

profile of v5, /device:TPU:1, one launch (start us, length us, event | category | flops | bytes accessed | tf_op | source)
XLA Modules:
  0.0 59.5 jit_solution(10434101305378726691)
XLA Ops:
  0.6 0.0 slice-start
  0.6 0.0 copy-start
  0.6 1.4 %fusion = (bf16[1,1,256,256]{3,2,1,0:T(8,128)(2,1)S(1)}, bf16[1,1,256,256]{3,2,1,0:T(8,128)(2,1)S(1)}, bf16[1,1,256,256]{3,2,1,0:T(8,128)(2,1)S(1)}, bf16[1,1,25...) fusion(bf16[1,9,256,256]{3,2,1,0:T(8,128)(2,1)} %own.5), kind=kLoop, calls=%fused_computation.3 | loop fusion | bytes 1572864 | tf_op jit(solution)/shard_map/slice | solution.py:319
  2.0 0.0 slice-done
  2.0 0.1 pad_maximum_fusion.earlier
  2.1 0.0 copy-start.1
  2.1 2.5 %collective-permute-start.5 = (bf16[1,4,256,256]{3,2,1,0:T(8,128)(2,1)S(1)}, bf16[1,4,256,256]{3,2,1,0:T(8,128)(2,1)S(1)}, u32[]{:S(2)}, u32[]{:S(2)}) collective-permute-start(bf16[1,4,256,256]{3,2,1,0:T(8,128)(2,1)S(1)} %pad_maximum_fusion.earlier), channel_id=1, source_target_pairs={{0,1},{1,2},{2,3},{3,4},{4,5},{5,6},{6,7},{7,0},{8,9},{9,10},{10,1... | collective-permute-start | bytes 1572872 | tf_op jit(solution)/shard_map/ppermute | solution.py:313
  4.6 0.0 copy-done
  4.7 0.9 %pack_halo.1 = (bf16[1,2,256,256]{3,2,1,0:T(8,128)(2,1)S(1)}, bf16[1,2,256,256]{3,2,1,0:T(8,128)(2,1)}, bf16[1,2,256,256]{3,2,1,0:T(8,128)(2,1)}, bf16[1,2,256,256]{3,2,1,0:T(8,128)(2,1)}) custom-call(bf16[1,9,256,256]{3,2,1,0:T(8,128)(2,1)S(1)} %copy-done, bf16[1,4,256,256]{3,2,1,0:T(8,128)(2,1)S(1)} %pad_maximum_fusion.earlier), custom_call_target="tpu_custom_call" | custom-call | flops 1 | bytes 1 | tf_op jit(solution)/shard_map/pack_halo/pallas_call | solution.py:270
  5.6 2.1 %collective-permute-start = (bf16[1,2,256,256]{3,2,1,0:T(8,128)(2,1)S(1)}, bf16[1,2,256,256]{3,2,1,0:T(8,128)(2,1)S(1)}, u32[]{:S(2)}, u32[]{:S(2)}) collective-permute-start(bf16[1,2,256,256]{3,2,1,0:T(8,128)(2,1)S(1)} %get-tuple-element.11), channel_id=1, source_target_pairs={{0,8},{8,16},{16,24},{24,32},{32,40},{40,48},{48,56},{56,64},{64,7... | collective-permute-start | bytes 786440 | tf_op jit(solution)/shard_map/ppermute | solution.py:313
  7.6 0.9 %pad_maximum_fusion.1 = bf16[1,4,256,256]{3,2,1,0:T(8,128)(2,1)} fusion(bf16[1,1,256,256]{3,2,1,0:T(8,128)(2,1)S(1)} %get-tuple-element.25, bf16[1,1,256,256]{3,2,1,0:T(8,128)(2,1)S(1)} %get-tuple-element.21, bf16[1,1,256,256]{3,2,1,0:T(8,128)(2,1)S(1)} %get-tuple-element.22, bf16[1,1,256,256]{3,2,1,0:T(8,128)(2,1)S(1)} %get-tuple-element.20), kind=kLoop, calls=%fused_computation.1 | loop fusion | flops 786432 | bytes 1048576 | tf_op jit(solution)/shard_map/concatenate | solution.py:319
  8.5 3.8 %collective-permute-start.4 = (bf16[1,4,256,256]{3,2,1,0:T(8,128)(2,1)}, bf16[1,4,256,256]{3,2,1,0:T(8,128)(2,1)S(1)}, u32[]{:S(2)}, u32[]{:S(2)}) collective-permute-start(bf16[1,4,256,256]{3,2,1,0:T(8,128)(2,1)} %pad_maximum_fusion.1), channel_id=1, source_target_pairs={{1,0},{2,1},{3,2},{4,3},{5,4},{6,5},{7,6},{0,7},{9,8},{10,9},{11,1... | collective-permute-start | bytes 1572872 | tf_op jit(solution)/shard_map/ppermute | solution.py:316
  12.3 0.3 collective-permute-start.1
  12.6 0.2 collective-permute-start.2
  12.8 0.0 collective-permute-done.r1a
  12.8 3.7 %collective-permute-start.3 = (bf16[1,2,256,256]{3,2,1,0:T(8,128)(2,1)}, bf16[1,2,256,256]{3,2,1,0:T(8,128)(2,1)}, u32[]{:S(2)}, u32[]{:S(2)}) collective-permute-start(bf16[1,2,256,256]{3,2,1,0:T(8,128)(2,1)} %get-tuple-element.14), channel_id=1, source_target_pairs={{8,0},{16,8},{24,16},{32,24},{40,32},{48,40},{56,48},{64,56},{72,6... | collective-permute-start | bytes 786440 | tf_op jit(solution)/shard_map/ppermute | solution.py:316
  17.2 0.0 collective-permute-done.1.r1b
  17.2 1.7 %collective-permute-done.2.r2a = bf16[1,2,256,256]{3,2,1,0:T(8,128)(2,1)S(1)} collective-permute-done((bf16[1,2,256,256]{3,2,1,0:T(8,128)(2,1)}, bf16[1,2,256,256]{3,2,1,0:T(8,128)(2,1)S(1)}, u32[]{:S(2)}, u32[]{:S(2)}) %collective-permute-start.2) | collective-permute-done | bytes 262176 | tf_op jit(solution)/shard_map/ppermute | solution.py:316
  18.9 2.6 %collective-permute-done.3.r2b = bf16[1,2,256,256]{3,2,1,0:T(8,128)(2,1)} collective-permute-done((bf16[1,2,256,256]{3,2,1,0:T(8,128)(2,1)}, bf16[1,2,256,256]{3,2,1,0:T(8,128)(2,1)}, u32[]{:S(2)}, u32[]{:S(2)}) %collective-permute-start.3) | collective-permute-done | bytes 262176 | tf_op jit(solution)/shard_map/ppermute | solution.py:316
  21.5 0.0 copy-done.1
  21.5 1.6 %early_blocks.1 = (f32[5,256,256]{2,1,0:T(8,128)S(1)}, bf16[4,256,256]{2,1,0:T(8,128)(2,1)S(1)}, f32[256,128]{1,0:T(8,128)S(1)}) custom-call(s32[1,5]{1,0:T(1,128)S(1)} %copy-done.1, f32[1,1]{1,0:T(1,128)} %bitcast.5.potential, bf16[1,9,256,256]{3,2,1,0:T(8,128)(2,1)S(1)} %copy-done, bf16[1,2,256,256]{3,2,1,0:T(8,128)(2,1)S(1)} %collective-permute-done.r1a, ...), custom_call_target="tpu_custom_call" | custom-call | flops 1 | bytes 1 | tf_op jit(solution)/shard_map/early_blocks/pallas_call | solution.py:222
  23.2 0.0 collective-permute-done.5.r3
  23.2 0.6 collective-permute-done.4.r4
  23.7 9.7 %density_rows.1 = (f32[1,256,1280]{2,1,0:T(8,128)}, f32[1,128]{1,0:T(1,128)S(1)}) custom-call(s32[1,5]{1,0:T(1,128)S(1)} %copy-done.1, f32[1,1]{1,0:T(1,128)} %bitcast.6.potential, bf16[1,9,256,256]{3,2,1,0:T(8,128)(2,1)S(1)} %copy-done, f32[5,256,256]{2,1,0:T(8,128)S(1)} %get-tuple-element.15.early, bf16[4,256,256]{2,1,0:T(8,128)(2,1)S(1)} %get-tuple-element.16.turned, ...), custom_call_target="tpu_custom_call" | custom-call | tf_op jit(solution)/shard_map/density_rows/pallas_call | solution.py:240
  33.4 1.6 %collective-permute-start.6 = (f32[1,128]{1,0:T(1,128)S(1)}, f32[1,128]{1,0:T(1,128)S(1)}, u32[]{:S(2)}, u32[]{:S(2)}) collective-permute-start(f32[1,128]{1,0:T(1,128)S(1)} %get-tuple-element.19), channel_id=1, source_target_pairs={{0,8},{8,0},{1,9},{9,1},{2,10},{10,2},{3,11},{11,3},{4,12},{12,4},... | collective-permute-start | bytes 1544 | tf_op jit(solution)/shard_map/ppermute | solution.py:333
  35.0 0.8 %collective-permute-done.6 = f32[1,128]{1,0:T(1,128)S(1)} collective-permute-done((f32[1,128]{1,0:T(1,128)S(1)}, f32[1,128]{1,0:T(1,128)S(1)}, u32[]{:S(2)}, u32[]{:S(2)}) %collective-permute-start.6) | collective-permute-done | bytes 544 | tf_op jit(solution)/shard_map/ppermute | solution.py:333
  35.9 22.9 %all_to_all.8 = f32[128,1,128]{2,1,0:T(1,128)S(1)} all-to-all(f32[128,1,128]{2,1,0:T(1,128)S(1)} %broadcast_in_dim.2), channel_id=1, replica_groups=mesh['chip'=16,'core'=2,'sub'=8] {'chip','sub'}, dimensions={0} | all-to-all | bytes 131072 | tf_op jit(solution)/shard_map/all_to_all | solution.py:335
  58.8 0.7 %order_charges.1 = f32[128,128]{1,0:T(8,128)} custom-call(f32[128,128]{1,0:T(8,128)S(1)} %bitcast.7), custom_call_target="tpu_custom_call" | custom-call | tf_op jit(solution)/shard_map/order_charges/pallas_call | solution.py:296
  (2 shorter events, 0.0 us)
Async XLA Ops:
  0.6 1.4 %slice-start = ((bf16[1,9,256,256]{3,2,1,0:T(8,128)(2,1)}), bf16[1,2,256,256]{3,2,1,0:T(8,128)(2,1)S(1)}, s32[]{:S(2)}) async-start(bf16[1,9,256,256]{3,2,1,0:T(8,128)(2,1)} %own.5), calls=%async_computation.1 | async-start | bytes 524288 | tf_op jit(solution)/shard_map/slice | solution.py:319
  0.6 4.0 %copy-start = (bf16[1,9,256,256]{3,2,1,0:T(8,128)(2,1)S(1)}, bf16[1,9,256,256]{3,2,1,0:T(8,128)(2,1)}, u32[]{:S(2)}) copy-start(bf16[1,9,256,256]{3,2,1,0:T(8,128)(2,1)} %own.5) | copy-start | bytes 3538948
  2.1 19.4 %copy-start.1 = (s32[1,5]{1,0:T(1,128)S(1)}, s32[1,5]{1,0:T(1,128)}, u32[]{:S(2)}) copy-start(s32[1,5]{1,0:T(1,128)} %slots.3) | copy-start | bytes 64
  2.1 21.1 %collective-permute-start.5 = (bf16[1,4,256,256]{3,2,1,0:T(8,128)(2,1)S(1)}, bf16[1,4,256,256]{3,2,1,0:T(8,128)(2,1)S(1)}, u32[]{:S(2)}, u32[]{:S(2)}) collective-permute-start(bf16[1,4,256,256]{3,2,1,0:T(8,128)(2,1)S(1)} %pad_maximum_fusion.earlier), channel_id=1, source_target_pairs={{0,1},{1,2},{2,3},{3,4},{4,5},{5,6},{6,7},{7,0},{8,9},{9,10},{10,1... | collective-permute-start | bytes 1572872 | tf_op jit(solution)/shard_map/ppermute | solution.py:313
  5.6 7.2 %collective-permute-start = (bf16[1,2,256,256]{3,2,1,0:T(8,128)(2,1)S(1)}, bf16[1,2,256,256]{3,2,1,0:T(8,128)(2,1)S(1)}, u32[]{:S(2)}, u32[]{:S(2)}) collective-permute-start(bf16[1,2,256,256]{3,2,1,0:T(8,128)(2,1)S(1)} %get-tuple-element.11), channel_id=1, source_target_pairs={{0,8},{8,16},{16,24},{24,32},{32,40},{40,48},{48,56},{56,64},{64,7... | collective-permute-start | bytes 786440 | tf_op jit(solution)/shard_map/ppermute | solution.py:313
  8.5 15.2 %collective-permute-start.4 = (bf16[1,4,256,256]{3,2,1,0:T(8,128)(2,1)}, bf16[1,4,256,256]{3,2,1,0:T(8,128)(2,1)S(1)}, u32[]{:S(2)}, u32[]{:S(2)}) collective-permute-start(bf16[1,4,256,256]{3,2,1,0:T(8,128)(2,1)} %pad_maximum_fusion.1), channel_id=1, source_target_pairs={{1,0},{2,1},{3,2},{4,3},{5,4},{6,5},{7,6},{0,7},{9,8},{10,9},{11,1... | collective-permute-start | bytes 1572872 | tf_op jit(solution)/shard_map/ppermute | solution.py:316
  12.3 4.9 %collective-permute-start.1 = (bf16[1,2,256,256]{3,2,1,0:T(8,128)(2,1)}, bf16[1,2,256,256]{3,2,1,0:T(8,128)(2,1)S(1)}, u32[]{:S(2)}, u32[]{:S(2)}) collective-permute-start(bf16[1,2,256,256]{3,2,1,0:T(8,128)(2,1)} %get-tuple-element.12), channel_id=1, source_target_pairs={{0,8},{8,16},{16,24},{24,32},{32,40},{40,48},{48,56},{56,64},{64,7... | collective-permute-start | bytes 786440 | tf_op jit(solution)/shard_map/ppermute | solution.py:313
  12.6 6.3 %collective-permute-start.2 = (bf16[1,2,256,256]{3,2,1,0:T(8,128)(2,1)}, bf16[1,2,256,256]{3,2,1,0:T(8,128)(2,1)S(1)}, u32[]{:S(2)}, u32[]{:S(2)}) collective-permute-start(bf16[1,2,256,256]{3,2,1,0:T(8,128)(2,1)} %get-tuple-element.13), channel_id=1, source_target_pairs={{8,0},{16,8},{24,16},{32,24},{40,32},{48,40},{56,48},{64,56},{72,6... | collective-permute-start | bytes 786440 | tf_op jit(solution)/shard_map/ppermute | solution.py:316
  12.8 8.7 %collective-permute-start.3 = (bf16[1,2,256,256]{3,2,1,0:T(8,128)(2,1)}, bf16[1,2,256,256]{3,2,1,0:T(8,128)(2,1)}, u32[]{:S(2)}, u32[]{:S(2)}) collective-permute-start(bf16[1,2,256,256]{3,2,1,0:T(8,128)(2,1)} %get-tuple-element.14), channel_id=1, source_target_pairs={{8,0},{16,8},{24,16},{32,24},{40,32},{48,40},{56,48},{64,56},{72,6... | collective-permute-start | bytes 786440 | tf_op jit(solution)/shard_map/ppermute | solution.py:316
  33.4 2.4 %collective-permute-start.6 = (f32[1,128]{1,0:T(1,128)S(1)}, f32[1,128]{1,0:T(1,128)S(1)}, u32[]{:S(2)}, u32[]{:S(2)}) collective-permute-start(f32[1,128]{1,0:T(1,128)S(1)} %get-tuple-element.19), channel_id=1, source_target_pairs={{0,8},{8,0},{1,9},{9,1},{2,10},{10,2},{3,11},{11,3},{4,12},{12,4},... | collective-permute-start | bytes 1544 | tf_op jit(solution)/shard_map/ppermute | solution.py:333

commit v6 on v3

--- a/solution.py
+++ b/solution.py
@@ -12,7 +12,12 @@
 LANES = 128
 MIB = 1024 * 1024
 STEPS = ((0, 0), (-1, 0), (1, 0), (0, -1), (0, 1))
-SENT = {1: (4, 7, 6, 8), 2: (4, 1, 0, 2), 3: (4, 5, 2, 8), 4: (4, 3, 0, 6)}
+SENT = {
+    1: ((4, 7), (6, 8)),
+    2: ((4, 1), (0, 2)),
+    3: ((4, 5, 2, 8),),
+    4: ((4, 3, 0, 6),),
+}
 ORDER = (0, 3, 4, 1, 2)
 EARLY = (0, 1, 2)
 
@@ -65,9 +70,9 @@
         k = tile_of(i, j)
         if i == 0:
             return self.own[0, k]
-        parts = self.received[i]
-        place = SENT[i].index(k)
-        return parts[place // parts[0].shape[1]][0, place % parts[0].shape[1]]
+        for part, group in zip(self.received[i], SENT[i]):
+            if k in group:
+                return part[0, group.index(k)]
 
     def block(self, i, j, turned=None):
         if turned is None:
@@ -111,7 +116,7 @@
 
 def late_kernel(
     slots, potential, own, early, turned, sums, r3, r4, density, charges,
-    x0, x0b, q0b, x1b, out, sems,
+    first, y, x1b, x0, x0b, q0b, out, sems,
 ):
     blk = own.shape[-1]
     f32, bf16 = jnp.float32, jnp.bfloat16
@@ -125,13 +130,20 @@
         return tile_of(ORDER[p], ORDER[q]) is not None
 
     def product(left, right, p, q):
+        total = None
+        full = right is x0b
         inner = [
             k for k in range(SLOTS)
-            if (left is not x0b or coupled(p, k)) and (right is not x0b or coupled(k, q))
+            if (left is not x0b or coupled(p, k)) and (not full or coupled(k, q))
         ]
-        total = None
-        for lo, hi in runs(inner):
+        for lo, hi in runs([k for k in inner if full or k <= q]):
             term = jnp.dot(left[at(p), at(lo, hi)], right[at(lo, hi), at(q)], preferred_element_type=f32)
+            total = added(total, term)
+        for lo, hi in runs([k for k in inner if not full and k > q]):
+            term = lax.dot_general(
+                left[at(p), at(lo, hi)], right[at(q), at(lo, hi)],
+                (((1,), (1,)), ((), ())), preferred_element_type=f32,
+            )
             total = added(total, term)
         return total
 
@@ -144,9 +156,8 @@
     def place(i, j):
         return ORDER.index(i), ORDER.index(j)
 
-    for i, j in LATE_PAIRS:
-        p, q = place(i, j)
-        x0[at(p), at(q)] = halo.block(i, j, turned[TURNED.index((i, j))] if (i, j) in TURNED else None)
+    for n, (i, j) in enumerate(LATE_PAIRS):
+        x0[n] = halo.block(i, j, turned[TURNED.index((i, j))] if (i, j) in TURNED else None)
     largest = None
     for i in range(SLOTS):
         total = halo.sums(i)
@@ -156,32 +167,29 @@
         largest = top if largest is None else jnp.maximum(largest, top)
     inv = 1.0 / (2.0 * jnp.sqrt(largest + 1e-06))
 
+    def unscaled(i, j):
+        if (i, j) in EARLY_PAIRS:
+            return early[EARLY_PAIRS.index((i, j))]
+        return x0[LATE_PAIRS.index((i, j))]
+
     for i, j in PAIRS:
-        p, q = place(i, j)
-        if (i, j) in EARLY_PAIRS:
-            block = early[EARLY_PAIRS.index((i, j))] * inv
-        else:
-            block = x0[at(p), at(q)] * inv
-        x0[at(p), at(q)] = block
-        mirror(x0b, p, q, block)
+        mirror(x0b, *place(i, j), unscaled(i, j) * inv)
+    linear = 1.5 * inv
     upper = [(p, q) for p in range(SLOTS) for q in range(p, SLOTS)]
     for p, q in upper:
-        mirror(q0b, p, q, product(x0b, x0b, p, q))
+        q0b[at(p), at(q)] = product(x0b, x0b, p, q).astype(bf16)
     for p, q in upper:
         block = -0.5 * product(x0b, q0b, p, q)
         if coupled(p, q):
-            block = 1.5 * x0[at(p), at(q)] + block
+            block = linear * unscaled(ORDER[p], ORDER[q]) + block
         if p == 0:
-            x0[at(0), at(q)] = block
-        mirror(x1b, p, q, block)
-    left = jnp.concatenate(
-        [product(x1b, x1b, 0, q).astype(bf16) for q in range(SLOTS)], axis=1
-    )
+            first[:, at(q)] = block
+        x1b[at(p), at(q)] = block.astype(bf16)
+    for q in range(SLOTS):
+        y[:, at(q)] = product(x1b, x1b, 0, q).astype(bf16)
     copies = []
     for q in range(SLOTS):
-        sign = 1.5 * x0[at(0), at(q)] - 0.5 * jnp.dot(
-            left, x1b[:, at(q)], preferred_element_type=f32
-        )
+        sign = 1.5 * first[:, at(q)] - 0.5 * product(y, x1b, 0, q)
         if q == 0:
             sign = jnp.where(eye, 1.0 + sign, sign)
         result = 0.5 * sign
@@ -195,7 +203,8 @@
             occupied = jnp.sum(jnp.where(eye, result, 0.0), axis=1, keepdims=True)
             lanes = charges.shape[1]
             atoms = blk // ORBS
-            atom = lax.broadcasted_iota(jnp.int32, (blk, lanes), 0) // ORBS + slots[0, 0] % 2 * atoms
+            half = slots[0, 0] % 2
+            atom = lax.broadcasted_iota(jnp.int32, (blk, lanes), 0) // ORBS + half * atoms
             lane = lax.broadcasted_iota(jnp.int32, (blk, lanes), 1)
             charges[...] = jnp.sum(
                 jnp.where(atom == lane, 4.0 / ORBS - 2.0 * occupied, 0.0), axis=0, keepdims=True
@@ -212,8 +221,7 @@
 SMALL = pl.CostEstimate(flops=1, bytes_accessed=1, transcendentals=0)
 
 
-def limit(mib):
-    return pltpu.CompilerParams(vmem_limit_bytes=mib * MIB)
+LIMIT = pltpu.CompilerParams(vmem_limit_bytes=20 * MIB)
 
 
 def early_part(slots, potential, own, *halves):
@@ -227,7 +235,7 @@
         ),
         in_specs=[SMEM, SMEM] + [VMEM] * 5,
         out_specs=(VMEM, VMEM, VMEM),
-        compiler_params=limit(12),
+        compiler_params=LIMIT,
         cost_estimate=SMALL,
         name="early_blocks",
     )(slots, potential, own, *halves)
@@ -245,14 +253,16 @@
         in_specs=[SMEM, SMEM] + [VMEM] * 6,
         out_specs=(ANY, VMEM),
         scratch_shapes=[
-            pltpu.VMEM((order, order), jnp.float32),
+            pltpu.VMEM((blk, order), jnp.float32),
+            pltpu.VMEM((blk, order), jnp.bfloat16),
             pltpu.VMEM((order, order), jnp.bfloat16),
+            pltpu.VMEM((len(LATE_PAIRS), blk, blk), jnp.float32),
             pltpu.VMEM((order, order), jnp.bfloat16),
             pltpu.VMEM((order, order), jnp.bfloat16),
             pltpu.VMEM((SLOTS, blk, blk), jnp.float32),
             pltpu.SemaphoreType.DMA((SLOTS,)),
         ],
-        compiler_params=limit(32),
+        compiler_params=LIMIT,
         name="density_rows",
     )(slots, potential, own, early, turned, sums, r3, r4)
 
@@ -272,7 +282,7 @@
         ),
         in_specs=[VMEM, ANY],
         out_specs=(VMEM,) * len(groups),
-        compiler_params=limit(4),
+        compiler_params=LIMIT,
         cost_estimate=SMALL,
         name="pack_halo",
     )(own, earlier)
@@ -289,14 +299,13 @@
         out_shape=jax.ShapeDtypeStruct((rows.shape[0] // 2, rows.shape[1]), rows.dtype),
         in_specs=[VMEM],
         out_specs=VMEM,
-        compiler_params=limit(2),
+        compiler_params=LIMIT,
         name="pair_charges",
     )(rows)
 
 
 def shards(hamiltonian, partitions, chemical_potential):
-    n_dom = lax.axis_size("dom")
-    n_sub = lax.axis_size("sub")
+    n_dom, n_sub = lax.axis_size("dom"), lax.axis_size("sub")
     potential = chemical_potential.reshape(1, 1)
 
     def up(x, axis, size):
@@ -305,11 +314,10 @@
     def down(x, axis, size):
         return lax.ppermute(x, axis, [((i + 1) % size, i) for i in range(size)])
 
-    sub_up, sub_down = packed(hamiltonian, hamiltonian, SENT[3], SENT[4])
-    dom_parts = packed(
-        hamiltonian, sub_up, SENT[1][:2], SENT[1][2:], SENT[2][:2], SENT[2][2:]
-    )
-    r3, r4 = up(sub_up, "sub", n_sub), down(sub_down, "sub", n_sub)
+    sub_down, sub_up = packed(hamiltonian, hamiltonian, *SENT[4], *SENT[3])
+    dom_parts = packed(hamiltonian, sub_down, *SENT[1], *SENT[2])
+    r4 = down(sub_down, "sub", n_sub)
+    r3 = up(sub_up, "sub", n_sub)
     halves = [up(x, "dom", n_dom) for x in dom_parts[:2]]
     halves += [down(x, "dom", n_dom) for x in dom_parts[2:]]
     early, turned, sums = early_part(partitions, potential, hamiltonian, *halves)
@@ -318,8 +326,7 @@
     )
     copies = jnp.broadcast_to(row, (n_dom * n_sub, LANES))
     rows = lax.all_to_all(copies, ("dom", "sub"), 0, 0, tiled=True)
-    charges = paired(rows).reshape(-1)
-    return (density, charges)
+    return (density, paired(rows).reshape(-1))
 
 
 def solution(mesh):

time: 57.2 us -> 58 us (1.014)
  blocking collectives: 21.7 us -> 25.4 us
  waiting for transfers between devices: 7.97 us -> 4.89 us
    all_to_all x1, blocking collectives: 21.7 us -> 25.4 us  [shards(): rows = lax.all_to_all(copies, ('dom', 'sub'), 0, 0, tiled=True)]
    ppermute x3, waiting for transfers between devices: 3.12 us -> 0.41 us  [up(): return lax.ppermute(x, axis, [(i, (i + 1) % size) for i in range(size)])]
    ppermute x3, starting transfers between devices: 2.89 us -> 4.55 us  [up(): return lax.ppermute(x, axis, [(i, (i + 1) % size) for i in range(size)])]
    ppermute x3, starting transfers between devices: 9.55 us -> 7.91 us  [down(): return lax.ppermute(x, axis, [((i + 1) % size, i) for i in range(size)])]
  transfers between devices with their start and end apart: 6 -> 6, of which waited for: 4 -> 3; matrix products, arithmetic and copies ran while one was open for 0% -> 0% of each run, Pallas kernels for 3% -> 3%
where the time goes in v6:
time: 58 us; the launch traced here: 57.8 us
  blocking collectives  25.4 us (44%)
  starting transfers between devices  12.5 us (22%)
  Pallas kernels  12.4 us (21%)
  waiting for transfers between devices  4.89 us (8%)
  local copies, waits for them, and re-layouts  1.34 us (2%)
  between operations  1.33 us (2%)
    all_to_all x1, blocking collectives, shards(): rows = lax.all_to_all(copies, ('dom', 'sub'), 0, 0, tiled=True)  25.4 us
    pallas_call x1, Pallas kernels, late_part(): pl.pallas_call(late_kernel, out_shape=(jax.ShapeDtypeStruct((1, blk, orde...  8.31 us
    ppermute x3, starting transfers between devices, down(): return lax.ppermute(x, axis, [((i + 1) % size, i) for i in range(size)])  7.91 us
    ppermute x3, starting transfers between devices, up(): return lax.ppermute(x, axis, [(i, (i + 1) % size) for i in range(size)])  4.55 us
    ppermute x3, waiting for transfers between devices, down(): return lax.ppermute(x, axis, [((i + 1) % size, i) for i in range(size)])  4.48 us
    pallas_call x2, Pallas kernels, packed(): pl.pallas_call(functools.partial(pack_kernel, groups), out_shape=tuple((j...  1.79 us
    pallas_call x1, Pallas kernels, early_part(): pl.pallas_call(early_kernel, out_shape=(jax.ShapeDtypeStruct((len(EARLY_P...  1.64 us
    unnamed x6, local copies, waits for them, and re-layouts  1.27 us
  transfers between devices with their start and end apart: 6, of which 3 were waited for; matrix products, arithmetic and copies ran while one was open for 0% of the time, Pallas kernels for 3%

profile of v6, /device:TPU:1, one launch (start us, length us, event | category | flops | bytes accessed | tf_op | source)
XLA Modules:
  0.0 57.8 jit_solution(7824129318702963564)
XLA Ops:
  0.6 0.0 copy-start
  0.6 1.3 %copy-done = bf16[1,9,256,256]{3,2,1,0:T(8,128)(2,1)S(1)} copy-done((bf16[1,9,256,256]{3,2,1,0:T(8,128)(2,1)S(1)}, bf16[1,9,256,256]{3,2,1,0:T(8,128)(2,1)}, u32[]{:S(2)}) %copy-start) | copy-done | bytes 1179672
  1.9 0.9 %pack_halo.2 = (bf16[1,4,256,256]{3,2,1,0:T(8,128)(2,1)S(1)}, bf16[1,4,256,256]{3,2,1,0:T(8,128)(2,1)}) custom-call(bf16[1,9,256,256]{3,2,1,0:T(8,128)(2,1)S(1)} %copy-done, bf16[1,9,256,256]{3,2,1,0:T(8,128)(2,1)S(1)} %copy-done), custom_call_target="tpu_custom_call" | custom-call | flops 1 | bytes 1 | tf_op jit(solution)/shard_map/pack_halo/pallas_call | solution.py:278
  2.8 0.0 copy-start.1
  2.8 0.0 copy-start.2
  2.8 0.9 %pack_halo.3 = (bf16[1,2,256,256]{3,2,1,0:T(8,128)(2,1)S(1)}, bf16[1,2,256,256]{3,2,1,0:T(8,128)(2,1)}, bf16[1,2,256,256]{3,2,1,0:T(8,128)(2,1)}, bf16[1,2,256,256]{3,2,1,0:T(8,128)(2,1)}) custom-call(bf16[1,9,256,256]{3,2,1,0:T(8,128)(2,1)S(1)} %copy-done, bf16[1,4,256,256]{3,2,1,0:T(8,128)(2,1)S(1)} %get-tuple-element.13.earlier), custom_call_target="tpu_custom_call" | custom-call | flops 1 | bytes 1 | tf_op jit(solution)/shard_map/pack_halo/pallas_call | solution.py:278
  3.7 2.6 %collective-permute-start = (bf16[1,2,256,256]{3,2,1,0:T(8,128)(2,1)S(1)}, bf16[1,2,256,256]{3,2,1,0:T(8,128)(2,1)S(1)}, u32[]{:S(2)}, u32[]{:S(2)}) collective-permute-start(bf16[1,2,256,256]{3,2,1,0:T(8,128)(2,1)S(1)} %get-tuple-element.14), channel_id=1, source_target_pairs={{0,8},{8,16},{16,24},{24,32},{32,40},{40,48},{48,56},{56,64},{64,7... | collective-permute-start | bytes 786440 | tf_op jit(solution)/shard_map/ppermute | solution.py:312
  6.3 1.6 %collective-permute-start.4 = (bf16[1,4,256,256]{3,2,1,0:T(8,128)(2,1)}, bf16[1,4,256,256]{3,2,1,0:T(8,128)(2,1)S(1)}, u32[]{:S(2)}, u32[]{:S(2)}) collective-permute-start(bf16[1,4,256,256]{3,2,1,0:T(8,128)(2,1)} %get-tuple-element.21), channel_id=1, source_target_pairs={{0,1},{1,2},{2,3},{3,4},{4,5},{5,6},{6,7},{7,0},{8,9},{9,10},{10,1... | collective-permute-start | bytes 1572872 | tf_op jit(solution)/shard_map/ppermute | solution.py:312
  7.9 3.9 %collective-permute-start.5 = (bf16[1,4,256,256]{3,2,1,0:T(8,128)(2,1)S(1)}, bf16[1,4,256,256]{3,2,1,0:T(8,128)(2,1)S(1)}, u32[]{:S(2)}, u32[]{:S(2)}) collective-permute-start(bf16[1,4,256,256]{3,2,1,0:T(8,128)(2,1)S(1)} %get-tuple-element.13.earlier), channel_id=1, source_target_pairs={{1,0},{2,1},{3,2},{4,3},{5,4},{6,5},{7,6},{0,7},{9,8},{10,9},{11,1... | collective-permute-start | bytes 1572872 | tf_op jit(solution)/shard_map/ppermute | solution.py:315
  11.9 0.3 collective-permute-start.1
  12.2 0.2 collective-permute-start.2
  12.4 0.0 collective-permute-done.r1a
  12.4 3.8 %collective-permute-start.3 = (bf16[1,2,256,256]{3,2,1,0:T(8,128)(2,1)}, bf16[1,2,256,256]{3,2,1,0:T(8,128)(2,1)}, u32[]{:S(2)}, u32[]{:S(2)}) collective-permute-start(bf16[1,2,256,256]{3,2,1,0:T(8,128)(2,1)} %get-tuple-element.17), channel_id=1, source_target_pairs={{8,0},{16,8},{24,16},{32,24},{40,32},{48,40},{56,48},{64,56},{72,6... | collective-permute-start | bytes 786440 | tf_op jit(solution)/shard_map/ppermute | solution.py:315
  16.8 0.0 collective-permute-done.1.r1b
  16.8 1.7 %collective-permute-done.2.r2a = bf16[1,2,256,256]{3,2,1,0:T(8,128)(2,1)S(1)} collective-permute-done((bf16[1,2,256,256]{3,2,1,0:T(8,128)(2,1)}, bf16[1,2,256,256]{3,2,1,0:T(8,128)(2,1)S(1)}, u32[]{:S(2)}, u32[]{:S(2)}) %collective-permute-start.2) | collective-permute-done | bytes 262176 | tf_op jit(solution)/shard_map/ppermute | solution.py:315
  18.5 2.8 %collective-permute-done.3.r2b = bf16[1,2,256,256]{3,2,1,0:T(8,128)(2,1)} collective-permute-done((bf16[1,2,256,256]{3,2,1,0:T(8,128)(2,1)}, bf16[1,2,256,256]{3,2,1,0:T(8,128)(2,1)}, u32[]{:S(2)}, u32[]{:S(2)}) %collective-permute-start.3) | collective-permute-done | bytes 262176 | tf_op jit(solution)/shard_map/ppermute | solution.py:315
  21.3 0.0 copy-done.1
  21.3 0.0 copy-done.2
  21.3 1.6 %early_blocks.1 = (f32[5,256,256]{2,1,0:T(8,128)S(1)}, bf16[4,256,256]{2,1,0:T(8,128)(2,1)S(1)}, f32[256,128]{1,0:T(8,128)S(1)}) custom-call(s32[1,5]{1,0:T(1,128)S(1)} %copy-done.2, f32[1,1]{1,0:T(1,128)} %bitcast.4.potential, bf16[1,9,256,256]{3,2,1,0:T(8,128)(2,1)S(1)} %copy-done.1, bf16[1,2,256,256]{3,2,1,0:T(8,128)(2,1)S(1)} %collective-permute-done.r1a, ...), custom_call_target="tpu_custom_call" | custom-call | flops 1 | bytes 1 | tf_op jit(solution)/shard_map/early_blocks/pallas_call | solution.py:229
  23.0 0.4 collective-permute-done.4.r3
  23.4 0.0 collective-permute-done.5.r4
  23.4 8.3 %density_rows.1 = (f32[1,256,1280]{2,1,0:T(8,128)}, f32[1,128]{1,0:T(1,128)S(1)}) custom-call(s32[1,5]{1,0:T(1,128)S(1)} %copy-done.2, f32[1,1]{1,0:T(1,128)} %bitcast.5.potential, bf16[1,9,256,256]{3,2,1,0:T(8,128)(2,1)S(1)} %copy-done.1, f32[5,256,256]{2,1,0:T(8,128)S(1)} %get-tuple-element.18.early, bf16[4,256,256]{2,1,0:T(8,128)(2,1)S(1)} %get-tuple-element.19.turned, ...), custom_call_target="tpu_custom_call" | custom-call | tf_op jit(solution)/shard_map/density_rows/pallas_call | solution.py:247
  31.7 0.1 broadcast_in_dim.2
  31.8 25.4 %all_to_all.8 = f32[256,1,128]{2,1,0:T(1,128)S(1)} all-to-all(f32[256,1,128]{2,1,0:T(1,128)S(1)} %broadcast_in_dim.2), channel_id=1, replica_groups=mesh['dom'=32,'sub'=8] {'dom','sub'}, dimensions={0} | all-to-all | bytes 262144 | tf_op jit(solution)/shard_map/all_to_all | solution.py:328
  57.2 0.6 %pair_charges.1 = f32[128,128]{1,0:T(8,128)} custom-call(f32[256,128]{1,0:T(8,128)S(1)} %bitcast.6), custom_call_target="tpu_custom_call" | custom-call | tf_op jit(solution)/shard_map/pair_charges/pallas_call | solution.py:297
Async XLA Ops:
  0.6 1.3 %copy-start = (bf16[1,9,256,256]{3,2,1,0:T(8,128)(2,1)S(1)}, bf16[1,9,256,256]{3,2,1,0:T(8,128)(2,1)}, u32[]{:S(2)}) copy-start(bf16[1,9,256,256]{3,2,1,0:T(8,128)(2,1)} %own.7) | copy-start | bytes 3538948
  2.8 18.5 %copy-start.1 = (bf16[1,9,256,256]{3,2,1,0:T(8,128)(2,1)S(1)}, bf16[1,9,256,256]{3,2,1,0:T(8,128)(2,1)}, u32[]{:S(2)}) copy-start(bf16[1,9,256,256]{3,2,1,0:T(8,128)(2,1)} %own.7) | copy-start | bytes 3538948
  2.8 18.5 %copy-start.2 = (s32[1,5]{1,0:T(1,128)S(1)}, s32[1,5]{1,0:T(1,128)}, u32[]{:S(2)}) copy-start(s32[1,5]{1,0:T(1,128)} %slots.3) | copy-start | bytes 64
  3.7 8.7 %collective-permute-start = (bf16[1,2,256,256]{3,2,1,0:T(8,128)(2,1)S(1)}, bf16[1,2,256,256]{3,2,1,0:T(8,128)(2,1)S(1)}, u32[]{:S(2)}, u32[]{:S(2)}) collective-permute-start(bf16[1,2,256,256]{3,2,1,0:T(8,128)(2,1)S(1)} %get-tuple-element.14), channel_id=1, source_target_pairs={{0,8},{8,16},{16,24},{24,32},{32,40},{40,48},{48,56},{56,64},{64,7... | collective-permute-start | bytes 786440 | tf_op jit(solution)/shard_map/ppermute | solution.py:312
  6.3 17.1 %collective-permute-start.4 = (bf16[1,4,256,256]{3,2,1,0:T(8,128)(2,1)}, bf16[1,4,256,256]{3,2,1,0:T(8,128)(2,1)S(1)}, u32[]{:S(2)}, u32[]{:S(2)}) collective-permute-start(bf16[1,4,256,256]{3,2,1,0:T(8,128)(2,1)} %get-tuple-element.21), channel_id=1, source_target_pairs={{0,1},{1,2},{2,3},{3,4},{4,5},{5,6},{6,7},{7,0},{8,9},{9,10},{10,1... | collective-permute-start | bytes 1572872 | tf_op jit(solution)/shard_map/ppermute | solution.py:312
  7.9 15.4 %collective-permute-start.5 = (bf16[1,4,256,256]{3,2,1,0:T(8,128)(2,1)S(1)}, bf16[1,4,256,256]{3,2,1,0:T(8,128)(2,1)S(1)}, u32[]{:S(2)}, u32[]{:S(2)}) collective-permute-start(bf16[1,4,256,256]{3,2,1,0:T(8,128)(2,1)S(1)} %get-tuple-element.13.earlier), channel_id=1, source_target_pairs={{1,0},{2,1},{3,2},{4,3},{5,4},{6,5},{7,6},{0,7},{9,8},{10,9},{11,1... | collective-permute-start | bytes 1572872 | tf_op jit(solution)/shard_map/ppermute | solution.py:315
  11.9 4.9 %collective-permute-start.1 = (bf16[1,2,256,256]{3,2,1,0:T(8,128)(2,1)}, bf16[1,2,256,256]{3,2,1,0:T(8,128)(2,1)S(1)}, u32[]{:S(2)}, u32[]{:S(2)}) collective-permute-start(bf16[1,2,256,256]{3,2,1,0:T(8,128)(2,1)} %get-tuple-element.15), channel_id=1, source_target_pairs={{0,8},{8,16},{16,24},{24,32},{32,40},{40,48},{48,56},{56,64},{64,7... | collective-permute-start | bytes 786440 | tf_op jit(solution)/shard_map/ppermute | solution.py:312
  12.2 6.3 %collective-permute-start.2 = (bf16[1,2,256,256]{3,2,1,0:T(8,128)(2,1)}, bf16[1,2,256,256]{3,2,1,0:T(8,128)(2,1)S(1)}, u32[]{:S(2)}, u32[]{:S(2)}) collective-permute-start(bf16[1,2,256,256]{3,2,1,0:T(8,128)(2,1)} %get-tuple-element.16), channel_id=1, source_target_pairs={{8,0},{16,8},{24,16},{32,24},{40,32},{48,40},{56,48},{64,56},{72,6... | collective-permute-start | bytes 786440 | tf_op jit(solution)/shard_map/ppermute | solution.py:315
  12.4 8.9 %collective-permute-start.3 = (bf16[1,2,256,256]{3,2,1,0:T(8,128)(2,1)}, bf16[1,2,256,256]{3,2,1,0:T(8,128)(2,1)}, u32[]{:S(2)}, u32[]{:S(2)}) collective-permute-start(bf16[1,2,256,256]{3,2,1,0:T(8,128)(2,1)} %get-tuple-element.17), channel_id=1, source_target_pairs={{8,0},{16,8},{24,16},{32,24},{40,32},{48,40},{56,48},{64,56},{72,6... | collective-permute-start | bytes 786440 | tf_op jit(solution)/shard_map/ppermute | solution.py:315

commit v7 on v6

--- a/solution.py
+++ b/solution.py
@@ -314,12 +314,14 @@
     def down(x, axis, size):
         return lax.ppermute(x, axis, [((i + 1) % size, i) for i in range(size)])
 
-    sub_down, sub_up = packed(hamiltonian, hamiltonian, *SENT[4], *SENT[3])
-    dom_parts = packed(hamiltonian, sub_down, *SENT[1], *SENT[2])
+    sub_down, sub_up, dom_first = packed(
+        hamiltonian, hamiltonian, *SENT[4], *SENT[3], SENT[1][0]
+    )
+    dom_parts = packed(hamiltonian, sub_down, SENT[1][1], *SENT[2])
     r4 = down(sub_down, "sub", n_sub)
     r3 = up(sub_up, "sub", n_sub)
-    halves = [up(x, "dom", n_dom) for x in dom_parts[:2]]
-    halves += [down(x, "dom", n_dom) for x in dom_parts[2:]]
+    halves = [up(x, "dom", n_dom) for x in (dom_first, dom_parts[0])]
+    halves += [down(x, "dom", n_dom) for x in dom_parts[1:]]
     early, turned, sums = early_part(partitions, potential, hamiltonian, *halves)
     density, row = late_part(
         partitions, potential, hamiltonian, early, turned, sums, r3, r4

time: 58 us -> 58 us (level)
  transfers between devices with their start and end apart: 6 -> 6, of which waited for: 3 -> 2; matrix products, arithmetic and copies ran while one was open for 0% -> 0% of each run, Pallas kernels for 3% -> 4%
where the time goes in v7:
time: 58 us; the launch traced here: 57.9 us
  blocking collectives  25.8 us (44%)
  starting transfers between devices  12.5 us (22%)
  Pallas kernels  12.4 us (21%)
  waiting for transfers between devices  4.49 us (8%)
  local copies, waits for them, and re-layouts  1.34 us (2%)
  between operations  1.34 us (2%)
    all_to_all x1, blocking collectives, shards(): rows = lax.all_to_all(copies, ('dom', 'sub'), 0, 0, tiled=True)  25.8 us
    pallas_call x1, Pallas kernels, late_part(): pl.pallas_call(late_kernel, out_shape=(jax.ShapeDtypeStruct((1, blk, orde...  8.31 us
    ppermute x3, starting transfers between devices, down(): return lax.ppermute(x, axis, [((i + 1) % size, i) for i in range(size)])  7.91 us
    ppermute x3, starting transfers between devices, up(): return lax.ppermute(x, axis, [(i, (i + 1) % size) for i in range(size)])  4.6 us
    ppermute x3, waiting for transfers between devices, down(): return lax.ppermute(x, axis, [((i + 1) % size, i) for i in range(size)])  4.48 us
    pallas_call x2, Pallas kernels, packed(): pl.pallas_call(functools.partial(pack_kernel, groups), out_shape=tuple((j...  1.8 us
    pallas_call x1, Pallas kernels, early_part(): pl.pallas_call(early_kernel, out_shape=(jax.ShapeDtypeStruct((len(EARLY_P...  1.64 us
    unnamed x6, local copies, waits for them, and re-layouts  1.27 us
  transfers between devices with their start and end apart: 6, of which 2 were waited for; matrix products, arithmetic and copies ran while one was open for 0% of the time, Pallas kernels for 4%

profile of v7, /device:TPU:1, one launch (start us, length us, event | category | flops | bytes accessed | tf_op | source)
XLA Modules:
  0.0 57.9 jit_solution(10177335128106568810)
XLA Ops:
  0.6 0.0 copy-start
  0.6 1.3 %copy-done = bf16[1,9,256,256]{3,2,1,0:T(8,128)(2,1)S(1)} copy-done((bf16[1,9,256,256]{3,2,1,0:T(8,128)(2,1)S(1)}, bf16[1,9,256,256]{3,2,1,0:T(8,128)(2,1)}, u32[]{:S(2)}) %copy-start) | copy-done | bytes 1179672
  1.9 0.9 %pack_halo.2 = (bf16[1,4,256,256]{3,2,1,0:T(8,128)(2,1)S(1)}, bf16[1,4,256,256]{3,2,1,0:T(8,128)(2,1)}, bf16[1,2,256,256]{3,2,1,0:T(8,128)(2,1)S(1)}) custom-call(bf16[1,9,256,256]{3,2,1,0:T(8,128)(2,1)S(1)} %copy-done, bf16[1,9,256,256]{3,2,1,0:T(8,128)(2,1)S(1)} %copy-done), custom_call_target="tpu_custom_call" | custom-call | flops 1 | bytes 1 | tf_op jit(solution)/shard_map/pack_halo/pallas_call | solution.py:278
  2.8 0.0 copy-start.1
  2.8 0.0 copy-start.2
  2.8 2.6 %collective-permute-start = (bf16[1,2,256,256]{3,2,1,0:T(8,128)(2,1)S(1)}, bf16[1,2,256,256]{3,2,1,0:T(8,128)(2,1)S(1)}, u32[]{:S(2)}, u32[]{:S(2)}) collective-permute-start(bf16[1,2,256,256]{3,2,1,0:T(8,128)(2,1)S(1)} %get-tuple-element.13), channel_id=1, source_target_pairs={{0,8},{8,16},{16,24},{24,32},{32,40},{40,48},{48,56},{56,64},{64,7... | collective-permute-start | bytes 786440 | tf_op jit(solution)/shard_map/ppermute | solution.py:312
  5.4 1.6 %collective-permute-start.4 = (bf16[1,4,256,256]{3,2,1,0:T(8,128)(2,1)}, bf16[1,4,256,256]{3,2,1,0:T(8,128)(2,1)S(1)}, u32[]{:S(2)}, u32[]{:S(2)}) collective-permute-start(bf16[1,4,256,256]{3,2,1,0:T(8,128)(2,1)} %get-tuple-element.21), channel_id=1, source_target_pairs={{0,1},{1,2},{2,3},{3,4},{4,5},{5,6},{6,7},{7,0},{8,9},{9,10},{10,1... | collective-permute-start | bytes 1572872 | tf_op jit(solution)/shard_map/ppermute | solution.py:312
  7.0 3.9 %collective-permute-start.5 = (bf16[1,4,256,256]{3,2,1,0:T(8,128)(2,1)S(1)}, bf16[1,4,256,256]{3,2,1,0:T(8,128)(2,1)S(1)}, u32[]{:S(2)}, u32[]{:S(2)}) collective-permute-start(bf16[1,4,256,256]{3,2,1,0:T(8,128)(2,1)S(1)} %get-tuple-element.14.earlier), channel_id=1, source_target_pairs={{1,0},{2,1},{3,2},{4,3},{5,4},{6,5},{7,6},{0,7},{9,8},{10,9},{11,1... | collective-permute-start | bytes 1572872 | tf_op jit(solution)/shard_map/ppermute | solution.py:315
  11.0 0.9 %pack_halo.3 = (bf16[1,2,256,256]{3,2,1,0:T(8,128)(2,1)}, bf16[1,2,256,256]{3,2,1,0:T(8,128)(2,1)}, bf16[1,2,256,256]{3,2,1,0:T(8,128)(2,1)}) custom-call(bf16[1,9,256,256]{3,2,1,0:T(8,128)(2,1)S(1)} %copy-done, bf16[1,4,256,256]{3,2,1,0:T(8,128)(2,1)S(1)} %get-tuple-element.14.earlier), custom_call_target="tpu_custom_call" | custom-call | flops 1 | bytes 1 | tf_op jit(solution)/shard_map/pack_halo/pallas_call | solution.py:278
  11.9 0.4 collective-permute-start.1
  12.3 0.1 collective-permute-start.2
  12.4 0.0 collective-permute-done.r1a
  12.4 3.8 %collective-permute-start.3 = (bf16[1,2,256,256]{3,2,1,0:T(8,128)(2,1)}, bf16[1,2,256,256]{3,2,1,0:T(8,128)(2,1)}, u32[]{:S(2)}, u32[]{:S(2)}) collective-permute-start(bf16[1,2,256,256]{3,2,1,0:T(8,128)(2,1)} %get-tuple-element.17), channel_id=1, source_target_pairs={{8,0},{16,8},{24,16},{32,24},{40,32},{48,40},{56,48},{64,56},{72,6... | collective-permute-start | bytes 786440 | tf_op jit(solution)/shard_map/ppermute | solution.py:315
  16.9 0.0 collective-permute-done.1.r1b
  16.9 1.7 %collective-permute-done.2.r2a = bf16[1,2,256,256]{3,2,1,0:T(8,128)(2,1)S(1)} collective-permute-done((bf16[1,2,256,256]{3,2,1,0:T(8,128)(2,1)}, bf16[1,2,256,256]{3,2,1,0:T(8,128)(2,1)S(1)}, u32[]{:S(2)}, u32[]{:S(2)}) %collective-permute-start.2) | collective-permute-done | bytes 262176 | tf_op jit(solution)/shard_map/ppermute | solution.py:315
  18.6 2.8 %collective-permute-done.3.r2b = bf16[1,2,256,256]{3,2,1,0:T(8,128)(2,1)} collective-permute-done((bf16[1,2,256,256]{3,2,1,0:T(8,128)(2,1)}, bf16[1,2,256,256]{3,2,1,0:T(8,128)(2,1)}, u32[]{:S(2)}, u32[]{:S(2)}) %collective-permute-start.3) | collective-permute-done | bytes 262176 | tf_op jit(solution)/shard_map/ppermute | solution.py:315
  21.4 0.0 copy-done.1
  21.4 0.0 copy-done.2
  21.4 1.6 %early_blocks.1 = (f32[5,256,256]{2,1,0:T(8,128)S(1)}, bf16[4,256,256]{2,1,0:T(8,128)(2,1)S(1)}, f32[256,128]{1,0:T(8,128)S(1)}) custom-call(s32[1,5]{1,0:T(1,128)S(1)} %copy-done.2, f32[1,1]{1,0:T(1,128)} %bitcast.4.potential, bf16[1,9,256,256]{3,2,1,0:T(8,128)(2,1)S(1)} %copy-done.1, bf16[1,2,256,256]{3,2,1,0:T(8,128)(2,1)S(1)} %collective-permute-done.r1a, ...), custom_call_target="tpu_custom_call" | custom-call | flops 1 | bytes 1 | tf_op jit(solution)/shard_map/early_blocks/pallas_call | solution.py:229
  23.0 0.0 collective-permute-done.4.r3
  23.0 0.0 collective-permute-done.5.r4
  23.0 8.3 %density_rows.1 = (f32[1,256,1280]{2,1,0:T(8,128)}, f32[1,128]{1,0:T(1,128)S(1)}) custom-call(s32[1,5]{1,0:T(1,128)S(1)} %copy-done.2, f32[1,1]{1,0:T(1,128)} %bitcast.5.potential, bf16[1,9,256,256]{3,2,1,0:T(8,128)(2,1)S(1)} %copy-done.1, f32[5,256,256]{2,1,0:T(8,128)S(1)} %get-tuple-element.18.early, bf16[4,256,256]{2,1,0:T(8,128)(2,1)S(1)} %get-tuple-element.19.turned, ...), custom_call_target="tpu_custom_call" | custom-call | tf_op jit(solution)/shard_map/density_rows/pallas_call | solution.py:247
  31.4 0.1 broadcast_in_dim.2
  31.4 25.8 %all_to_all.8 = f32[256,1,128]{2,1,0:T(1,128)S(1)} all-to-all(f32[256,1,128]{2,1,0:T(1,128)S(1)} %broadcast_in_dim.2), channel_id=1, replica_groups=mesh['dom'=32,'sub'=8] {'dom','sub'}, dimensions={0} | all-to-all | bytes 262144 | tf_op jit(solution)/shard_map/all_to_all | solution.py:330
  57.2 0.6 %pair_charges.1 = f32[128,128]{1,0:T(8,128)} custom-call(f32[256,128]{1,0:T(8,128)S(1)} %bitcast.6), custom_call_target="tpu_custom_call" | custom-call | tf_op jit(solution)/shard_map/pair_charges/pallas_call | solution.py:297
Async XLA Ops:
  0.6 1.3 %copy-start = (bf16[1,9,256,256]{3,2,1,0:T(8,128)(2,1)S(1)}, bf16[1,9,256,256]{3,2,1,0:T(8,128)(2,1)}, u32[]{:S(2)}) copy-start(bf16[1,9,256,256]{3,2,1,0:T(8,128)(2,1)} %own.7) | copy-start | bytes 3538948
  2.8 18.6 %copy-start.1 = (bf16[1,9,256,256]{3,2,1,0:T(8,128)(2,1)S(1)}, bf16[1,9,256,256]{3,2,1,0:T(8,128)(2,1)}, u32[]{:S(2)}) copy-start(bf16[1,9,256,256]{3,2,1,0:T(8,128)(2,1)} %own.7) | copy-start | bytes 3538948
  2.8 18.6 %copy-start.2 = (s32[1,5]{1,0:T(1,128)S(1)}, s32[1,5]{1,0:T(1,128)}, u32[]{:S(2)}) copy-start(s32[1,5]{1,0:T(1,128)} %slots.3) | copy-start | bytes 64
  2.8 9.6 %collective-permute-start = (bf16[1,2,256,256]{3,2,1,0:T(8,128)(2,1)S(1)}, bf16[1,2,256,256]{3,2,1,0:T(8,128)(2,1)S(1)}, u32[]{:S(2)}, u32[]{:S(2)}) collective-permute-start(bf16[1,2,256,256]{3,2,1,0:T(8,128)(2,1)S(1)} %get-tuple-element.13), channel_id=1, source_target_pairs={{0,8},{8,16},{16,24},{24,32},{32,40},{40,48},{48,56},{56,64},{64,7... | collective-permute-start | bytes 786440 | tf_op jit(solution)/shard_map/ppermute | solution.py:312
  5.4 17.6 %collective-permute-start.4 = (bf16[1,4,256,256]{3,2,1,0:T(8,128)(2,1)}, bf16[1,4,256,256]{3,2,1,0:T(8,128)(2,1)S(1)}, u32[]{:S(2)}, u32[]{:S(2)}) collective-permute-start(bf16[1,4,256,256]{3,2,1,0:T(8,128)(2,1)} %get-tuple-element.21), channel_id=1, source_target_pairs={{0,1},{1,2},{2,3},{3,4},{4,5},{5,6},{6,7},{7,0},{8,9},{9,10},{10,1... | collective-permute-start | bytes 1572872 | tf_op jit(solution)/shard_map/ppermute | solution.py:312
  7.0 16.0 %collective-permute-start.5 = (bf16[1,4,256,256]{3,2,1,0:T(8,128)(2,1)S(1)}, bf16[1,4,256,256]{3,2,1,0:T(8,128)(2,1)S(1)}, u32[]{:S(2)}, u32[]{:S(2)}) collective-permute-start(bf16[1,4,256,256]{3,2,1,0:T(8,128)(2,1)S(1)} %get-tuple-element.14.earlier), channel_id=1, source_target_pairs={{1,0},{2,1},{3,2},{4,3},{5,4},{6,5},{7,6},{0,7},{9,8},{10,9},{11,1... | collective-permute-start | bytes 1572872 | tf_op jit(solution)/shard_map/ppermute | solution.py:315
  11.9 5.0 %collective-permute-start.1 = (bf16[1,2,256,256]{3,2,1,0:T(8,128)(2,1)}, bf16[1,2,256,256]{3,2,1,0:T(8,128)(2,1)S(1)}, u32[]{:S(2)}, u32[]{:S(2)}) collective-permute-start(bf16[1,2,256,256]{3,2,1,0:T(8,128)(2,1)} %get-tuple-element.15), channel_id=1, source_target_pairs={{0,8},{8,16},{16,24},{24,32},{32,40},{40,48},{48,56},{56,64},{64,7... | collective-permute-start | bytes 786440 | tf_op jit(solution)/shard_map/ppermute | solution.py:312
  12.3 6.3 %collective-permute-start.2 = (bf16[1,2,256,256]{3,2,1,0:T(8,128)(2,1)}, bf16[1,2,256,256]{3,2,1,0:T(8,128)(2,1)S(1)}, u32[]{:S(2)}, u32[]{:S(2)}) collective-permute-start(bf16[1,2,256,256]{3,2,1,0:T(8,128)(2,1)} %get-tuple-element.16), channel_id=1, source_target_pairs={{8,0},{16,8},{24,16},{32,24},{40,32},{48,40},{56,48},{64,56},{72,6... | collective-permute-start | bytes 786440 | tf_op jit(solution)/shard_map/ppermute | solution.py:315
  12.4 9.0 %collective-permute-start.3 = (bf16[1,2,256,256]{3,2,1,0:T(8,128)(2,1)}, bf16[1,2,256,256]{3,2,1,0:T(8,128)(2,1)}, u32[]{:S(2)}, u32[]{:S(2)}) collective-permute-start(bf16[1,2,256,256]{3,2,1,0:T(8,128)(2,1)} %get-tuple-element.17), channel_id=1, source_target_pairs={{8,0},{16,8},{24,16},{32,24},{40,32},{48,40},{56,48},{64,56},{72,6... | collective-permute-start | bytes 786440 | tf_op jit(solution)/shard_map/ppermute | solution.py:315

commit v8 on v7

--- a/solution.py
+++ b/solution.py
@@ -38,7 +38,6 @@
 ]
 EARLY_PAIRS = [pair for pair in PAIRS if pair[0] in EARLY and pair[1] in EARLY]
 LATE_PAIRS = [pair for pair in PAIRS if pair not in EARLY_PAIRS]
-TURNED = [(i, j) for i, j in LATE_PAIRS if j in EARLY]
 
 
 def runs(blocks):
@@ -74,10 +73,8 @@
             if k in group:
                 return part[0, group.index(k)]
 
-    def block(self, i, j, turned=None):
-        if turned is None:
-            turned = self.tile(j, i).T
-        both = self.tile(i, j).astype(jnp.float32) + turned.astype(jnp.float32)
+    def block(self, i, j):
+        both = self.tile(i, j).astype(jnp.float32) + self.tile(j, i).T.astype(jnp.float32)
         if i == j:
             block = (jnp.where(self.eye, self.potential, 0.0) - 0.5 * both) * self.live[i]
         else:
@@ -101,10 +98,8 @@
         return total
 
 
-def early_kernel(slots, potential, own, r1a, r1b, r2a, r2b, blocks, turned, sums):
-    halo = Halo(slots, potential, own, {1: (r1a, r1b), 2: (r2a, r2b)})
-    for place, (i, j) in enumerate(TURNED):
-        turned[place] = halo.tile(j, i).T
+def early_kernel(slots, potential, own, r1a, r2a, blocks, sums):
+    halo = Halo(slots, potential, own, {1: (r1a,), 2: (r2a,)})
     for place, (i, j) in enumerate(EARLY_PAIRS):
         blocks[place] = halo.block(i, j)
     lane = lax.broadcasted_iota(jnp.int32, sums.shape, 1)
@@ -115,12 +110,12 @@
 
 
 def late_kernel(
-    slots, potential, own, early, turned, sums, r3, r4, density, charges,
+    slots, potential, own, early, sums, r1b, r2b, r3, r4, density, charges,
     first, y, x1b, x0, x0b, q0b, out, sems,
 ):
     blk = own.shape[-1]
     f32, bf16 = jnp.float32, jnp.bfloat16
-    halo = Halo(slots, potential, own, {3: (r3,), 4: (r4,)})
+    halo = Halo(slots, potential, own, {1: (None, r1b), 2: (None, r2b), 3: (r3,), 4: (r4,)})
     eye = halo.eye
 
     def at(p, q=None):
@@ -157,7 +152,7 @@
         return ORDER.index(i), ORDER.index(j)
 
     for n, (i, j) in enumerate(LATE_PAIRS):
-        x0[n] = halo.block(i, j, turned[TURNED.index((i, j))] if (i, j) in TURNED else None)
+        x0[n] = halo.block(i, j)
     largest = None
     for i in range(SLOTS):
         total = halo.sums(i)
@@ -224,24 +219,23 @@
 LIMIT = pltpu.CompilerParams(vmem_limit_bytes=20 * MIB)
 
 
-def early_part(slots, potential, own, *halves):
+def early_part(slots, potential, own, r1a, r2a):
     blk = own.shape[-1]
     return pl.pallas_call(
         early_kernel,
         out_shape=(
             jax.ShapeDtypeStruct((len(EARLY_PAIRS), blk, blk), jnp.float32),
-            jax.ShapeDtypeStruct((len(TURNED), blk, blk), own.dtype),
             jax.ShapeDtypeStruct((blk, LANES), jnp.float32),
         ),
-        in_specs=[SMEM, SMEM] + [VMEM] * 5,
-        out_specs=(VMEM, VMEM, VMEM),
+        in_specs=[SMEM, SMEM] + [VMEM] * 3,
+        out_specs=(VMEM, VMEM),
         compiler_params=LIMIT,
         cost_estimate=SMALL,
         name="early_blocks",
-    )(slots, potential, own, *halves)
-
-
-def late_part(slots, potential, own, early, turned, sums, r3, r4):
+    )(slots, potential, own, r1a, r2a)
+
+
+def late_part(slots, potential, own, early, sums, r1b, r2b, r3, r4):
     blk = own.shape[-1]
     order = SLOTS * blk
     return pl.pallas_call(
@@ -250,7 +244,7 @@
             jax.ShapeDtypeStruct((1, blk, order), jnp.float32),
             jax.ShapeDtypeStruct((1, LANES), jnp.float32),
         ),
-        in_specs=[SMEM, SMEM] + [VMEM] * 6,
+        in_specs=[SMEM, SMEM] + [VMEM] * 7,
         out_specs=(ANY, VMEM),
         scratch_shapes=[
             pltpu.VMEM((blk, order), jnp.float32),
@@ -264,7 +258,7 @@
         ],
         compiler_params=LIMIT,
         name="density_rows",
-    )(slots, potential, own, early, turned, sums, r3, r4)
+    )(slots, potential, own, early, sums, r1b, r2b, r3, r4)
 
 
 def pack_kernel(groups, own, earlier, *packs):
@@ -320,11 +314,11 @@
     dom_parts = packed(hamiltonian, sub_down, SENT[1][1], *SENT[2])
     r4 = down(sub_down, "sub", n_sub)
     r3 = up(sub_up, "sub", n_sub)
-    halves = [up(x, "dom", n_dom) for x in (dom_first, dom_parts[0])]
-    halves += [down(x, "dom", n_dom) for x in dom_parts[1:]]
-    early, turned, sums = early_part(partitions, potential, hamiltonian, *halves)
+    r1a, r1b = [up(x, "dom", n_dom) for x in (dom_first, dom_parts[0])]
+    r2a, r2b = [down(x, "dom", n_dom) for x in dom_parts[1:]]
+    early, sums = early_part(partitions, potential, hamiltonian, r1a, r2a)
     density, row = late_part(
-        partitions, potential, hamiltonian, early, turned, sums, r3, r4
+        partitions, potential, hamiltonian, early, sums, r1b, r2b, r3, r4
     )
     copies = jnp.broadcast_to(row, (n_dom * n_sub, LANES))
     rows = lax.all_to_all(copies, ("dom", "sub"), 0, 0, tiled=True)

time: 58 us -> 58 us (level)
    ppermute x3, starting transfers between devices: 7.91 us -> 6.17 us  [down(): return lax.ppermute(x, axis, [((i + 1) % size, i) for i in range(size)])]
    ppermute x3, waiting for transfers between devices: 0.01 us -> 1.73 us  [up(): return lax.ppermute(x, axis, [(i, (i + 1) % size) for i in range(size)])]
    ppermute x3, waiting for transfers between devices: 4.48 us -> 2.96 us  [down(): return lax.ppermute(x, axis, [((i + 1) % size, i) for i in range(size)])]
    ppermute x3, starting transfers between devices: 4.6 us -> 5.98 us  [up(): return lax.ppermute(x, axis, [(i, (i + 1) % size) for i in range(size)])]
  transfers between devices with their start and end apart: 6 -> 6, of which waited for: 2 -> 3; matrix products, arithmetic and copies ran while one was open for 0% -> 0% of each run, Pallas kernels for 4% -> 4%
where the time goes in v8:
time: 58 us; the launch traced here: 57.8 us
  blocking collectives  26 us (45%)
  Pallas kernels  12.3 us (21%)
  starting transfers between devices  12.2 us (21%)
  waiting for transfers between devices  4.69 us (8%)
  local copies, waits for them, and re-layouts  1.34 us (2%)
  between operations  1.33 us (2%)
    all_to_all x1, blocking collectives, shards(): rows = lax.all_to_all(copies, ('dom', 'sub'), 0, 0, tiled=True)  26 us
    pallas_call x1, Pallas kernels, late_part(): pl.pallas_call(late_kernel, out_shape=(jax.ShapeDtypeStruct((1, blk, orde...  8.36 us
    ppermute x3, starting transfers between devices, down(): return lax.ppermute(x, axis, [((i + 1) % size, i) for i in range(size)])  6.17 us
    ppermute x3, starting transfers between devices, up(): return lax.ppermute(x, axis, [(i, (i + 1) % size) for i in range(size)])  5.98 us
    ppermute x3, waiting for transfers between devices, down(): return lax.ppermute(x, axis, [((i + 1) % size, i) for i in range(size)])  2.96 us
    pallas_call x2, Pallas kernels, packed(): pl.pallas_call(functools.partial(pack_kernel, groups), out_shape=tuple((j...  1.82 us
    ppermute x3, waiting for transfers between devices, up(): return lax.ppermute(x, axis, [(i, (i + 1) % size) for i in range(size)])  1.73 us
    pallas_call x1, Pallas kernels, early_part(): pl.pallas_call(early_kernel, out_shape=(jax.ShapeDtypeStruct((len(EARLY_P...  1.5 us
  transfers between devices with their start and end apart: 6, of which 3 were waited for; matrix products, arithmetic and copies ran while one was open for 0% of the time, Pallas kernels for 4%

profile of v8, /device:TPU:1, one launch (start us, length us, event | category | flops | bytes accessed | tf_op | source)
XLA Modules:
  0.0 57.8 jit_solution(12078800816763196165)
XLA Ops:
  0.6 0.0 copy-start
  0.6 1.3 %copy-done = bf16[1,9,256,256]{3,2,1,0:T(8,128)(2,1)S(1)} copy-done((bf16[1,9,256,256]{3,2,1,0:T(8,128)(2,1)S(1)}, bf16[1,9,256,256]{3,2,1,0:T(8,128)(2,1)}, u32[]{:S(2)}) %copy-start) | copy-done | bytes 1179672
  1.9 0.9 %pack_halo.2 = (bf16[1,4,256,256]{3,2,1,0:T(8,128)(2,1)S(1)}, bf16[1,4,256,256]{3,2,1,0:T(8,128)(2,1)}, bf16[1,2,256,256]{3,2,1,0:T(8,128)(2,1)S(1)}) custom-call(bf16[1,9,256,256]{3,2,1,0:T(8,128)(2,1)S(1)} %copy-done, bf16[1,9,256,256]{3,2,1,0:T(8,128)(2,1)S(1)} %copy-done), custom_call_target="tpu_custom_call" | custom-call | flops 1 | bytes 1 | tf_op jit(solution)/shard_map/pack_halo/pallas_call | solution.py:272
  2.8 0.0 copy-start.1
  2.8 0.0 copy-start.2
  2.8 2.6 %collective-permute-start = (bf16[1,2,256,256]{3,2,1,0:T(8,128)(2,1)S(1)}, bf16[1,2,256,256]{3,2,1,0:T(8,128)(2,1)S(1)}, u32[]{:S(2)}, u32[]{:S(2)}) collective-permute-start(bf16[1,2,256,256]{3,2,1,0:T(8,128)(2,1)S(1)} %get-tuple-element.12), channel_id=1, source_target_pairs={{0,8},{8,16},{16,24},{24,32},{32,40},{40,48},{48,56},{56,64},{64,7... | collective-permute-start | bytes 786440 | tf_op jit(solution)/shard_map/ppermute | solution.py:306
  5.4 1.6 %collective-permute-start.4 = (bf16[1,4,256,256]{3,2,1,0:T(8,128)(2,1)}, bf16[1,4,256,256]{3,2,1,0:T(8,128)(2,1)S(1)}, u32[]{:S(2)}, u32[]{:S(2)}) collective-permute-start(bf16[1,4,256,256]{3,2,1,0:T(8,128)(2,1)} %get-tuple-element.19), channel_id=1, source_target_pairs={{0,1},{1,2},{2,3},{3,4},{4,5},{5,6},{6,7},{7,0},{8,9},{9,10},{10,1... | collective-permute-start | bytes 1572872 | tf_op jit(solution)/shard_map/ppermute | solution.py:306
  7.0 3.9 %collective-permute-start.5 = (bf16[1,4,256,256]{3,2,1,0:T(8,128)(2,1)S(1)}, bf16[1,4,256,256]{3,2,1,0:T(8,128)(2,1)S(1)}, u32[]{:S(2)}, u32[]{:S(2)}) collective-permute-start(bf16[1,4,256,256]{3,2,1,0:T(8,128)(2,1)S(1)} %get-tuple-element.13.earlier), channel_id=1, source_target_pairs={{1,0},{2,1},{3,2},{4,3},{5,4},{6,5},{7,6},{0,7},{9,8},{10,9},{11,1... | collective-permute-start | bytes 1572872 | tf_op jit(solution)/shard_map/ppermute | solution.py:309
  11.0 0.9 %pack_halo.3 = (bf16[1,2,256,256]{3,2,1,0:T(8,128)(2,1)}, bf16[1,2,256,256]{3,2,1,0:T(8,128)(2,1)}, bf16[1,2,256,256]{3,2,1,0:T(8,128)(2,1)}) custom-call(bf16[1,9,256,256]{3,2,1,0:T(8,128)(2,1)S(1)} %copy-done, bf16[1,4,256,256]{3,2,1,0:T(8,128)(2,1)S(1)} %get-tuple-element.13.earlier), custom_call_target="tpu_custom_call" | custom-call | flops 1 | bytes 1 | tf_op jit(solution)/shard_map/pack_halo/pallas_call | solution.py:272
  11.9 0.0 collective-permute-start.1
  11.9 1.7 %collective-permute-start.2 = (bf16[1,2,256,256]{3,2,1,0:T(8,128)(2,1)}, bf16[1,2,256,256]{3,2,1,0:T(8,128)(2,1)S(1)}, u32[]{:S(2)}, u32[]{:S(2)}) collective-permute-start(bf16[1,2,256,256]{3,2,1,0:T(8,128)(2,1)} %get-tuple-element.17), channel_id=1, source_target_pairs={{0,8},{8,16},{16,24},{24,32},{32,40},{40,48},{48,56},{56,64},{64,7... | collective-permute-start | bytes 786440 | tf_op jit(solution)/shard_map/ppermute | solution.py:306
  13.7 0.0 collective-permute-done.r1a
  13.7 2.2 %collective-permute-start.3 = (bf16[1,2,256,256]{3,2,1,0:T(8,128)(2,1)}, bf16[1,2,256,256]{3,2,1,0:T(8,128)(2,1)S(1)}, u32[]{:S(2)}, u32[]{:S(2)}) collective-permute-start(bf16[1,2,256,256]{3,2,1,0:T(8,128)(2,1)} %get-tuple-element.18), channel_id=1, source_target_pairs={{8,0},{16,8},{24,16},{32,24},{40,32},{48,40},{56,48},{64,56},{72,6... | collective-permute-start | bytes 786440 | tf_op jit(solution)/shard_map/ppermute | solution.py:309
  16.5 1.7 %collective-permute-done.1.r2a = bf16[1,2,256,256]{3,2,1,0:T(8,128)(2,1)} collective-permute-done((bf16[1,2,256,256]{3,2,1,0:T(8,128)(2,1)}, bf16[1,2,256,256]{3,2,1,0:T(8,128)(2,1)}, u32[]{:S(2)}, u32[]{:S(2)}) %collective-permute-start.1) | collective-permute-done | bytes 262176 | tf_op jit(solution)/shard_map/ppermute | solution.py:309
  18.2 0.0 copy-done.1
  18.2 0.0 copy-done.2
  18.2 1.5 %early_blocks.1 = (f32[5,256,256]{2,1,0:T(8,128)S(1)}, f32[256,128]{1,0:T(8,128)S(1)}) custom-call(s32[1,5]{1,0:T(1,128)S(1)} %copy-done.2, f32[1,1]{1,0:T(1,128)} %bitcast.4.potential, bf16[1,9,256,256]{3,2,1,0:T(8,128)(2,1)S(1)} %copy-done.1, bf16[1,2,256,256]{3,2,1,0:T(8,128)(2,1)S(1)} %collective-permute-done.r1a, ...), custom_call_target="tpu_custom_call" | custom-call | flops 1 | bytes 1 | tf_op jit(solution)/shard_map/early_blocks/pallas_call | solution.py:224
  19.7 0.0 collective-permute-done.2.r1b
  19.7 1.3 %collective-permute-done.3.r2b = bf16[1,2,256,256]{3,2,1,0:T(8,128)(2,1)S(1)} collective-permute-done((bf16[1,2,256,256]{3,2,1,0:T(8,128)(2,1)}, bf16[1,2,256,256]{3,2,1,0:T(8,128)(2,1)S(1)}, u32[]{:S(2)}, u32[]{:S(2)}) %collective-permute-start.3) | collective-permute-done | bytes 262176 | tf_op jit(solution)/shard_map/ppermute | solution.py:309
  21.0 1.7 %collective-permute-done.4.r3 = bf16[1,4,256,256]{3,2,1,0:T(8,128)(2,1)S(1)} collective-permute-done((bf16[1,4,256,256]{3,2,1,0:T(8,128)(2,1)}, bf16[1,4,256,256]{3,2,1,0:T(8,128)(2,1)S(1)}, u32[]{:S(2)}, u32[]{:S(2)}) %collective-permute-start.4) | collective-permute-done | bytes 524320 | tf_op jit(solution)/shard_map/ppermute | solution.py:306
  22.7 0.0 collective-permute-done.5.r4
  22.7 8.4 %density_rows.1 = (f32[1,256,1280]{2,1,0:T(8,128)}, f32[1,128]{1,0:T(1,128)S(1)}) custom-call(s32[1,5]{1,0:T(1,128)S(1)} %copy-done.2, f32[1,1]{1,0:T(1,128)} %bitcast.5.potential, bf16[1,9,256,256]{3,2,1,0:T(8,128)(2,1)S(1)} %copy-done.1, f32[5,256,256]{2,1,0:T(8,128)S(1)} %get-tuple-element.15.early, f32[256,128]{1,0:T(8,128)S(1)} %get-tuple-element.16.sums, ...), custom_call_target="tpu_custom_call" | custom-call | tf_op jit(solution)/shard_map/density_rows/pallas_call | solution.py:241
  31.1 0.1 broadcast_in_dim.2
  31.2 26.0 %all_to_all.8 = f32[256,1,128]{2,1,0:T(1,128)S(1)} all-to-all(f32[256,1,128]{2,1,0:T(1,128)S(1)} %broadcast_in_dim.2), channel_id=1, replica_groups=mesh['dom'=32,'sub'=8] {'dom','sub'}, dimensions={0} | all-to-all | bytes 262144 | tf_op jit(solution)/shard_map/all_to_all | solution.py:324
  57.2 0.6 %pair_charges.1 = f32[128,128]{1,0:T(8,128)} custom-call(f32[256,128]{1,0:T(8,128)S(1)} %bitcast.6), custom_call_target="tpu_custom_call" | custom-call | tf_op jit(solution)/shard_map/pair_charges/pallas_call | solution.py:291
Async XLA Ops:
  0.6 1.3 %copy-start = (bf16[1,9,256,256]{3,2,1,0:T(8,128)(2,1)S(1)}, bf16[1,9,256,256]{3,2,1,0:T(8,128)(2,1)}, u32[]{:S(2)}) copy-start(bf16[1,9,256,256]{3,2,1,0:T(8,128)(2,1)} %own.7) | copy-start | bytes 3538948
  2.8 15.4 %copy-start.1 = (bf16[1,9,256,256]{3,2,1,0:T(8,128)(2,1)S(1)}, bf16[1,9,256,256]{3,2,1,0:T(8,128)(2,1)}, u32[]{:S(2)}) copy-start(bf16[1,9,256,256]{3,2,1,0:T(8,128)(2,1)} %own.7) | copy-start | bytes 3538948
  2.8 15.4 %copy-start.2 = (s32[1,5]{1,0:T(1,128)S(1)}, s32[1,5]{1,0:T(1,128)}, u32[]{:S(2)}) copy-start(s32[1,5]{1,0:T(1,128)} %slots.3) | copy-start | bytes 64
  2.8 10.9 %collective-permute-start = (bf16[1,2,256,256]{3,2,1,0:T(8,128)(2,1)S(1)}, bf16[1,2,256,256]{3,2,1,0:T(8,128)(2,1)S(1)}, u32[]{:S(2)}, u32[]{:S(2)}) collective-permute-start(bf16[1,2,256,256]{3,2,1,0:T(8,128)(2,1)S(1)} %get-tuple-element.12), channel_id=1, source_target_pairs={{0,8},{8,16},{16,24},{24,32},{32,40},{40,48},{48,56},{56,64},{64,7... | collective-permute-start | bytes 786440 | tf_op jit(solution)/shard_map/ppermute | solution.py:306
  5.4 17.4 %collective-permute-start.4 = (bf16[1,4,256,256]{3,2,1,0:T(8,128)(2,1)}, bf16[1,4,256,256]{3,2,1,0:T(8,128)(2,1)S(1)}, u32[]{:S(2)}, u32[]{:S(2)}) collective-permute-start(bf16[1,4,256,256]{3,2,1,0:T(8,128)(2,1)} %get-tuple-element.19), channel_id=1, source_target_pairs={{0,1},{1,2},{2,3},{3,4},{4,5},{5,6},{6,7},{7,0},{8,9},{9,10},{10,1... | collective-permute-start | bytes 1572872 | tf_op jit(solution)/shard_map/ppermute | solution.py:306
  7.0 15.7 %collective-permute-start.5 = (bf16[1,4,256,256]{3,2,1,0:T(8,128)(2,1)S(1)}, bf16[1,4,256,256]{3,2,1,0:T(8,128)(2,1)S(1)}, u32[]{:S(2)}, u32[]{:S(2)}) collective-permute-start(bf16[1,4,256,256]{3,2,1,0:T(8,128)(2,1)S(1)} %get-tuple-element.13.earlier), channel_id=1, source_target_pairs={{1,0},{2,1},{3,2},{4,3},{5,4},{6,5},{7,6},{0,7},{9,8},{10,9},{11,1... | collective-permute-start | bytes 1572872 | tf_op jit(solution)/shard_map/ppermute | solution.py:309
  11.9 6.3 %collective-permute-start.1 = (bf16[1,2,256,256]{3,2,1,0:T(8,128)(2,1)}, bf16[1,2,256,256]{3,2,1,0:T(8,128)(2,1)}, u32[]{:S(2)}, u32[]{:S(2)}) collective-permute-start(bf16[1,2,256,256]{3,2,1,0:T(8,128)(2,1)} %get-tuple-element.14), channel_id=1, source_target_pairs={{8,0},{16,8},{24,16},{32,24},{40,32},{48,40},{56,48},{64,56},{72,6... | collective-permute-start | bytes 786440 | tf_op jit(solution)/shard_map/ppermute | solution.py:309
  11.9 7.8 %collective-permute-start.2 = (bf16[1,2,256,256]{3,2,1,0:T(8,128)(2,1)}, bf16[1,2,256,256]{3,2,1,0:T(8,128)(2,1)S(1)}, u32[]{:S(2)}, u32[]{:S(2)}) collective-permute-start(bf16[1,2,256,256]{3,2,1,0:T(8,128)(2,1)} %get-tuple-element.17), channel_id=1, source_target_pairs={{0,8},{8,16},{16,24},{24,32},{32,40},{40,48},{48,56},{56,64},{64,7... | collective-permute-start | bytes 786440 | tf_op jit(solution)/shard_map/ppermute | solution.py:306
  13.7 7.4 %collective-permute-start.3 = (bf16[1,2,256,256]{3,2,1,0:T(8,128)(2,1)}, bf16[1,2,256,256]{3,2,1,0:T(8,128)(2,1)S(1)}, u32[]{:S(2)}, u32[]{:S(2)}) collective-permute-start(bf16[1,2,256,256]{3,2,1,0:T(8,128)(2,1)} %get-tuple-element.18), channel_id=1, source_target_pairs={{8,0},{16,8},{24,16},{32,24},{40,32},{48,40},{56,48},{64,56},{72,6... | collective-permute-start | bytes 786440 | tf_op jit(solution)/shard_map/ppermute | solution.py:309

commit v9 on v8

--- a/solution.py
+++ b/solution.py
@@ -308,12 +308,12 @@
     def down(x, axis, size):
         return lax.ppermute(x, axis, [((i + 1) % size, i) for i in range(size)])
 
-    sub_down, sub_up, dom_first = packed(
-        hamiltonian, hamiltonian, *SENT[4], *SENT[3], SENT[1][0]
+    sub_up, sub_down, dom_first = packed(
+        hamiltonian, hamiltonian, *SENT[3], *SENT[4], SENT[1][0]
     )
-    dom_parts = packed(hamiltonian, sub_down, SENT[1][1], *SENT[2])
+    dom_parts = packed(hamiltonian, sub_up, SENT[1][1], *SENT[2])
+    r3 = up(sub_up, "sub", n_sub)
     r4 = down(sub_down, "sub", n_sub)
-    r3 = up(sub_up, "sub", n_sub)
     r1a, r1b = [up(x, "dom", n_dom) for x in (dom_first, dom_parts[0])]
     r2a, r2b = [down(x, "dom", n_dom) for x in dom_parts[1:]]
     early, sums = early_part(partitions, potential, hamiltonian, r1a, r2a)

time: 58 us -> 56.8 us (0.979)
  blocking collectives: 26 us -> 22 us
  waiting for transfers between devices: 4.69 us -> 7.44 us
    all_to_all x1, blocking collectives: 26 us -> 22 us  [shards(): rows = lax.all_to_all(copies, ('dom', 'sub'), 0, 0, tiled=True)]
    ppermute x3, starting transfers between devices: 6.17 us -> 7.81 us  [down(): return lax.ppermute(x, axis, [((i + 1) % size, i) for i in range(size)])]
    ppermute x3, starting transfers between devices: 5.98 us -> 4.35 us  [up(): return lax.ppermute(x, axis, [(i, (i + 1) % size) for i in range(size)])]
    ppermute x3, waiting for transfers between devices: 1.73 us -> 3.12 us  [up(): return lax.ppermute(x, axis, [(i, (i + 1) % size) for i in range(size)])]
    ppermute x3, waiting for transfers between devices: 2.96 us -> 4.33 us  [down(): return lax.ppermute(x, axis, [((i + 1) % size, i) for i in range(size)])]
  transfers between devices with their start and end apart: 6 -> 6, of which waited for: 3 -> 4; matrix products, arithmetic and copies ran while one was open for 0% -> 0% of each run, Pallas kernels for 4% -> 4%
where the time goes in v9:
time: 56.8 us; the launch traced here: 56.6 us
  blocking collectives  22 us (39%)
  Pallas kernels  12.3 us (22%)
  starting transfers between devices  12.2 us (21%)
  waiting for transfers between devices  7.44 us (13%)
  local copies, waits for them, and re-layouts  1.34 us (2%)
  between operations  1.33 us (2%)
    all_to_all x1, blocking collectives, shards(): rows = lax.all_to_all(copies, ('dom', 'sub'), 0, 0, tiled=True)  22 us
    pallas_call x1, Pallas kernels, late_part(): pl.pallas_call(late_kernel, out_shape=(jax.ShapeDtypeStruct((1, blk, orde...  8.36 us
    ppermute x3, starting transfers between devices, down(): return lax.ppermute(x, axis, [((i + 1) % size, i) for i in range(size)])  7.81 us
    ppermute x3, starting transfers between devices, up(): return lax.ppermute(x, axis, [(i, (i + 1) % size) for i in range(size)])  4.35 us
    ppermute x3, waiting for transfers between devices, down(): return lax.ppermute(x, axis, [((i + 1) % size, i) for i in range(size)])  4.33 us
    ppermute x3, waiting for transfers between devices, up(): return lax.ppermute(x, axis, [(i, (i + 1) % size) for i in range(size)])  3.12 us
    pallas_call x2, Pallas kernels, packed(): pl.pallas_call(functools.partial(pack_kernel, groups), out_shape=tuple((j...  1.82 us
    pallas_call x1, Pallas kernels, early_part(): pl.pallas_call(early_kernel, out_shape=(jax.ShapeDtypeStruct((len(EARLY_P...  1.5 us
  transfers between devices with their start and end apart: 6, of which 4 were waited for; matrix products, arithmetic and copies ran while one was open for 0% of the time, Pallas kernels for 4%

profile of v9, /device:TPU:1, one launch (start us, length us, event | category | flops | bytes accessed | tf_op | source)
XLA Modules:
  0.0 56.6 jit_solution(5035377965809492998)
XLA Ops:
  0.6 0.0 copy-start
  0.6 1.3 %copy-done = bf16[1,9,256,256]{3,2,1,0:T(8,128)(2,1)S(1)} copy-done((bf16[1,9,256,256]{3,2,1,0:T(8,128)(2,1)S(1)}, bf16[1,9,256,256]{3,2,1,0:T(8,128)(2,1)}, u32[]{:S(2)}) %copy-start) | copy-done | bytes 1179672
  1.9 0.9 %pack_halo.2 = (bf16[1,4,256,256]{3,2,1,0:T(8,128)(2,1)S(1)}, bf16[1,4,256,256]{3,2,1,0:T(8,128)(2,1)}, bf16[1,2,256,256]{3,2,1,0:T(8,128)(2,1)S(1)}) custom-call(bf16[1,9,256,256]{3,2,1,0:T(8,128)(2,1)S(1)} %copy-done, bf16[1,9,256,256]{3,2,1,0:T(8,128)(2,1)S(1)} %copy-done), custom_call_target="tpu_custom_call" | custom-call | flops 1 | bytes 1 | tf_op jit(solution)/shard_map/pack_halo/pallas_call | solution.py:272
  2.8 0.0 copy-start.1
  2.8 0.0 copy-start.2
  2.8 2.6 %collective-permute-start = (bf16[1,2,256,256]{3,2,1,0:T(8,128)(2,1)S(1)}, bf16[1,2,256,256]{3,2,1,0:T(8,128)(2,1)S(1)}, u32[]{:S(2)}, u32[]{:S(2)}) collective-permute-start(bf16[1,2,256,256]{3,2,1,0:T(8,128)(2,1)S(1)} %get-tuple-element.12), channel_id=1, source_target_pairs={{0,8},{8,16},{16,24},{24,32},{32,40},{40,48},{48,56},{56,64},{64,7... | collective-permute-start | bytes 786440 | tf_op jit(solution)/shard_map/ppermute | solution.py:306
  5.4 5.6 %collective-permute-start.5 = (bf16[1,4,256,256]{3,2,1,0:T(8,128)(2,1)}, bf16[1,4,256,256]{3,2,1,0:T(8,128)(2,1)S(1)}, u32[]{:S(2)}, u32[]{:S(2)}) collective-permute-start(bf16[1,4,256,256]{3,2,1,0:T(8,128)(2,1)} %get-tuple-element.19), channel_id=1, source_target_pairs={{1,0},{2,1},{3,2},{4,3},{5,4},{6,5},{7,6},{0,7},{9,8},{10,9},{11,1... | collective-permute-start | bytes 1572872 | tf_op jit(solution)/shard_map/ppermute | solution.py:309
  11.0 0.0 collective-permute-start.4
  11.0 0.9 %pack_halo.3 = (bf16[1,2,256,256]{3,2,1,0:T(8,128)(2,1)}, bf16[1,2,256,256]{3,2,1,0:T(8,128)(2,1)}, bf16[1,2,256,256]{3,2,1,0:T(8,128)(2,1)}) custom-call(bf16[1,9,256,256]{3,2,1,0:T(8,128)(2,1)S(1)} %copy-done, bf16[1,4,256,256]{3,2,1,0:T(8,128)(2,1)S(1)} %get-tuple-element.13.earlier), custom_call_target="tpu_custom_call" | custom-call | flops 1 | bytes 1 | tf_op jit(solution)/shard_map/pack_halo/pallas_call | solution.py:272
  11.9 0.0 collective-permute-start.1
  11.9 1.7 %collective-permute-start.2 = (bf16[1,2,256,256]{3,2,1,0:T(8,128)(2,1)}, bf16[1,2,256,256]{3,2,1,0:T(8,128)(2,1)S(1)}, u32[]{:S(2)}, u32[]{:S(2)}) collective-permute-start(bf16[1,2,256,256]{3,2,1,0:T(8,128)(2,1)} %get-tuple-element.17), channel_id=1, source_target_pairs={{0,8},{8,16},{16,24},{24,32},{32,40},{40,48},{48,56},{56,64},{64,7... | collective-permute-start | bytes 786440 | tf_op jit(solution)/shard_map/ppermute | solution.py:306
  13.7 0.0 collective-permute-done.r1a
  13.7 2.2 %collective-permute-start.3 = (bf16[1,2,256,256]{3,2,1,0:T(8,128)(2,1)}, bf16[1,2,256,256]{3,2,1,0:T(8,128)(2,1)S(1)}, u32[]{:S(2)}, u32[]{:S(2)}) collective-permute-start(bf16[1,2,256,256]{3,2,1,0:T(8,128)(2,1)} %get-tuple-element.18), channel_id=1, source_target_pairs={{8,0},{16,8},{24,16},{32,24},{40,32},{48,40},{56,48},{64,56},{72,6... | collective-permute-start | bytes 786440 | tf_op jit(solution)/shard_map/ppermute | solution.py:309
  16.5 1.7 %collective-permute-done.1.r2a = bf16[1,2,256,256]{3,2,1,0:T(8,128)(2,1)} collective-permute-done((bf16[1,2,256,256]{3,2,1,0:T(8,128)(2,1)}, bf16[1,2,256,256]{3,2,1,0:T(8,128)(2,1)}, u32[]{:S(2)}, u32[]{:S(2)}) %collective-permute-start.1) | collective-permute-done | bytes 262176 | tf_op jit(solution)/shard_map/ppermute | solution.py:309
  18.2 0.0 copy-done.1
  18.2 0.0 copy-done.2
  18.2 1.5 %early_blocks.1 = (f32[5,256,256]{2,1,0:T(8,128)S(1)}, f32[256,128]{1,0:T(8,128)S(1)}) custom-call(s32[1,5]{1,0:T(1,128)S(1)} %copy-done.2, f32[1,1]{1,0:T(1,128)} %bitcast.4.potential, bf16[1,9,256,256]{3,2,1,0:T(8,128)(2,1)S(1)} %copy-done.1, bf16[1,2,256,256]{3,2,1,0:T(8,128)(2,1)S(1)} %collective-permute-done.r1a, ...), custom_call_target="tpu_custom_call" | custom-call | flops 1 | bytes 1 | tf_op jit(solution)/shard_map/early_blocks/pallas_call | solution.py:224
  19.7 0.0 collective-permute-done.2.r1b
  19.7 1.3 %collective-permute-done.3.r2b = bf16[1,2,256,256]{3,2,1,0:T(8,128)(2,1)S(1)} collective-permute-done((bf16[1,2,256,256]{3,2,1,0:T(8,128)(2,1)}, bf16[1,2,256,256]{3,2,1,0:T(8,128)(2,1)S(1)}, u32[]{:S(2)}, u32[]{:S(2)}) %collective-permute-start.3) | collective-permute-done | bytes 262176 | tf_op jit(solution)/shard_map/ppermute | solution.py:309
  21.0 1.4 %collective-permute-done.5.r4 = bf16[1,4,256,256]{3,2,1,0:T(8,128)(2,1)S(1)} collective-permute-done((bf16[1,4,256,256]{3,2,1,0:T(8,128)(2,1)}, bf16[1,4,256,256]{3,2,1,0:T(8,128)(2,1)S(1)}, u32[]{:S(2)}, u32[]{:S(2)}) %collective-permute-start.5) | collective-permute-done | bytes 524320 | tf_op jit(solution)/shard_map/ppermute | solution.py:309
  22.4 3.1 %collective-permute-done.4.r3 = bf16[1,4,256,256]{3,2,1,0:T(8,128)(2,1)S(1)} collective-permute-done((bf16[1,4,256,256]{3,2,1,0:T(8,128)(2,1)S(1)}, bf16[1,4,256,256]{3,2,1,0:T(8,128)(2,1)S(1)}, u32[]{:S(2)}, u32[]{:S(2)}) %collective-permute-start.4) | collective-permute-done | bytes 524320 | tf_op jit(solution)/shard_map/ppermute | solution.py:306
  25.5 8.4 %density_rows.1 = (f32[1,256,1280]{2,1,0:T(8,128)}, f32[1,128]{1,0:T(1,128)S(1)}) custom-call(s32[1,5]{1,0:T(1,128)S(1)} %copy-done.2, f32[1,1]{1,0:T(1,128)} %bitcast.5.potential, bf16[1,9,256,256]{3,2,1,0:T(8,128)(2,1)S(1)} %copy-done.1, f32[5,256,256]{2,1,0:T(8,128)S(1)} %get-tuple-element.15.early, f32[256,128]{1,0:T(8,128)S(1)} %get-tuple-element.16.sums, ...), custom_call_target="tpu_custom_call" | custom-call | tf_op jit(solution)/shard_map/density_rows/pallas_call | solution.py:241
  33.9 0.1 broadcast_in_dim.2
  33.9 22.0 %all_to_all.8 = f32[256,1,128]{2,1,0:T(1,128)S(1)} all-to-all(f32[256,1,128]{2,1,0:T(1,128)S(1)} %broadcast_in_dim.2), channel_id=1, replica_groups=mesh['dom'=32,'sub'=8] {'dom','sub'}, dimensions={0} | all-to-all | bytes 262144 | tf_op jit(solution)/shard_map/all_to_all | solution.py:324
  56.0 0.6 %pair_charges.1 = f32[128,128]{1,0:T(8,128)} custom-call(f32[256,128]{1,0:T(8,128)S(1)} %bitcast.6), custom_call_target="tpu_custom_call" | custom-call | tf_op jit(solution)/shard_map/pair_charges/pallas_call | solution.py:291
Async XLA Ops:
  0.6 1.3 %copy-start = (bf16[1,9,256,256]{3,2,1,0:T(8,128)(2,1)S(1)}, bf16[1,9,256,256]{3,2,1,0:T(8,128)(2,1)}, u32[]{:S(2)}) copy-start(bf16[1,9,256,256]{3,2,1,0:T(8,128)(2,1)} %own.7) | copy-start | bytes 3538948
  2.8 15.4 %copy-start.1 = (bf16[1,9,256,256]{3,2,1,0:T(8,128)(2,1)S(1)}, bf16[1,9,256,256]{3,2,1,0:T(8,128)(2,1)}, u32[]{:S(2)}) copy-start(bf16[1,9,256,256]{3,2,1,0:T(8,128)(2,1)} %own.7) | copy-start | bytes 3538948
  2.8 15.4 %copy-start.2 = (s32[1,5]{1,0:T(1,128)S(1)}, s32[1,5]{1,0:T(1,128)}, u32[]{:S(2)}) copy-start(s32[1,5]{1,0:T(1,128)} %slots.3) | copy-start | bytes 64
  2.8 10.9 %collective-permute-start = (bf16[1,2,256,256]{3,2,1,0:T(8,128)(2,1)S(1)}, bf16[1,2,256,256]{3,2,1,0:T(8,128)(2,1)S(1)}, u32[]{:S(2)}, u32[]{:S(2)}) collective-permute-start(bf16[1,2,256,256]{3,2,1,0:T(8,128)(2,1)S(1)} %get-tuple-element.12), channel_id=1, source_target_pairs={{0,8},{8,16},{16,24},{24,32},{32,40},{40,48},{48,56},{56,64},{64,7... | collective-permute-start | bytes 786440 | tf_op jit(solution)/shard_map/ppermute | solution.py:306
  5.4 17.0 %collective-permute-start.5 = (bf16[1,4,256,256]{3,2,1,0:T(8,128)(2,1)}, bf16[1,4,256,256]{3,2,1,0:T(8,128)(2,1)S(1)}, u32[]{:S(2)}, u32[]{:S(2)}) collective-permute-start(bf16[1,4,256,256]{3,2,1,0:T(8,128)(2,1)} %get-tuple-element.19), channel_id=1, source_target_pairs={{1,0},{2,1},{3,2},{4,3},{5,4},{6,5},{7,6},{0,7},{9,8},{10,9},{11,1... | collective-permute-start | bytes 1572872 | tf_op jit(solution)/shard_map/ppermute | solution.py:309
  11.0 14.5 %collective-permute-start.4 = (bf16[1,4,256,256]{3,2,1,0:T(8,128)(2,1)S(1)}, bf16[1,4,256,256]{3,2,1,0:T(8,128)(2,1)S(1)}, u32[]{:S(2)}, u32[]{:S(2)}) collective-permute-start(bf16[1,4,256,256]{3,2,1,0:T(8,128)(2,1)S(1)} %get-tuple-element.13.earlier), channel_id=1, source_target_pairs={{0,1},{1,2},{2,3},{3,4},{4,5},{5,6},{6,7},{7,0},{8,9},{9,10},{10,1... | collective-permute-start | bytes 1572872 | tf_op jit(solution)/shard_map/ppermute | solution.py:306
  11.9 6.3 %collective-permute-start.1 = (bf16[1,2,256,256]{3,2,1,0:T(8,128)(2,1)}, bf16[1,2,256,256]{3,2,1,0:T(8,128)(2,1)}, u32[]{:S(2)}, u32[]{:S(2)}) collective-permute-start(bf16[1,2,256,256]{3,2,1,0:T(8,128)(2,1)} %get-tuple-element.14), channel_id=1, source_target_pairs={{8,0},{16,8},{24,16},{32,24},{40,32},{48,40},{56,48},{64,56},{72,6... | collective-permute-start | bytes 786440 | tf_op jit(solution)/shard_map/ppermute | solution.py:309
  11.9 7.8 %collective-permute-start.2 = (bf16[1,2,256,256]{3,2,1,0:T(8,128)(2,1)}, bf16[1,2,256,256]{3,2,1,0:T(8,128)(2,1)S(1)}, u32[]{:S(2)}, u32[]{:S(2)}) collective-permute-start(bf16[1,2,256,256]{3,2,1,0:T(8,128)(2,1)} %get-tuple-element.17), channel_id=1, source_target_pairs={{0,8},{8,16},{16,24},{24,32},{32,40},{40,48},{48,56},{56,64},{64,7... | collective-permute-start | bytes 786440 | tf_op jit(solution)/shard_map/ppermute | solution.py:306
  13.7 7.4 %collective-permute-start.3 = (bf16[1,2,256,256]{3,2,1,0:T(8,128)(2,1)}, bf16[1,2,256,256]{3,2,1,0:T(8,128)(2,1)S(1)}, u32[]{:S(2)}, u32[]{:S(2)}) collective-permute-start(bf16[1,2,256,256]{3,2,1,0:T(8,128)(2,1)} %get-tuple-element.18), channel_id=1, source_target_pairs={{8,0},{16,8},{24,16},{32,24},{40,32},{48,40},{56,48},{64,56},{72,6... | collective-permute-start | bytes 786440 | tf_op jit(solution)/shard_map/ppermute | solution.py:309

commit v10 on v9

--- a/solution.py
+++ b/solution.py
@@ -74,11 +74,11 @@
                 return part[0, group.index(k)]
 
     def block(self, i, j):
-        both = self.tile(i, j).astype(jnp.float32) + self.tile(j, i).T.astype(jnp.float32)
+        half = 0.5 * self.live[i] if i == j else -0.5 * self.live[i] * self.live[j]
+        both = half * self.tile(i, j).astype(jnp.float32) + half * self.tile(j, i).T.astype(jnp.float32)
+        block = both
         if i == j:
-            block = (jnp.where(self.eye, self.potential, 0.0) - 0.5 * both) * self.live[i]
-        else:
-            block = both * (-0.5 * self.live[i] * self.live[j])
+            block = jnp.where(self.eye, self.potential * self.live[i], 0.0) - both
         squares = block * block
         folded = squares[:, :LANES]
         for lane in range(LANES, squares.shape[1], LANES):

time: 56.8 us -> 56.8 us (level)
  no operation moved by 1% of the time
where the time goes in v10:
time: 56.8 us; the launch traced here: 56.6 us
  blocking collectives  22 us (39%)
  Pallas kernels  12.4 us (22%)
  starting transfers between devices  12.2 us (21%)
  waiting for transfers between devices  7.44 us (13%)
  local copies, waits for them, and re-layouts  1.34 us (2%)
  between operations  1.33 us (2%)
    all_to_all x1, blocking collectives, shards(): rows = lax.all_to_all(copies, ('dom', 'sub'), 0, 0, tiled=True)  22 us
    pallas_call x1, Pallas kernels, late_part(): pl.pallas_call(late_kernel, out_shape=(jax.ShapeDtypeStruct((1, blk, orde...  8.4 us
    ppermute x3, starting transfers between devices, down(): return lax.ppermute(x, axis, [((i + 1) % size, i) for i in range(size)])  7.81 us
    ppermute x3, starting transfers between devices, up(): return lax.ppermute(x, axis, [(i, (i + 1) % size) for i in range(size)])  4.35 us
    ppermute x3, waiting for transfers between devices, down(): return lax.ppermute(x, axis, [((i + 1) % size, i) for i in range(size)])  4.32 us
    ppermute x3, waiting for transfers between devices, up(): return lax.ppermute(x, axis, [(i, (i + 1) % size) for i in range(size)])  3.12 us
    pallas_call x2, Pallas kernels, packed(): pl.pallas_call(functools.partial(pack_kernel, groups), out_shape=tuple((j...  1.82 us
    pallas_call x1, Pallas kernels, early_part(): pl.pallas_call(early_kernel, out_shape=(jax.ShapeDtypeStruct((len(EARLY_P...  1.51 us
  transfers between devices with their start and end apart: 6, of which 4 were waited for; matrix products, arithmetic and copies ran while one was open for 0% of the time, Pallas kernels for 4%

profile of v10, /device:TPU:1, one launch (start us, length us, event | category | flops | bytes accessed | tf_op | source)
XLA Modules:
  0.0 56.6 jit_solution(7419325824908861685)
XLA Ops:
  0.6 0.0 copy-start
  0.6 1.3 %copy-done = bf16[1,9,256,256]{3,2,1,0:T(8,128)(2,1)S(1)} copy-done((bf16[1,9,256,256]{3,2,1,0:T(8,128)(2,1)S(1)}, bf16[1,9,256,256]{3,2,1,0:T(8,128)(2,1)}, u32[]{:S(2)}) %copy-start) | copy-done | bytes 1179672
  1.9 0.9 %pack_halo.2 = (bf16[1,4,256,256]{3,2,1,0:T(8,128)(2,1)S(1)}, bf16[1,4,256,256]{3,2,1,0:T(8,128)(2,1)}, bf16[1,2,256,256]{3,2,1,0:T(8,128)(2,1)S(1)}) custom-call(bf16[1,9,256,256]{3,2,1,0:T(8,128)(2,1)S(1)} %copy-done, bf16[1,9,256,256]{3,2,1,0:T(8,128)(2,1)S(1)} %copy-done), custom_call_target="tpu_custom_call" | custom-call | flops 1 | bytes 1 | tf_op jit(solution)/shard_map/pack_halo/pallas_call | solution.py:272
  2.8 0.0 copy-start.1
  2.8 0.0 copy-start.2
  2.8 2.6 %collective-permute-start = (bf16[1,2,256,256]{3,2,1,0:T(8,128)(2,1)S(1)}, bf16[1,2,256,256]{3,2,1,0:T(8,128)(2,1)S(1)}, u32[]{:S(2)}, u32[]{:S(2)}) collective-permute-start(bf16[1,2,256,256]{3,2,1,0:T(8,128)(2,1)S(1)} %get-tuple-element.12), channel_id=1, source_target_pairs={{0,8},{8,16},{16,24},{24,32},{32,40},{40,48},{48,56},{56,64},{64,7... | collective-permute-start | bytes 786440 | tf_op jit(solution)/shard_map/ppermute | solution.py:306
  5.4 5.6 %collective-permute-start.5 = (bf16[1,4,256,256]{3,2,1,0:T(8,128)(2,1)}, bf16[1,4,256,256]{3,2,1,0:T(8,128)(2,1)S(1)}, u32[]{:S(2)}, u32[]{:S(2)}) collective-permute-start(bf16[1,4,256,256]{3,2,1,0:T(8,128)(2,1)} %get-tuple-element.19), channel_id=1, source_target_pairs={{1,0},{2,1},{3,2},{4,3},{5,4},{6,5},{7,6},{0,7},{9,8},{10,9},{11,1... | collective-permute-start | bytes 1572872 | tf_op jit(solution)/shard_map/ppermute | solution.py:309
  11.0 0.0 collective-permute-start.4
  11.0 0.9 %pack_halo.3 = (bf16[1,2,256,256]{3,2,1,0:T(8,128)(2,1)}, bf16[1,2,256,256]{3,2,1,0:T(8,128)(2,1)}, bf16[1,2,256,256]{3,2,1,0:T(8,128)(2,1)}) custom-call(bf16[1,9,256,256]{3,2,1,0:T(8,128)(2,1)S(1)} %copy-done, bf16[1,4,256,256]{3,2,1,0:T(8,128)(2,1)S(1)} %get-tuple-element.13.earlier), custom_call_target="tpu_custom_call" | custom-call | flops 1 | bytes 1 | tf_op jit(solution)/shard_map/pack_halo/pallas_call | solution.py:272
  11.9 0.0 collective-permute-start.1
  11.9 1.7 %collective-permute-start.2 = (bf16[1,2,256,256]{3,2,1,0:T(8,128)(2,1)}, bf16[1,2,256,256]{3,2,1,0:T(8,128)(2,1)S(1)}, u32[]{:S(2)}, u32[]{:S(2)}) collective-permute-start(bf16[1,2,256,256]{3,2,1,0:T(8,128)(2,1)} %get-tuple-element.17), channel_id=1, source_target_pairs={{0,8},{8,16},{16,24},{24,32},{32,40},{40,48},{48,56},{56,64},{64,7... | collective-permute-start | bytes 786440 | tf_op jit(solution)/shard_map/ppermute | solution.py:306
  13.7 0.0 collective-permute-done.r1a
  13.7 2.2 %collective-permute-start.3 = (bf16[1,2,256,256]{3,2,1,0:T(8,128)(2,1)}, bf16[1,2,256,256]{3,2,1,0:T(8,128)(2,1)S(1)}, u32[]{:S(2)}, u32[]{:S(2)}) collective-permute-start(bf16[1,2,256,256]{3,2,1,0:T(8,128)(2,1)} %get-tuple-element.18), channel_id=1, source_target_pairs={{8,0},{16,8},{24,16},{32,24},{40,32},{48,40},{56,48},{64,56},{72,6... | collective-permute-start | bytes 786440 | tf_op jit(solution)/shard_map/ppermute | solution.py:309
  16.5 1.7 %collective-permute-done.1.r2a = bf16[1,2,256,256]{3,2,1,0:T(8,128)(2,1)} collective-permute-done((bf16[1,2,256,256]{3,2,1,0:T(8,128)(2,1)}, bf16[1,2,256,256]{3,2,1,0:T(8,128)(2,1)}, u32[]{:S(2)}, u32[]{:S(2)}) %collective-permute-start.1) | collective-permute-done | bytes 262176 | tf_op jit(solution)/shard_map/ppermute | solution.py:309
  18.2 0.0 copy-done.1
  18.2 0.0 copy-done.2
  18.2 1.5 %early_blocks.1 = (f32[5,256,256]{2,1,0:T(8,128)S(1)}, f32[256,128]{1,0:T(8,128)S(1)}) custom-call(s32[1,5]{1,0:T(1,128)S(1)} %copy-done.2, f32[1,1]{1,0:T(1,128)} %bitcast.4.potential, bf16[1,9,256,256]{3,2,1,0:T(8,128)(2,1)S(1)} %copy-done.1, bf16[1,2,256,256]{3,2,1,0:T(8,128)(2,1)S(1)} %collective-permute-done.r1a, ...), custom_call_target="tpu_custom_call" | custom-call | flops 1 | bytes 1 | tf_op jit(solution)/shard_map/early_blocks/pallas_call | solution.py:224
  19.7 0.0 collective-permute-done.2.r1b
  19.7 1.3 %collective-permute-done.3.r2b = bf16[1,2,256,256]{3,2,1,0:T(8,128)(2,1)S(1)} collective-permute-done((bf16[1,2,256,256]{3,2,1,0:T(8,128)(2,1)}, bf16[1,2,256,256]{3,2,1,0:T(8,128)(2,1)S(1)}, u32[]{:S(2)}, u32[]{:S(2)}) %collective-permute-start.3) | collective-permute-done | bytes 262176 | tf_op jit(solution)/shard_map/ppermute | solution.py:309
  21.0 1.4 %collective-permute-done.5.r4 = bf16[1,4,256,256]{3,2,1,0:T(8,128)(2,1)S(1)} collective-permute-done((bf16[1,4,256,256]{3,2,1,0:T(8,128)(2,1)}, bf16[1,4,256,256]{3,2,1,0:T(8,128)(2,1)S(1)}, u32[]{:S(2)}, u32[]{:S(2)}) %collective-permute-start.5) | collective-permute-done | bytes 524320 | tf_op jit(solution)/shard_map/ppermute | solution.py:309
  22.4 3.1 %collective-permute-done.4.r3 = bf16[1,4,256,256]{3,2,1,0:T(8,128)(2,1)S(1)} collective-permute-done((bf16[1,4,256,256]{3,2,1,0:T(8,128)(2,1)S(1)}, bf16[1,4,256,256]{3,2,1,0:T(8,128)(2,1)S(1)}, u32[]{:S(2)}, u32[]{:S(2)}) %collective-permute-start.4) | collective-permute-done | bytes 524320 | tf_op jit(solution)/shard_map/ppermute | solution.py:306
  25.5 8.4 %density_rows.1 = (f32[1,256,1280]{2,1,0:T(8,128)}, f32[1,128]{1,0:T(1,128)S(1)}) custom-call(s32[1,5]{1,0:T(1,128)S(1)} %copy-done.2, f32[1,1]{1,0:T(1,128)} %bitcast.5.potential, bf16[1,9,256,256]{3,2,1,0:T(8,128)(2,1)S(1)} %copy-done.1, f32[5,256,256]{2,1,0:T(8,128)S(1)} %get-tuple-element.15.early, f32[256,128]{1,0:T(8,128)S(1)} %get-tuple-element.16.sums, ...), custom_call_target="tpu_custom_call" | custom-call | tf_op jit(solution)/shard_map/density_rows/pallas_call | solution.py:241
  33.9 0.1 broadcast_in_dim.2
  34.0 22.0 %all_to_all.8 = f32[256,1,128]{2,1,0:T(1,128)S(1)} all-to-all(f32[256,1,128]{2,1,0:T(1,128)S(1)} %broadcast_in_dim.2), channel_id=1, replica_groups=mesh['dom'=32,'sub'=8] {'dom','sub'}, dimensions={0} | all-to-all | bytes 262144 | tf_op jit(solution)/shard_map/all_to_all | solution.py:324
  56.0 0.6 %pair_charges.1 = f32[128,128]{1,0:T(8,128)} custom-call(f32[256,128]{1,0:T(8,128)S(1)} %bitcast.6), custom_call_target="tpu_custom_call" | custom-call | tf_op jit(solution)/shard_map/pair_charges/pallas_call | solution.py:291
Async XLA Ops:
  0.6 1.3 %copy-start = (bf16[1,9,256,256]{3,2,1,0:T(8,128)(2,1)S(1)}, bf16[1,9,256,256]{3,2,1,0:T(8,128)(2,1)}, u32[]{:S(2)}) copy-start(bf16[1,9,256,256]{3,2,1,0:T(8,128)(2,1)} %own.7) | copy-start | bytes 3538948
  2.8 15.4 %copy-start.1 = (bf16[1,9,256,256]{3,2,1,0:T(8,128)(2,1)S(1)}, bf16[1,9,256,256]{3,2,1,0:T(8,128)(2,1)}, u32[]{:S(2)}) copy-start(bf16[1,9,256,256]{3,2,1,0:T(8,128)(2,1)} %own.7) | copy-start | bytes 3538948
  2.8 15.4 %copy-start.2 = (s32[1,5]{1,0:T(1,128)S(1)}, s32[1,5]{1,0:T(1,128)}, u32[]{:S(2)}) copy-start(s32[1,5]{1,0:T(1,128)} %slots.3) | copy-start | bytes 64
  2.8 10.9 %collective-permute-start = (bf16[1,2,256,256]{3,2,1,0:T(8,128)(2,1)S(1)}, bf16[1,2,256,256]{3,2,1,0:T(8,128)(2,1)S(1)}, u32[]{:S(2)}, u32[]{:S(2)}) collective-permute-start(bf16[1,2,256,256]{3,2,1,0:T(8,128)(2,1)S(1)} %get-tuple-element.12), channel_id=1, source_target_pairs={{0,8},{8,16},{16,24},{24,32},{32,40},{40,48},{48,56},{56,64},{64,7... | collective-permute-start | bytes 786440 | tf_op jit(solution)/shard_map/ppermute | solution.py:306
  5.4 17.0 %collective-permute-start.5 = (bf16[1,4,256,256]{3,2,1,0:T(8,128)(2,1)}, bf16[1,4,256,256]{3,2,1,0:T(8,128)(2,1)S(1)}, u32[]{:S(2)}, u32[]{:S(2)}) collective-permute-start(bf16[1,4,256,256]{3,2,1,0:T(8,128)(2,1)} %get-tuple-element.19), channel_id=1, source_target_pairs={{1,0},{2,1},{3,2},{4,3},{5,4},{6,5},{7,6},{0,7},{9,8},{10,9},{11,1... | collective-permute-start | bytes 1572872 | tf_op jit(solution)/shard_map/ppermute | solution.py:309
  11.0 14.5 %collective-permute-start.4 = (bf16[1,4,256,256]{3,2,1,0:T(8,128)(2,1)S(1)}, bf16[1,4,256,256]{3,2,1,0:T(8,128)(2,1)S(1)}, u32[]{:S(2)}, u32[]{:S(2)}) collective-permute-start(bf16[1,4,256,256]{3,2,1,0:T(8,128)(2,1)S(1)} %get-tuple-element.13.earlier), channel_id=1, source_target_pairs={{0,1},{1,2},{2,3},{3,4},{4,5},{5,6},{6,7},{7,0},{8,9},{9,10},{10,1... | collective-permute-start | bytes 1572872 | tf_op jit(solution)/shard_map/ppermute | solution.py:306
  11.9 6.3 %collective-permute-start.1 = (bf16[1,2,256,256]{3,2,1,0:T(8,128)(2,1)}, bf16[1,2,256,256]{3,2,1,0:T(8,128)(2,1)}, u32[]{:S(2)}, u32[]{:S(2)}) collective-permute-start(bf16[1,2,256,256]{3,2,1,0:T(8,128)(2,1)} %get-tuple-element.14), channel_id=1, source_target_pairs={{8,0},{16,8},{24,16},{32,24},{40,32},{48,40},{56,48},{64,56},{72,6... | collective-permute-start | bytes 786440 | tf_op jit(solution)/shard_map/ppermute | solution.py:309
  11.9 7.8 %collective-permute-start.2 = (bf16[1,2,256,256]{3,2,1,0:T(8,128)(2,1)}, bf16[1,2,256,256]{3,2,1,0:T(8,128)(2,1)S(1)}, u32[]{:S(2)}, u32[]{:S(2)}) collective-permute-start(bf16[1,2,256,256]{3,2,1,0:T(8,128)(2,1)} %get-tuple-element.17), channel_id=1, source_target_pairs={{0,8},{8,16},{16,24},{24,32},{32,40},{40,48},{48,56},{56,64},{64,7... | collective-permute-start | bytes 786440 | tf_op jit(solution)/shard_map/ppermute | solution.py:306
  13.7 7.4 %collective-permute-start.3 = (bf16[1,2,256,256]{3,2,1,0:T(8,128)(2,1)}, bf16[1,2,256,256]{3,2,1,0:T(8,128)(2,1)S(1)}, u32[]{:S(2)}, u32[]{:S(2)}) collective-permute-start(bf16[1,2,256,256]{3,2,1,0:T(8,128)(2,1)} %get-tuple-element.18), channel_id=1, source_target_pairs={{8,0},{16,8},{24,16},{32,24},{40,32},{48,40},{56,48},{64,56},{72,6... | collective-permute-start | bytes 786440 | tf_op jit(solution)/shard_map/ppermute | solution.py:309
